TPU v7x, 32 devices: a whole 2x2x4 slice. The times are simulated.
32 devices in a mesh: segment: 2 (over core), seq: 8 (over z, x), mp: 2 (over y).
Axes of the slice: x: 2, y: 2, z: 4, core: 2. Of those that a mesh axis runs over, the one named last changes fastest.
Arguments:
- hidden: bfloat16 [2, 2, 1280, 2048], P('segment', None, 'seq', 'mp'), may hold values from -120 to 120
- memory: bfloat16 [2, 2, 1280, 2048], P('segment', None, 'seq', 'mp'), may hold values from -120 to 120
- w_query: bfloat16 [2, 2048, 2048], P('segment', None, 'mp'), may hold values from -1 to 1
- w_key: bfloat16 [2, 2048, 2048], P('segment', None, 'mp'), may hold values from -4 to 4
- w_value: bfloat16 [2, 2048, 2048], P('segment', None, 'mp'), may hold values from -0.125 to 0.125
- w_out: bfloat16 [2, 2048, 2048], P('segment', 'mp'), may hold values from -3 to 3
- norm_gain: float32 [2, 2048], P('segment'), may hold values from 0.1 to 1.9
- final_gain: float32 [2048], replicated, may hold values from 0.1 to 1.9
- lengths: int32 [2, 2, 2], P('segment'), may hold values from 640 to 1280, as said below
Outputs:
- sublayer: bfloat16 [2, 2, 1280, 2048], P('segment', None, 'seq', 'mp')
Inputs may be any that keep to these rules, and one draw needn't show every extreme that they name: For each sequence b: lengths[0, b, 0] equals lengths[0, b, 1] (the encoder's document length); lengths[1, b, 0] is the target length and lengths[1, b, 1] the length of the document whose memory the decoder reads; one of these three lengths equals 1280.
All inputs are finite; a program needn't handle non-finite values.
Results may differ from a plain program's by a relative error of at most 0.018.
Values may be sent and summed in bfloat16 or wider, within the bound.
No kernel may reach another device: no remote copies, remote signals or barrier semaphores. Data moves between devices by JAX's collectives and lax.ppermute only.
A program may use at most 128 MiB of HBM per device.

v0:
```python
import jax
import jax.numpy as jnp
from jax import lax
from jax.sharding import PartitionSpec as P

DH = 64


def passed_along(value, axis, steps):
    count = lax.axis_size(axis)
    leading, last = (max(0, -steps), min(count, count - steps))
    return lax.ppermute(value, axis, [(source, source + steps) for source in range(leading, last)])


def normalize(values, gain_row):
    widened = values.astype(jnp.float32)
    square = jnp.mean(widened * widened, axis=-1, keepdims=True)
    return (widened * lax.rsqrt(square + 1e-06) * gain_row).astype(jnp.bfloat16)


def body(hidden, memory, w_query, w_key, w_value, w_out, norm_gain, final_gain, lengths):
    encoder_side = lax.axis_index("segment") == 0
    own_part = hidden[0]
    arrived = passed_along(memory[0], "segment", 1)
    source_part = jnp.where(encoder_side, own_part, arrived)
    query_rows, source_rows = (
        lax.all_gather(own_part, "mp", axis=2, tiled=True),
        lax.all_gather(source_part, "mp", axis=2, tiled=True),
    )
    batch = own_part.shape[0]
    row_count = own_part.shape[1]
    width = query_rows.shape[2]
    key_gain = jnp.where(encoder_side, norm_gain[0], final_gain)
    query_in = normalize(query_rows.reshape(batch * row_count, width), norm_gain[0])
    key_in = normalize(source_rows.reshape(batch * row_count, width), key_gain)
    head_cols = w_query.shape[2]
    local_heads = head_cols // DH
    queries = jnp.dot(query_in, w_query[0], preferred_element_type=jnp.float32).astype(jnp.bfloat16)
    keys = jnp.dot(key_in, w_key[0], preferred_element_type=jnp.float32).astype(jnp.bfloat16)
    values = jnp.dot(key_in, w_value[0], preferred_element_type=jnp.float32).astype(jnp.bfloat16)
    keys = keys.reshape(batch, row_count, head_cols)
    values = values.reshape(batch, row_count, head_cols)
    query_length = lengths[0, :, 0]
    key_length = lengths[0, :, 1]
    split_queries = queries.reshape(batch, row_count, local_heads, DH)
    key_piece = lax.all_gather(keys, "seq", axis=1, tiled=True)
    value_piece = lax.all_gather(values, "seq", axis=1, tiled=True)
    key_count = key_piece.shape[1]
    running_max = jnp.full((batch, row_count, local_heads), -1e30, jnp.float32)
    scores = (
        jnp.einsum(
            "bqhd,bkhd->bqhk",
            split_queries,
            key_piece.reshape(batch, key_count, local_heads, DH),
            preferred_element_type=jnp.float32,
        )
        * 0.25
    )
    visible = jnp.arange(key_count)[None, :] < key_length[:, None]
    mask = visible[:, None, None, :]
    scores = jnp.where(mask, scores, -1e30)
    new_max = jnp.maximum(running_max, jnp.max(scores, axis=-1))
    exponent = jnp.where(mask, jnp.exp(scores - new_max[..., None]), 0.0)
    totals = jnp.sum(exponent, axis=-1)
    weighted = jnp.einsum(
        "bqhk,bkhd->bqhd",
        exponent.astype(jnp.bfloat16),
        value_piece.reshape(batch, key_count, local_heads, DH),
        preferred_element_type=jnp.float32,
    )
    numerator = weighted
    running_max, totals, numerator = (new_max, totals, numerator)
    context = numerator / totals[..., None]
    positions = lax.axis_index("seq") * row_count + jnp.arange(row_count)
    live_rows = positions[None, :] < query_length[:, None]
    context = jnp.where(live_rows[:, :, None, None], context, 0.0)
    context = context.astype(jnp.bfloat16).reshape(batch * row_count, head_cols)
    partial_value = jnp.dot(context, w_out[0], preferred_element_type=jnp.float32)
    branch = lax.psum_scatter(
        partial_value.astype(jnp.bfloat16), "mp", scatter_dimension=1, tiled=True
    ).astype(jnp.float32)
    branch = branch.reshape(batch, row_count, branch.shape[1])
    return (own_part.astype(jnp.float32) + branch).astype(jnp.bfloat16)[None]


def solution(mesh):
    return jax.shard_map(
        body,
        mesh=mesh,
        in_specs=(
            P("segment", None, "seq", "mp"),
            P("segment", None, "seq", "mp"),
            P("segment", None, "mp"),
            P("segment", None, "mp"),
            P("segment", None, "mp"),
            P("segment", "mp", None),
            P("segment", None),
            P(),
            P("segment", None, None),
        ),
        out_specs=P("segment", None, "seq", "mp"),
        check_vma=False,
    )
```

profile of v0, /device:TPU:0, one launch (start us, length us, event | category | flops | bytes accessed | tf_op | source)
XLA Modules:
  0.0 298.0 jit_solution(374687399100853642)
XLA Ops:
  6.5 0.0 all-gather.6.cloned.1.call-start
  6.5 2.4 collective-permute-start
  8.9 1.9 collective-permute-done
  10.8 2.0 bitcast_select_fusion
  12.8 0.0 all-gather.6.cloned.1.call-update
  12.8 0.0 all-gather.12.cloned.1.call-start
  12.9 0.7 all-gather.12.cloned.1.call-update
  13.6 0.0 all-gather.10.cloned.1.call-start
  13.6 0.7 broadcast_select_fusion
  14.3 25.0 %all-gather.6.cloned.1.call-done = bf16[2,160,2048]{2,1,0:T(8,128)(2,1)} async-done(((bf16[2,160,1024]{2,1,0:T(8,128)(2,1)}), bf16[2,160,2048]{2,1,0:T(8,128)(2,1)}) %all-gather.6.cloned.1.call-update) | async-done | bytes 1310736 | tf_op jit(solution)/shard_map/all_gather | solution.py:28
  39.4 1.7 fusion.19
  41.0 1.7 fusion.21
  42.7 4.6 %fusion.32 = bf16[320,1024]{1,0:T(8,128)(2,1)} fusion(bf16[320,2048]{1,0:T(8,128)(2,1)S(1)} %bitcast.66, bf16[1,2048,1024]{2,1,0:T(8,128)(2,1)} %param.12), kind=kOutput, calls=%fused_computation.33 | convolution fusion | flops 1342504960 | bytes 6160384 | tf_op jit(solution)/shard_map/dot_general | solution.py:39
  47.3 0.0 all-gather.10.cloned.1.call-update
  47.3 0.0 copy-start.2
  47.3 0.0 copy-start.1
  47.3 0.0 all-gather.8.cloned.1.call-start
  47.4 4.8 %fusion.29 = bf16[320,1024]{1,0:T(8,128)(2,1)} fusion(bf16[320,2048]{1,0:T(8,128)(2,1)S(1)} %bitcast.67, bf16[1,2048,1024]{2,1,0:T(8,128)(2,1)} %param.13), kind=kOutput, calls=%fused_computation.32 | convolution fusion | flops 1342504960 | bytes 6160384 | tf_op jit(solution)/shard_map/dot_general | solution.py:40
  52.2 0.0 all-gather.8.cloned.1.call-update
  52.2 0.2 reduce-scatter.2.cloned.1.call-start
  52.4 0.0 copy-done.2
  52.4 0.2 slice_reduce_fusion.1
  52.6 0.1 broadcast_compare_fusion
  52.7 0.1 iota_compare_fusion
  52.8 12.4 %all-gather.12.cloned.1.call-done = bf16[1,2,160,2048]{3,2,1,0:T(8,128)(2,1)} async-done(((bf16[1,2,160,1024]{3,2,1,0:T(8,128)(2,1)}), bf16[1,2,160,2048]{3,2,1,0:T(8,128)(2,1)}) %all-gather.12.cloned.1.call-update) | async-done | bytes 1310736 | tf_op jit(solution)/shard_map/all_gather | solution.py:27
  65.2 1.7 fusion.22
  66.8 0.0 copy-done.1
  66.9 1.7 fusion.24
  68.5 3.7 %fusion.35 = bf16[320,1024]{1,0:T(8,128)(2,1)S(1)} fusion(bf16[320,2048]{1,0:T(8,128)(2,1)S(1)} %bitcast.68, bf16[1,2048,1024]{2,1,0:T(8,128)(2,1)} %param.11), kind=kOutput, calls=%fused_computation.34 | convolution fusion | flops 1342504960 | bytes 6160384 | tf_op jit(solution)/shard_map/dot_general | solution.py:38
  72.3 0.8 reshape.153
  73.1 80.6 %all-gather.10.cloned.1.call-done = bf16[2,1280,1024]{2,1,0:T(8,128)(2,1)} async-done(((bf16[2,160,1024]{2,1,0:T(8,128)(2,1)}), bf16[2,1280,1024]{2,1,0:T(8,128)(2,1)}) %all-gather.10.cloned.1.call-update) | async-done | bytes 5242896 | tf_op jit(solution)/shard_map/all_gather | solution.py:46
  153.7 7.8 %copy.14 = bf16[2,1280,1024]{1,2,0:T(8,128)(2,1)} copy(bf16[2,1280,1024]{2,1,0:T(8,128)(2,1)} %all-gather.10.cloned.1.call-done) | data formatting | bytes 10485760 | tf_op jit(solution)/shard_map/all_gather | solution.py:46
  161.5 12.5 %bitcast_reduce_fusion = (f32[2,160,16]{1,2,0:T(8,128)S(1)}, f32[2,16,1280,160]{2,3,1,0:T(8,128)}) fusion(pred[2,1280]{1,0:T(4,128)(4,1)S(1)} %iota_compare_fusion, bf16[2,1280,16,64]{1,3,2,0:T(8,128)(2,1)} %bitcast.64, bf16[2,160,16,64]{3,2,1,0:T(8,128)(2,1)S(1)} %reshape.153), kind=kOutput, calls=%fused_computation.1 | convolution fusion | flops 858516480 | bytes 32135680 | tf_op jit(solution)/shard_map/bqhd,bkhd->bqhk/dot_general | solution.py:51
  174.0 9.9 %fusion.2 = f32[2,160,16]{1,2,0:T(8,128)S(1)} fusion(f32[2,16,1280,160]{2,3,1,0:T(8,128)} %get-tuple-element.8, f32[2,160,16]{1,2,0:T(8,128)S(1)} %broadcast_maximum_fusion, pred[2,1280]{1,0:T(4,128)(4,1)S(1)} %iota_compare_fusion), kind=kLoop, calls=%fused_computation.5 | loop fusion | flops 32762880 | bytes 26257920 | tf_op jit(solution)/shard_map/reduce_sum | solution.py:64
  184.0 56.3 %all-gather.8.cloned.1.call-done = bf16[2,1280,1024]{2,1,0:T(8,128)(2,1)} async-done(((bf16[2,160,1024]{2,1,0:T(8,128)(2,1)}), bf16[2,1280,1024]{2,1,0:T(8,128)(2,1)}) %all-gather.8.cloned.1.call-update) | async-done | bytes 5242896 | tf_op jit(solution)/shard_map/all_gather | solution.py:47
  240.2 7.8 %copy.13 = bf16[2,1280,1024]{1,2,0:T(8,128)(2,1)} copy(bf16[2,1280,1024]{2,1,0:T(8,128)(2,1)} %all-gather.8.cloned.1.call-done) | data formatting | bytes 10485760 | tf_op jit(solution)/shard_map/all_gather | solution.py:47
  248.0 13.2 %fusion.26 = bf16[2,160,16,64]{1,3,2,0:T(8,128)(2,1)S(1)} fusion(bf16[2,1280,16,64]{1,3,2,0:T(8,128)(2,1)} %bitcast.65, f32[2,16,1280,160]{2,3,1,0:T(8,128)} %get-tuple-element.8, f32[2,160,16]{1,2,0:T(8,128)S(1)} %broadcast_maximum_fusion, pred[2,1280]{1,0:T(4,128)(4,1)S(1)} %iota_compare_fusion, f32[2,160,16]{1,2,0:T(8,128)S(1)} %fusion.2, ...), kind=kOutput, calls=%fused_computation.31 | convolution fusion | flops 872611840 | bytes 32156480 | tf_op jit(solution)/shard_map/bqhk,bkhd->bqhd/dot_general | solution.py:65
  261.2 1.1 copy.17
  262.3 0.5 reshape.146
  262.8 0.0 copy-start
  262.9 4.9 %fusion.16 = bf16[320,2048]{1,0:T(8,128)(2,1)} fusion(bf16[320,1024]{0,1:T(8,128)(2,1)S(1)} %reshape.146, bf16[1,1024,2048]{2,1,0:T(8,128)(2,1)} %param.14), kind=kOutput, calls=%fused_computation.22 | convolution fusion | flops 1342832640 | bytes 6160384 | tf_op jit(solution)/shard_map/dot_general | solution.py:78
  267.7 0.0 reduce-scatter.2.cloned.1.call-update
  267.8 21.5 %reduce-scatter.2.cloned.1.call-done = bf16[320,1024]{1,0:T(8,128)(2,1)} async-done(((bf16[320,2048]{1,0:T(8,128)(2,1)}), bf16[320,1024]{1,0:T(8,128)(2,1)}) %reduce-scatter.2.cloned.1.call-update) | async-done | bytes 655376 | tf_op jit(solution)/shard_map/reduce_scatter | solution.py:79
  289.3 0.0 copy-done
  289.3 2.2 fusion.38
  (4 shorter events, 0.0 us)
Async XLA Ops:
  6.5 32.8 %all-gather.6.cloned.1.call-start = ((), (), s32[]{:S(2)}) async-start(), calls=%async_computation.1 | async-start | bytes 1966080 | tf_op jit(solution)/shard_map/all_gather | solution.py:28
  6.5 4.3 %collective-permute-start = (bf16[2,160,1024]{2,1,0:T(8,128)(2,1)}, bf16[2,160,1024]{2,1,0:T(8,128)(2,1)S(1)}, u32[]{:S(2)}, u32[]{:S(2)}) collective-permute-start(bf16[2,160,1024]{2,1,0:T(8,128)(2,1)} %bitcast.74), channel_id=1, source_target_pairs={{0,16},{1,17},{2,18},{3,19},{4,20},{5,21},{6,22},{7,23},{8,24},{9,... | collective-permute-start | bytes 1966088 | tf_op jit(solution)/shard_map/ppermute | solution.py:12
  12.8 52.4 %all-gather.12.cloned.1.call-start = ((), (), s32[]{:S(2)}) async-start(), calls=%async_computation.5 | async-start | bytes 1966080 | tf_op jit(solution)/shard_map/all_gather | solution.py:27
  13.6 140.1 %all-gather.10.cloned.1.call-start = ((), (), s32[]{:S(2)}) async-start(), calls=%async_computation.3 | async-start | bytes 5898240 | tf_op jit(solution)/shard_map/all_gather | solution.py:46
  47.3 5.2 %copy-start.2 = (s32[1,2,2]{2,1,0:T(2,128)S(1)}, s32[1,2,2]{2,1,0:T(2,128)}, u32[]{:S(2)}) copy-start(s32[1,2,2]{2,1,0:T(2,128)} %param.17) | copy-start | bytes 52
  47.3 19.5 %copy-start.1 = (f32[1,2048]{1,0:T(1,128)S(1)}, f32[1,2048]{1,0:T(1,128)}, u32[]{:S(2)}) copy-start(f32[1,2048]{1,0:T(1,128)} %param.15) | copy-start | bytes 24580
  47.3 192.9 %all-gather.8.cloned.1.call-start = ((), (), s32[]{:S(2)}) async-start(), calls=%async_computation.2 | async-start | bytes 5898240 | tf_op jit(solution)/shard_map/all_gather | solution.py:47
  52.2 237.1 %reduce-scatter.2.cloned.1.call-start = ((), (), s32[]{:S(2)}) async-start(), calls=%async_computation.4 | async-start | bytes 1966080 | tf_op jit(solution)/shard_map/reduce_scatter | solution.py:79
  262.8 26.4 %copy-start = (bf16[1,2,160,1024]{3,2,1,0:T(8,128)(2,1)S(1)}, bf16[1,2,160,1024]{3,2,1,0:T(8,128)(2,1)}, u32[]{:S(2)}) copy-start(bf16[1,2,160,1024]{3,2,1,0:T(8,128)(2,1)} %param.9) | copy-start | bytes 1966084
Sparse Core Ops, SparseCore 0:
  12.9 26.3 all-gather.5
  40.9 24.2 all-gather.11
  67.4 86.2 all-gather.9
  155.7 84.4 all-gather.7
  267.9 21.3 reduce-scatter.1
where the time goes:
time: 299 us; the launch traced here: 298 us
  waiting for transfers between devices  198 us (66%)
  matrix products  43.6 us (15%)
  other arithmetic  21.7 us (7%)
  local copies, waits for them, and re-layouts  18.3 us (6%)
  between operations  13.3 us (4%)
    all_gather x1, waiting for transfers between devices, body(): key_piece = lax.all_gather(keys, 'seq', axis=1, tiled=True)  80.6 us
    all_gather x1, waiting for transfers between devices, body(): value_piece = lax.all_gather(values, 'seq', axis=1, tiled=True)  56.3 us
    all_gather x1, waiting for transfers between devices, body(): lax.all_gather(source_part, 'mp', axis=2, tiled=True)  25 us
    reduce_scatter x1, waiting for transfers between devices, body(): lax.psum_scatter(partial_value.astype(jnp.bfloat16), 'mp', scatter_dimens...  21.5 us
    dot_general x1, matrix products, body(): jnp.einsum('bqhk,bkhd->bqhd', exponent.astype(jnp.bfloat16), value_piece....  13.2 us
    dot_general x1, matrix products, body(): jnp.einsum('bqhd,bkhd->bqhk', split_queries, key_piece.reshape(batch, key...  12.5 us
    all_gather x1, waiting for transfers between devices, body(): lax.all_gather(own_part, 'mp', axis=2, tiled=True)  12.4 us
    reduce_sum x1, other arithmetic, body(): totals = jnp.sum(exponent, axis=-1)  9.94 us
  transfers between devices with their start and end apart: 6, of which 6 were waited for; matrix products, arithmetic and copies ran while one was open for 17% of the time, Pallas kernels for 0%

commit v1 on v0

--- a/solution.py
+++ b/solution.py
@@ -1,9 +1,16 @@
+import functools
+
 import jax
 import jax.numpy as jnp
 from jax import lax
+from jax.experimental import pallas as pl
+from jax.experimental.pallas import tpu as pltpu
 from jax.sharding import PartitionSpec as P
 
 DH = 64
+LANES = 128
+SCALE = 0.25 * 1.4426950408889634
+MIB = 1024 * 1024
 
 
 def passed_along(value, axis, steps):
@@ -18,7 +25,7 @@
     return (widened * lax.rsqrt(square + 1e-06) * gain_row).astype(jnp.bfloat16)
 
 
-def body(hidden, memory, w_query, w_key, w_value, w_out, norm_gain, final_gain, lengths):
+def gathered_body(hidden, memory, w_query, w_key, w_value, w_out, norm_gain, final_gain, lengths):
     encoder_side = lax.axis_index("segment") == 0
     own_part = hidden[0]
     arrived = passed_along(memory[0], "segment", 1)
@@ -46,7 +53,6 @@
     key_piece = lax.all_gather(keys, "seq", axis=1, tiled=True)
     value_piece = lax.all_gather(values, "seq", axis=1, tiled=True)
     key_count = key_piece.shape[1]
-    running_max = jnp.full((batch, row_count, local_heads), -1e30, jnp.float32)
     scores = (
         jnp.einsum(
             "bqhd,bkhd->bqhk",
@@ -59,8 +65,8 @@
     visible = jnp.arange(key_count)[None, :] < key_length[:, None]
     mask = visible[:, None, None, :]
     scores = jnp.where(mask, scores, -1e30)
-    new_max = jnp.maximum(running_max, jnp.max(scores, axis=-1))
-    exponent = jnp.where(mask, jnp.exp(scores - new_max[..., None]), 0.0)
+    largest = jnp.max(scores, axis=-1)
+    exponent = jnp.where(mask, jnp.exp(scores - largest[..., None]), 0.0)
     totals = jnp.sum(exponent, axis=-1)
     weighted = jnp.einsum(
         "bqhk,bkhd->bqhd",
@@ -68,9 +74,7 @@
         value_piece.reshape(batch, key_count, local_heads, DH),
         preferred_element_type=jnp.float32,
     )
-    numerator = weighted
-    running_max, totals, numerator = (new_max, totals, numerator)
-    context = numerator / totals[..., None]
+    context = weighted / totals[..., None]
     positions = lax.axis_index("seq") * row_count + jnp.arange(row_count)
     live_rows = positions[None, :] < query_length[:, None]
     context = jnp.where(live_rows[:, :, None, None], context, 0.0)
@@ -83,21 +87,334 @@
     return (own_part.astype(jnp.float32) + branch).astype(jnp.bfloat16)[None]
 
 
+HEAD, SIDE, INNER, ENC = 0, 1, 2, 3
+BLOCK = 4
+
+
+def project_kernel(steps, table, qo, qn, ko, kn, gain, last_gain, wq, wk, wv, *rest):
+    outs, (xq, xk) = rest[:steps], rest[steps:]
+    step = pl.program_id(0)
+    half = qo.shape[1]
+    side = table[SIDE]
+
+    @pl.when(step == 0)
+    def _():
+        encoder = table[ENC] == 1
+
+        def fill(own, other, gains, into):
+            a = own.astype(jnp.float32)
+            b = other.astype(jnp.float32)
+            square = jnp.sum(a * a, axis=-1, keepdims=True) + jnp.sum(b * b, axis=-1, keepdims=True)
+            factor = lax.rsqrt(square / (2 * half) + 1e-06)
+            into[0] = (a * factor * gains(side)).astype(jnp.bfloat16)
+            into[1] = (b * factor * gains(1 - side)).astype(jnp.bfloat16)
+
+        fill(qo[...], qn[...], lambda s: gain[pl.ds(s, 1), :], xq)
+
+        @pl.when(encoder)
+        def _():
+            xk[...] = xq[...]
+
+        @pl.when(jnp.logical_not(encoder))
+        def _():
+            fill(ko[...], kn[...], lambda s: last_gain[pl.ds(s, 1), :], xk)
+
+    def rows(s):
+        return pl.ds(pl.multiple_of(s * half, half), half)
+
+    def times(x, w):
+        total = jnp.dot(x[0], w[rows(side), :], preferred_element_type=jnp.float32)
+        total += jnp.dot(x[1], w[rows(1 - side), :], preferred_element_type=jnp.float32)
+        return total.astype(jnp.bfloat16)
+
+    width = wq.shape[1]
+    products = [times(xq, wq), times(xk, wk), times(xk, wv)]
+    for i in range(steps):
+
+        @pl.when(step == i)
+        def _(i=i):
+            for place, product in enumerate(products):
+                outs[i][:, place * width : (place + 1) * width] = product
+
+
+def project(table, turns, qo, qn, ko, kn, gain, last_gain, wq, wk, wv, width):
+    rows, half = qo.shape
+    steps = len(turns)
+
+    def weight_block(i, table):
+        turn = sum((jnp.where(i == n, t, 0) for n, t in enumerate(turns)), 0)
+        return (0, table[HEAD] ^ turn)
+
+    whole = lambda i, table: (0, 0)
+    part = pl.BlockSpec((rows, half), whole)
+    gains = pl.BlockSpec((2, half), whole)
+    weight = pl.BlockSpec((2 * half, width), weight_block)
+    return pl.pallas_call(
+        functools.partial(project_kernel, steps),
+        out_shape=[jax.ShapeDtypeStruct((rows, 3 * width), jnp.bfloat16)] * steps,
+        grid_spec=pltpu.PrefetchScalarGridSpec(
+            num_scalar_prefetch=1,
+            grid=(steps,),
+            in_specs=[part] * 4 + [gains] * 2 + [weight] * 3,
+            out_specs=[pl.BlockSpec((rows, 3 * width), whole)] * steps,
+            scratch_shapes=[pltpu.VMEM((2, rows, half), jnp.bfloat16)] * 2,
+        ),
+        compiler_params=pltpu.CompilerParams(vmem_limit_bytes=24 * MIB),
+        cost_estimate=pl.CostEstimate(
+            flops=2 * rows * 2 * half * 3 * width * steps,
+            bytes_accessed=2 * (4 * rows * half + 6 * half * width * steps + rows * 3 * width * steps),
+            transcendentals=0,
+        ),
+    )(table, qo, qn, ko, kn, gain, last_gain, wq, wk, wv)
+
+
+def attend_kernel(blocks, table, lengths, *refs):
+    q_refs, k_refs, v_refs = refs[:blocks], refs[blocks : 2 * blocks], refs[2 * blocks : 3 * blocks]
+    outs = refs[3 * blocks : 3 * blocks + blocks // 2]
+    qs, ks, vs = refs[3 * blocks + blocks // 2 :]
+    rows = q_refs[0].shape[0]
+    key_length = lengths[2 * table[INNER] + 1]
+    query_length = lengths[2 * table[INNER]]
+    lane = lax.broadcasted_iota(jnp.int32, (rows, LANES), 1)
+    low = lane < DH
+    row = lax.broadcasted_iota(jnp.int32, (rows, LANES), 0)
+    zero = jnp.zeros((rows, LANES), jnp.bfloat16)
+    one = jnp.ones((rows, LANES), jnp.bfloat16)
+    unit = jnp.where(lane == 0, one, zero)
+    for j in range(blocks):
+        here = pl.ds(j * rows, rows)
+        qs[here, :LANES] = q_refs[j][...]
+        qs[here, LANES:] = unit
+        key = k_refs[j][...]
+        hides = jnp.logical_and(lane == 0, row + table[BLOCK + j] >= key_length)
+        bias = jnp.where(hides, -1e30, 0.0).astype(jnp.bfloat16)
+        value = v_refs[j][...]
+        ks[0, here, :LANES] = jnp.where(low, key, zero)
+        ks[1, here, :LANES] = jnp.where(low, zero, key)
+        ks[0, here, LANES:] = bias
+        ks[1, here, LANES:] = bias
+        vs[0, here, :] = jnp.where(low, value, one)
+        vs[1, here, :] = jnp.where(low, one, value)
+
+    for j in range(blocks):
+        query = qs[pl.ds(j * rows, rows), :]
+        sums = []
+        for head in range(2):
+            scores = lax.dot_general(
+                query, ks[head], (((1,), (1,)), ((), ())), preferred_element_type=jnp.float32
+            )
+            largest = jnp.max(scores, axis=-1, keepdims=True)
+            weights = jnp.exp2((scores - largest) * SCALE).astype(jnp.bfloat16)
+            sums.append(jnp.dot(weights, vs[head], preferred_element_type=jnp.float32))
+        weighted = jnp.where(low, sums[0], sums[1])
+        totals = jnp.where(low, pltpu.roll(sums[0], DH, 1), pltpu.roll(sums[1], DH, 1))
+        live = row + table[BLOCK + j] < query_length
+        context = jnp.where(live, weighted / totals, 0.0).astype(jnp.bfloat16)
+        outs[j // 2][pl.ds((j % 2) * rows, rows), :] = context
+
+
+def attend(table, lengths, parts, pair, pairs):
+    blocks = len(parts)
+    rows = parts[0].shape[0]
+    count = blocks * rows
+
+    def column(place):
+        return pl.BlockSpec((rows, LANES), lambda i, table, lengths: (0, place * pairs + pair))
+
+    return pl.pallas_call(
+        functools.partial(attend_kernel, blocks),
+        out_shape=[jax.ShapeDtypeStruct((2 * rows, LANES), jnp.bfloat16)] * (blocks // 2),
+        grid_spec=pltpu.PrefetchScalarGridSpec(
+            num_scalar_prefetch=2,
+            grid=(1,),
+            in_specs=[column(0)] * blocks + [column(1)] * blocks + [column(2)] * blocks,
+            out_specs=[pl.BlockSpec((2 * rows, LANES), lambda i, table, lengths: (0, 0))] * (blocks // 2),
+            scratch_shapes=[
+                pltpu.VMEM((count, 2 * LANES), jnp.bfloat16),
+                pltpu.VMEM((2, count, 2 * LANES), jnp.bfloat16),
+                pltpu.VMEM((2, count, LANES), jnp.bfloat16),
+            ],
+        ),
+        compiler_params=pltpu.CompilerParams(vmem_limit_bytes=32 * MIB),
+        cost_estimate=pl.CostEstimate(
+            flops=4 * count * count * 2 * LANES,
+            bytes_accessed=8 * count * LANES,
+            transcendentals=2 * count * count,
+        ),
+    )(table, lengths, *parts, *parts, *parts)
+
+
+def output_kernel(count, pairs, table, w, *refs):
+    pieces, (first, second), x = refs[: count * pairs], refs[count * pairs : count * pairs + 2], refs[-1]
+    for turn in range(count):
+        for pair in range(pairs):
+            place = (table[HEAD] ^ turn) * pairs + pair
+            x[:, pl.ds(pl.multiple_of(place * LANES, LANES), LANES)] = pieces[turn * pairs + pair][...]
+    total = jnp.dot(x[...], w[...], preferred_element_type=jnp.float32).astype(jnp.bfloat16)
+    rows = first.shape[0]
+    first[...] = total[:rows]
+    second[...] = total[rows:]
+
+
+def output_part(table, pieces, w_out, count, pairs, own):
+    rows, depth, half = pieces[0].shape[0] // 2, w_out.shape[0], w_out.shape[1] // 2
+
+    def weight_block(i, table):
+        return (0, table[SIDE] if own else 1 - table[SIDE])
+
+    return pl.pallas_call(
+        functools.partial(output_kernel, count, pairs),
+        out_shape=[jax.ShapeDtypeStruct((rows, half), jnp.bfloat16)] * 2,
+        grid_spec=pltpu.PrefetchScalarGridSpec(
+            num_scalar_prefetch=1,
+            grid=(1,),
+            in_specs=[pl.BlockSpec((depth, half), weight_block)]
+            + [pl.BlockSpec((2 * rows, LANES), lambda i, table: (0, 0))] * (count * pairs),
+            out_specs=[pl.BlockSpec((rows, half), lambda i, table: (0, 0))] * 2,
+            scratch_shapes=[pltpu.VMEM((2 * rows, depth), jnp.bfloat16)],
+        ),
+        compiler_params=pltpu.CompilerParams(vmem_limit_bytes=24 * MIB),
+        cost_estimate=pl.CostEstimate(
+            flops=4 * rows * depth * half,
+            bytes_accessed=2 * (depth * half + 2 * rows * depth + 2 * rows * half),
+            transcendentals=0,
+        ),
+    )(table, w_out, *pieces)
+
+
+def add_kernel(table, hidden, own, beside, across, corner, out):
+    def total(a, b):
+        out[0, 0] = (
+            hidden[0, 0].astype(jnp.float32) + (a[...].astype(jnp.float32) + b[...].astype(jnp.float32))
+        ).astype(jnp.bfloat16)
+
+    @pl.when(pl.program_id(0) == 0)
+    def _():
+        total(own, beside)
+
+    @pl.when(pl.program_id(0) == 1)
+    def _():
+        total(across, corner)
+
+
+def add_all(table, hidden, own, beside, across, corner):
+    rows, half = own.shape
+    block = pl.BlockSpec((1, 1, rows, half), lambda i, table: (0, table[INNER] ^ i, 0, 0))
+    part = pl.BlockSpec((rows, half), lambda i, table: (0, 0))
+    return pl.pallas_call(
+        add_kernel,
+        out_shape=jax.ShapeDtypeStruct(hidden.shape, jnp.bfloat16),
+        grid_spec=pltpu.PrefetchScalarGridSpec(
+            num_scalar_prefetch=1,
+            grid=(2,),
+            in_specs=[block, part, part, part, part],
+            out_specs=block,
+        ),
+        compiler_params=pltpu.CompilerParams(vmem_limit_bytes=16 * MIB),
+    )(table, hidden, own, beside, across, corner)
+
+
+def body(hidden, memory, w_query, w_key, w_value, w_out, norm_gain, final_gain, lengths):
+    seq, mp = lax.axis_size("seq"), lax.axis_size("mp")
+    count = seq // 2
+    rows, half = hidden.shape[2:]
+    width = w_query.shape[2] // count
+    pairs = width // LANES
+
+    place, side = lax.axis_index("seq"), lax.axis_index("mp")
+    outer, inner = place // 2, place % 2
+    encoder = (lax.axis_index("segment") == 0).astype(jnp.int32)
+    starts = [
+        (2 * (outer ^ turn) + (inner ^ chunk)) * rows for turn in range(count) for chunk in range(2)
+    ]
+    table = jnp.stack([outer, side, inner, encoder] + starts).astype(jnp.int32)
+
+    def moved(value, swap_seq, swap_mp):
+        pairs = [
+            (s * mp + m, (s ^ swap_seq) * mp + (m ^ swap_mp)) for s in range(seq) for m in range(mp)
+        ]
+        return lax.ppermute(value, ("seq", "mp"), pairs)
+
+    def handed(value, swap_seq, swap_mp):
+        pairs = [
+            (s * mp + m, seq * mp + (s ^ swap_seq) * mp + (m ^ swap_mp)) for s in range(seq) for m in range(mp)
+        ]
+        return lax.ppermute(value, ("segment", "seq", "mp"), pairs)
+
+    def turned(value, turn):
+        return lax.ppermute(value, "seq", [(s, s ^ (2 * turn)) for s in range(seq)])
+
+    hidden_own = lax.dynamic_index_in_dim(hidden[0], inner, 0, keepdims=False)
+    hidden_away = lax.dynamic_index_in_dim(hidden[0], 1 - inner, 0, keepdims=False)
+    memory_own = lax.dynamic_index_in_dim(memory[0], inner, 0, keepdims=False)
+    memory_away = lax.dynamic_index_in_dim(memory[0], 1 - inner, 0, keepdims=False)
+
+    query_beside = moved(hidden_own, 0, 1)
+    source_beside = handed(memory_own, 0, 1)
+    source_here = handed(memory_own, 0, 0)
+    query_corner = moved(hidden_away, 1, 1)
+    source_corner = handed(memory_away, 1, 1)
+    query_across = moved(hidden_away, 1, 0)
+    source_across = handed(memory_away, 1, 0)
+
+    gain = norm_gain[0].reshape(2, half)
+    last_gain = final_gain.reshape(2, half)
+    weights = (w_query[0], w_key[0], w_value[0])
+    turns = tuple(range(count - 1, -1, -1))
+    chunks = []
+    for qo, qn, ko, kn in (
+        (hidden_own, query_beside, source_here, source_beside),
+        (query_across, query_corner, source_across, source_corner),
+    ):
+        products = project(table, turns, qo, qn, ko, kn, gain, last_gain, *weights, width)
+        chunks.append({t: turned(p, t) if t else p for t, p in zip(turns, products)})
+    parts = [chunks[chunk][turn] for turn in range(count) for chunk in range(2)]
+
+    pieces = [[None] * pairs for _ in range(count)]
+    for pair in range(pairs):
+        contexts = attend(table, lengths.reshape(-1), parts, pair, pairs)
+        for turn in turns:
+            pieces[turn][pair] = turned(contexts[turn], turn) if turn else contexts[turn]
+    flat = [piece for row in pieces for piece in row]
+
+    beside, corner = output_part(table, flat, w_out[0], count, pairs, False)
+    corner = moved(corner, 1, 1)
+    beside = moved(beside, 0, 1)
+    own, across = output_part(table, flat, w_out[0], count, pairs, True)
+    across = moved(across, 1, 0)
+    return add_all(table, hidden, own, beside, across, corner)
+
+
 def solution(mesh):
-    return jax.shard_map(
-        body,
-        mesh=mesh,
-        in_specs=(
-            P("segment", None, "seq", "mp"),
-            P("segment", None, "seq", "mp"),
-            P("segment", None, "mp"),
-            P("segment", None, "mp"),
-            P("segment", None, "mp"),
-            P("segment", "mp", None),
-            P("segment", None),
-            P(),
-            P("segment", None, None),
-        ),
-        out_specs=P("segment", None, "seq", "mp"),
-        check_vma=False,
-    )
+    seq, mp = mesh.shape["seq"], mesh.shape["mp"]
+
+    def chosen(*arrays):
+        batch, columns = arrays[0].shape[1], arrays[2].shape[2]
+        count = seq // 2
+        fits = (
+            batch == 2
+            and mp == 2
+            and seq % 2 == 0
+            and count & (count - 1) == 0
+            and (columns // mp) % (count * LANES) == 0
+            and (arrays[0].shape[2] // seq) % 16 == 0
+        )
+        return jax.shard_map(
+            body if fits else gathered_body,
+            mesh=mesh,
+            in_specs=(
+                P("segment", None, "seq", "mp"),
+                P("segment", None, "seq", "mp"),
+                P("segment", None, "mp"),
+                P("segment", None, "mp"),
+                P("segment", None, "mp"),
+                P("segment", "mp", None),
+                P("segment", None),
+                P(),
+                P("segment", None, None),
+            ),
+            out_specs=P("segment", None, "seq", "mp"),
+            check_vma=False,
+        )(*arrays)
+
+    return chosen

time: 299 us -> 136 us (0.45)
  waiting for transfers between devices: 198 us -> 51.4 us
  matrix products: 43.6 us -> 0 us
  Pallas kernels: 0 us -> 36.1 us
  starting transfers between devices: 2.73 us -> 35.3 us
  other arithmetic: 21.7 us -> 1.27 us
  between operations: 13.3 us -> 0.13 us
  local copies, waits for them, and re-layouts: 18.3 us -> 10.9 us
    all_gather x4 -> x0, waiting for transfers between devices: 174 us -> none  [the longest x1 80.6 us: body(): key_piece = lax.all_gather(keys, 'seq', axis=1, tiled=True)]
    ppermute x1 -> x22, waiting for transfers between devices: 1.87 us -> 51.4 us  [the longest x12 32 us: turned(): return lax.ppermute(value, 'seq', [(s, s ^ 2 * turn) for s in range(seq)])]
    dot_general x6 -> x0, matrix products: 43.6 us -> none  [the longest x1 13.2 us: body(): jnp.einsum('bqhk,bkhd->bqhd', exponent.astype(jnp.bfloat16), value_piece....]
    pallas_call x0 -> x7, Pallas kernels: none -> 36.1 us  [the longest x2 19.5 us: attend(): pl.pallas_call(functools.partial(attend_kernel, blocks), out_shape=[jax.S...]
    ppermute x1 -> x22, starting transfers between devices: 2.39 us -> 35.3 us  [the longest x12 16.5 us: turned(): return lax.ppermute(value, 'seq', [(s, s ^ 2 * turn) for s in range(seq)])]
    reduce_scatter x1 -> x0, waiting for transfers between devices: 21.5 us -> none  [body(): lax.psum_scatter(partial_value.astype(jnp.bfloat16), 'mp', scatter_dimens...]
    all_gather x2 -> x0, local copies, waits for them, and re-layouts: 15.7 us -> none  [the longest x1 7.84 us: body(): key_piece = lax.all_gather(keys, 'seq', axis=1, tiled=True)]
    reduce_sum x3 -> x0, other arithmetic: 13.2 us -> none  [the longest x1 9.94 us: body(): totals = jnp.sum(exponent, axis=-1)]
  transfers between devices with their start and end apart: 6 -> 22, of which waited for: 6 -> 13; matrix products, arithmetic and copies ran while one was open for 17% -> 3% of each run, Pallas kernels for 0% -> 17%
where the time goes in v1:
time: 136 us; the launch traced here: 135 us
  waiting for transfers between devices  51.4 us (38%)
  Pallas kernels  36.1 us (27%)
  starting transfers between devices  35.3 us (26%)
  local copies, waits for them, and re-layouts  10.9 us (8%)
    ppermute x12, waiting for transfers between devices, turned(): return lax.ppermute(value, 'seq', [(s, s ^ 2 * turn) for s in range(seq)])  32 us
    pallas_call x2, Pallas kernels, attend(): pl.pallas_call(functools.partial(attend_kernel, blocks), out_shape=[jax.S...  19.5 us
    ppermute x12, starting transfers between devices, turned(): return lax.ppermute(value, 'seq', [(s, s ^ 2 * turn) for s in range(seq)])  16.5 us
    ppermute x6, waiting for transfers between devices, moved(): return lax.ppermute(value, ('seq', 'mp'), pairs)  16.3 us
    pallas_call x2, Pallas kernels, project(): pl.pallas_call(functools.partial(project_kernel, steps), out_shape=[jax.S...  12 us
    ppermute x4, starting transfers between devices, handed(): return lax.ppermute(value, ('segment', 'seq', 'mp'), pairs)  11.6 us
    ppermute x6, starting transfers between devices, moved(): return lax.ppermute(value, ('seq', 'mp'), pairs)  7.24 us
    unnamed x15, local copies, waits for them, and re-layouts  7.06 us
  transfers between devices with their start and end apart: 22, of which 13 were waited for; matrix products, arithmetic and copies ran while one was open for 3% of the time, Pallas kernels for 17%

profile of v1, /device:TPU:0, one launch (start us, length us, event | category | flops | bytes accessed | tf_op | source)
XLA Modules:
  0.0 135.2 jit_solution(1721770544758072908)
XLA Ops:
  0.0 1.8 %dynamic-slice_bitcast_fusion = (bf16[160,1024]{1,0:T(8,128)(2,1)S(1)}, bf16[160,1024]{1,0:T(8,128)(2,1)}) fusion(bf16[1,2,160,1024]{3,2,1,0:T(8,128)(2,1)} %param.10, s32[]{:T(128)S(6)} %select_n.23, s32[]{:T(128)S(6)} %select_n.22), kind=kLoop, calls=%fused_computation | loop fusion | bytes 1310728 | tf_op jit(solution)/shard_map/jit(dynamic_index_in_dim)/squeeze | solution.py:350
  1.8 4.3 %collective-permute-start.5 = (bf16[160,1024]{1,0:T(8,128)(2,1)S(1)}, bf16[160,1024]{1,0:T(8,128)(2,1)S(1)}, u32[]{:S(2)}, u32[]{:S(2)}) collective-permute-start(bf16[160,1024]{1,0:T(8,128)(2,1)S(1)} %get-tuple-element.45), channel_id=1, source_target_pairs={{0,18},{1,19},{2,16},{3,17},{4,22},{5,23},{6,20},{7,21},{8,26},{9,... | collective-permute-start | bytes 983048 | tf_op jit(solution)/shard_map/ppermute | solution.py:342
  6.1 2.2 %collective-permute-start.6 = (bf16[160,1024]{1,0:T(8,128)(2,1)S(1)}, bf16[160,1024]{1,0:T(8,128)(2,1)S(1)}, u32[]{:S(2)}, u32[]{:S(2)}) collective-permute-start(bf16[160,1024]{1,0:T(8,128)(2,1)S(1)} %get-tuple-element.45), channel_id=1, source_target_pairs={{0,19},{1,18},{2,17},{3,16},{4,23},{5,22},{6,21},{7,20},{8,27},{9,... | collective-permute-start | bytes 983048 | tf_op jit(solution)/shard_map/ppermute | solution.py:342
  8.4 1.1 dynamic-slice_bitcast_fusion.1
  9.5 0.6 collective-permute-start.3
  10.1 1.5 %collective-permute-start.4 = (bf16[160,1024]{1,0:T(8,128)(2,1)S(1)}, bf16[160,1024]{1,0:T(8,128)(2,1)S(1)}, u32[]{:S(2)}, u32[]{:S(2)}) collective-permute-start(bf16[160,1024]{1,0:T(8,128)(2,1)S(1)} %get-tuple-element.47), channel_id=1, source_target_pairs={{0,3},{1,2},{2,1},{3,0},{4,7},{5,6},{6,5},{7,4},{8,11},{9,10},{10,... | collective-permute-start | bytes 983048 | tf_op jit(solution)/shard_map/ppermute | solution.py:336
  11.6 1.3 collective-permute-start.1
  12.9 0.0 collective-permute-done.5.ko
  12.9 3.7 %collective-permute-start.2 = (bf16[160,1024]{1,0:T(8,128)(2,1)}, bf16[160,1024]{1,0:T(8,128)(2,1)S(1)}, u32[]{:S(2)}, u32[]{:S(2)}) collective-permute-start(bf16[160,1024]{1,0:T(8,128)(2,1)} %get-tuple-element.46), channel_id=1, source_target_pairs={{0,17},{1,16},{2,19},{3,18},{4,21},{5,20},{6,23},{7,22},{8,25},{9,... | collective-permute-start | bytes 983048 | tf_op jit(solution)/shard_map/ppermute | solution.py:342
  16.7 3.2 %collective-permute-done.6.kn = bf16[160,1024]{1,0:T(8,128)(2,1)S(1)} collective-permute-done((bf16[160,1024]{1,0:T(8,128)(2,1)S(1)}, bf16[160,1024]{1,0:T(8,128)(2,1)S(1)}, u32[]{:S(2)}, u32[]{:S(2)}) %collective-permute-start.6) | collective-permute-done | bytes 327712 | tf_op jit(solution)/shard_map/ppermute | solution.py:342
  19.9 1.5 %collective-permute-start = (bf16[160,1024]{1,0:T(8,128)(2,1)S(1)}, bf16[160,1024]{1,0:T(8,128)(2,1)S(1)}, u32[]{:S(2)}, u32[]{:S(2)}) collective-permute-start(bf16[160,1024]{1,0:T(8,128)(2,1)S(1)} %get-tuple-element.48.qo), channel_id=1, source_target_pairs={{0,1},{1,0},{2,3},{3,2},{4,5},{5,4},{6,7},{7,6},{8,9},{9,8},{10,11... | collective-permute-start | bytes 983048 | tf_op jit(solution)/shard_map/ppermute | solution.py:336
  21.4 0.5 broadcast.5
  21.9 1.3 reduce.3
  23.2 0.7 reshape.16.last_gain
  23.9 0.1 stack.55.table
  24.0 1.2 collective-permute-done.3.qo
  25.1 5.2 %collective-permute-done.4.qn = bf16[160,1024]{1,0:T(8,128)(2,1)S(1)} collective-permute-done((bf16[160,1024]{1,0:T(8,128)(2,1)S(1)}, bf16[160,1024]{1,0:T(8,128)(2,1)S(1)}, u32[]{:S(2)}, u32[]{:S(2)}) %collective-permute-start.4) | collective-permute-done | bytes 327712 | tf_op jit(solution)/shard_map/ppermute | solution.py:336
  30.3 2.2 %copy-done.1 = bf16[1,2048,1024]{2,1,0:T(8,128)(2,1)S(1)} copy-done((bf16[1,2048,1024]{2,1,0:T(8,128)(2,1)S(1)}, bf16[1,2048,1024]{2,1,0:T(8,128)(2,1)}, u32[]{:S(2)}) %copy-start.1) | copy-done | bytes 4194328
  32.5 2.2 %copy-done.3 = bf16[1,2048,1024]{2,1,0:T(8,128)(2,1)S(1)} copy-done((bf16[1,2048,1024]{2,1,0:T(8,128)(2,1)S(1)}, bf16[1,2048,1024]{2,1,0:T(8,128)(2,1)}, u32[]{:S(2)}) %copy-start.3) | copy-done | bytes 4194328
  34.7 2.2 %copy-done.4 = bf16[1,2048,1024]{2,1,0:T(8,128)(2,1)S(1)} copy-done((bf16[1,2048,1024]{2,1,0:T(8,128)(2,1)S(1)}, bf16[1,2048,1024]{2,1,0:T(8,128)(2,1)}, u32[]{:S(2)}) %copy-start.4) | copy-done | bytes 4194328
  36.9 5.6 %shard_map.92 = (bf16[160,768]{1,0:T(8,128)(2,1)S(1)}, bf16[160,768]{1,0:T(8,128)(2,1)S(1)}, bf16[160,768]{1,0:T(8,128)(2,1)S(1)}, bf16[160,768]{1,0:T(8,128)(2,1)S(1)}) custom-call(s32[12]{0:T(128)S(1)} %stack.55.table, bf16[160,1024]{1,0:T(8,128)(2,1)S(1)} %collective-permute-done.3.qo, bf16[160,1024]{1,0:T(8,128)(2,1)S(1)} %collective-permute-done.4.qn, ...), custom_call_target="tpu_custom_call" | custom-call | flops 2013265920 | bytes 14876672 | tf_op jit(solution)/shard_map/pallas_call | solution.py:152
  42.5 2.7 %collective-permute-start.10 = (bf16[160,768]{1,0:T(8,128)(2,1)S(1)}, bf16[160,768]{1,0:T(8,128)(2,1)S(1)}, u32[]{:S(2)}, u32[]{:S(2)}) collective-permute-start(bf16[160,768]{1,0:T(8,128)(2,1)S(1)} %get-tuple-element.30), channel_id=1, source_target_pairs={{0,8},{2,10},{4,12},{6,14},{8,0},{10,2},{12,4},{14,6},{1,9},{3,11}... | collective-permute-start | bytes 737288 | tf_op jit(solution)/shard_map/ppermute | solution.py:345
  45.2 1.4 collective-permute-start.12
  46.5 0.0 collective-permute-done.1.ko
  46.5 0.3 collective-permute-start.8
  46.8 0.0 collective-permute-done.2.kn
  46.8 0.0 collective-permute-done.qn
  46.8 6.4 %shard_map.91 = (bf16[160,768]{1,0:T(8,128)(2,1)}, bf16[160,768]{1,0:T(8,128)(2,1)}, bf16[160,768]{1,0:T(8,128)(2,1)}, bf16[160,768]{1,0:T(8,128)(2,1)S(1)}) custom-call(s32[12]{0:T(128)S(1)} %stack.55.table, bf16[160,1024]{1,0:T(8,128)(2,1)S(1)} %get-tuple-element.48.qo, bf16[160,1024]{1,0:T(8,128)(2,1)S(1)} %collective-permute-done.qn, ...), custom_call_target="tpu_custom_call" | custom-call | flops 2013265920 | bytes 14876672 | tf_op jit(solution)/shard_map/pallas_call | solution.py:152
  53.3 2.9 %collective-permute-start.11 = (bf16[160,768]{1,0:T(8,128)(2,1)}, bf16[160,768]{1,0:T(8,128)(2,1)S(1)}, u32[]{:S(2)}, u32[]{:S(2)}) collective-permute-start(bf16[160,768]{1,0:T(8,128)(2,1)} %get-tuple-element.31), channel_id=1, source_target_pairs={{0,12},{2,14},{4,8},{6,10},{8,4},{10,6},{12,0},{14,2},{1,13},{3,15... | collective-permute-start | bytes 737288 | tf_op jit(solution)/shard_map/ppermute | solution.py:345
  56.1 0.5 collective-permute-start.7
  56.6 3.8 %collective-permute-done.10.refs_5_.refs_13_.refs_21_ = bf16[160,768]{1,0:T(8,128)(2,1)S(1)} collective-permute-done((bf16[160,768]{1,0:T(8,128)(2,1)S(1)}, bf16[160,768]{1,0:T(8,128)(2,1)S(1)}, u32[]{:S(2)}, u32[]{:S(2)}) %collective-permute-start.10) | collective-permute-done | bytes 245792 | tf_op jit(solution)/shard_map/ppermute | solution.py:345
  60.3 0.0 collective-permute-start.9
  60.3 0.1 reshape.15.lengths
  60.4 0.0 collective-permute-done.12.refs_7_.refs_15_.refs_23_
  60.4 1.1 collective-permute-done.8.refs_3_.refs_11_.refs_19_
  61.5 6.7 %collective-permute-done.11.refs_6_.refs_14_.refs_22_ = bf16[160,768]{1,0:T(8,128)(2,1)S(1)} collective-permute-done((bf16[160,768]{1,0:T(8,128)(2,1)}, bf16[160,768]{1,0:T(8,128)(2,1)S(1)}, u32[]{:S(2)}, u32[]{:S(2)}) %collective-permute-start.11) | collective-permute-done | bytes 245792 | tf_op jit(solution)/shard_map/ppermute | solution.py:345
  68.2 0.8 collective-permute-done.7.refs_2_.refs_10_.refs_18_
  69.0 13.7 %collective-permute-done.9.refs_4_.refs_12_.refs_20_ = bf16[160,768]{1,0:T(8,128)(2,1)S(1)} collective-permute-done((bf16[160,768]{1,0:T(8,128)(2,1)}, bf16[160,768]{1,0:T(8,128)(2,1)S(1)}, u32[]{:S(2)}, u32[]{:S(2)}) %collective-permute-start.9) | collective-permute-done | bytes 245792 | tf_op jit(solution)/shard_map/ppermute | solution.py:345
  82.7 9.6 %shard_map.94 = (bf16[320,128]{1,0:T(8,128)(2,1)S(1)}, bf16[320,128]{1,0:T(8,128)(2,1)S(1)}, bf16[320,128]{1,0:T(8,128)(2,1)S(1)}, bf16[320,128]{1,0:T(8,128)(2,1)S(1)}) custom-call(s32[12]{0:T(128)S(1)} %stack.55.table, s32[4]{0:T(128)S(1)} %reshape.15.lengths, bf16[160,768]{1,0:T(8,128)(2,1)S(1)} %get-tuple-element.25.refs_0_.refs_8_.refs_16_, ...), custom_call_target="tpu_custom_call" | custom-call | flops 1677721600 | bytes 1310720 | tf_op jit(solution)/shard_map/pallas_call | solution.py:224
  92.3 0.0 copy-start
  92.3 0.9 collective-permute-start.14
  93.2 3.3 %collective-permute-start.16 = (bf16[320,128]{1,0:T(8,128)(2,1)S(1)}, bf16[320,128]{1,0:T(8,128)(2,1)S(1)}, u32[]{:S(2)}, u32[]{:S(2)}) collective-permute-start(bf16[320,128]{1,0:T(8,128)(2,1)S(1)} %get-tuple-element.38), channel_id=1, source_target_pairs={{0,8},{2,10},{4,12},{6,14},{8,0},{10,2},{12,4},{14,6},{1,9},{3,11}... | collective-permute-start | bytes 245768 | tf_op jit(solution)/shard_map/ppermute | solution.py:345
  96.5 0.3 collective-permute-start.18
  96.8 9.8 %shard_map.93 = (bf16[320,128]{1,0:T(8,128)(2,1)S(1)}, bf16[320,128]{1,0:T(8,128)(2,1)S(1)}, bf16[320,128]{1,0:T(8,128)(2,1)S(1)}, bf16[320,128]{1,0:T(8,128)(2,1)S(1)}) custom-call(s32[12]{0:T(128)S(1)} %stack.55.table, s32[4]{0:T(128)S(1)} %reshape.15.lengths, bf16[160,768]{1,0:T(8,128)(2,1)S(1)} %get-tuple-element.25.refs_0_.refs_8_.refs_16_, ...), custom_call_target="tpu_custom_call" | custom-call | flops 1677721600 | bytes 1310720 | tf_op jit(solution)/shard_map/pallas_call | solution.py:224
  106.6 0.3 collective-permute-start.13
  107.0 3.8 %collective-permute-start.15 = (bf16[320,128]{1,0:T(8,128)(2,1)S(1)}, bf16[320,128]{1,0:T(8,128)(2,1)S(1)}, u32[]{:S(2)}, u32[]{:S(2)}) collective-permute-start(bf16[320,128]{1,0:T(8,128)(2,1)S(1)} %get-tuple-element.37), channel_id=1, source_target_pairs={{0,8},{2,10},{4,12},{6,14},{8,0},{10,2},{12,4},{14,6},{1,9},{3,11}... | collective-permute-start | bytes 245768 | tf_op jit(solution)/shard_map/ppermute | solution.py:345
  110.8 0.0 collective-permute-done.14.refs_3_
  110.8 0.3 collective-permute-start.17
  111.1 0.0 collective-permute-done.16.refs_5_
  111.1 0.0 collective-permute-done.18.refs_7_
  111.1 0.2 collective-permute-done.13.refs_2_
  111.3 3.6 %collective-permute-done.15.refs_4_ = bf16[320,128]{1,0:T(8,128)(2,1)S(1)} collective-permute-done((bf16[320,128]{1,0:T(8,128)(2,1)S(1)}, bf16[320,128]{1,0:T(8,128)(2,1)S(1)}, u32[]{:S(2)}, u32[]{:S(2)}) %collective-permute-start.15) | collective-permute-done | bytes 81952 | tf_op jit(solution)/shard_map/ppermute | solution.py:345
  114.9 2.1 %collective-permute-done.17.refs_6_ = bf16[320,128]{1,0:T(8,128)(2,1)S(1)} collective-permute-done((bf16[320,128]{1,0:T(8,128)(2,1)S(1)}, bf16[320,128]{1,0:T(8,128)(2,1)S(1)}, u32[]{:S(2)}, u32[]{:S(2)}) %collective-permute-start.17) | collective-permute-done | bytes 81952 | tf_op jit(solution)/shard_map/ppermute | solution.py:345
  117.0 0.0 copy-done
  117.0 1.5 %shard_map.96 = (bf16[160,1024]{1,0:T(8,128)(2,1)S(1)}, bf16[160,1024]{1,0:T(8,128)(2,1)S(1)}) custom-call(s32[12]{0:T(128)S(1)} %stack.55.table, bf16[1024,2048]{1,0:T(8,128)(2,1)S(1)} %bitcast.24, bf16[320,128]{1,0:T(8,128)(2,1)S(1)} %get-tuple-element.33.refs_0_, bf16[320,128]{1,0:T(8,128)(2,1)S(1)} %get-tuple-element.34.refs_1_, ...), custom_call_target="tpu_custom_call" | custom-call | flops 671088640 | bytes 3407872 | tf_op jit(solution)/shard_map/pallas_call | solution.py:265
  118.6 1.6 %collective-permute-start.19 = (bf16[160,1024]{1,0:T(8,128)(2,1)S(1)}, bf16[160,1024]{1,0:T(8,128)(2,1)S(1)}, u32[]{:S(2)}, u32[]{:S(2)}) collective-permute-start(bf16[160,1024]{1,0:T(8,128)(2,1)S(1)} %get-tuple-element.42), channel_id=1, source_target_pairs={{0,1},{1,0},{2,3},{3,2},{4,5},{5,4},{6,7},{7,6},{8,9},{9,8},{10,11... | collective-permute-start | bytes 983048 | tf_op jit(solution)/shard_map/ppermute | solution.py:336
  120.2 1.4 %collective-permute-start.21 = (bf16[160,1024]{1,0:T(8,128)(2,1)S(1)}, bf16[160,1024]{1,0:T(8,128)(2,1)S(1)}, u32[]{:S(2)}, u32[]{:S(2)}) collective-permute-start(bf16[160,1024]{1,0:T(8,128)(2,1)S(1)} %get-tuple-element.44), channel_id=1, source_target_pairs={{0,3},{1,2},{2,1},{3,0},{4,7},{5,6},{6,5},{7,4},{8,11},{9,10},{10,... | collective-permute-start | bytes 983048 | tf_op jit(solution)/shard_map/ppermute | solution.py:336
  121.6 1.5 %shard_map.95 = (bf16[160,1024]{1,0:T(8,128)(2,1)S(1)}, bf16[160,1024]{1,0:T(8,128)(2,1)S(1)}) custom-call(s32[12]{0:T(128)S(1)} %stack.55.table, bf16[1024,2048]{1,0:T(8,128)(2,1)S(1)} %bitcast.25, bf16[320,128]{1,0:T(8,128)(2,1)S(1)} %get-tuple-element.33.refs_0_, bf16[320,128]{1,0:T(8,128)(2,1)S(1)} %get-tuple-element.34.refs_1_, ...), custom_call_target="tpu_custom_call" | custom-call | flops 671088640 | bytes 3407872 | tf_op jit(solution)/shard_map/pallas_call | solution.py:265
  123.1 0.6 collective-permute-start.20
  123.8 8.6 %collective-permute-done.19.beside = bf16[160,1024]{1,0:T(8,128)(2,1)S(1)} collective-permute-done((bf16[160,1024]{1,0:T(8,128)(2,1)S(1)}, bf16[160,1024]{1,0:T(8,128)(2,1)S(1)}, u32[]{:S(2)}, u32[]{:S(2)}) %collective-permute-start.19) | collective-permute-done | bytes 327712 | tf_op jit(solution)/shard_map/ppermute | solution.py:336
  132.4 0.0 collective-permute-done.21.corner
  132.4 1.3 collective-permute-done.20.across
  133.7 0.0 copy-done.5
  133.7 1.6 %shard_map.97 = bf16[1,2,160,1024]{3,2,1,0:T(8,128)(2,1)} custom-call(s32[12]{0:T(128)S(1)} %stack.55.table, bf16[1,2,160,1024]{3,2,1,0:T(8,128)(2,1)S(1)} %copy-done.5, bf16[160,1024]{1,0:T(8,128)(2,1)S(1)} %get-tuple-element.41.own, bf16[160,1024]{1,0:T(8,128)(2,1)S(1)} %collective-permute-done.19.beside, ...), custom_call_target="tpu_custom_call" | custom-call | tf_op jit(solution)/shard_map/pallas_call | solution.py:304
  (9 shorter events, 0.0 us)
Async XLA Ops:
  1.8 11.1 %collective-permute-start.5 = (bf16[160,1024]{1,0:T(8,128)(2,1)S(1)}, bf16[160,1024]{1,0:T(8,128)(2,1)S(1)}, u32[]{:S(2)}, u32[]{:S(2)}) collective-permute-start(bf16[160,1024]{1,0:T(8,128)(2,1)S(1)} %get-tuple-element.45), channel_id=1, source_target_pairs={{0,18},{1,19},{2,16},{3,17},{4,22},{5,23},{6,20},{7,21},{8,26},{9,... | collective-permute-start | bytes 983048 | tf_op jit(solution)/shard_map/ppermute | solution.py:342
  6.1 13.8 %collective-permute-start.6 = (bf16[160,1024]{1,0:T(8,128)(2,1)S(1)}, bf16[160,1024]{1,0:T(8,128)(2,1)S(1)}, u32[]{:S(2)}, u32[]{:S(2)}) collective-permute-start(bf16[160,1024]{1,0:T(8,128)(2,1)S(1)} %get-tuple-element.45), channel_id=1, source_target_pairs={{0,19},{1,18},{2,17},{3,16},{4,23},{5,22},{6,21},{7,20},{8,27},{9,... | collective-permute-start | bytes 983048 | tf_op jit(solution)/shard_map/ppermute | solution.py:342
  9.5 15.6 %collective-permute-start.3 = (bf16[160,1024]{1,0:T(8,128)(2,1)S(1)}, bf16[160,1024]{1,0:T(8,128)(2,1)S(1)}, u32[]{:S(2)}, u32[]{:S(2)}) collective-permute-start(bf16[160,1024]{1,0:T(8,128)(2,1)S(1)} %get-tuple-element.47), channel_id=1, source_target_pairs={{0,2},{1,3},{2,0},{3,1},{4,6},{5,7},{6,4},{7,5},{8,10},{9,11},{10,... | collective-permute-start | bytes 983048 | tf_op jit(solution)/shard_map/ppermute | solution.py:336
  10.1 20.2 %collective-permute-start.4 = (bf16[160,1024]{1,0:T(8,128)(2,1)S(1)}, bf16[160,1024]{1,0:T(8,128)(2,1)S(1)}, u32[]{:S(2)}, u32[]{:S(2)}) collective-permute-start(bf16[160,1024]{1,0:T(8,128)(2,1)S(1)} %get-tuple-element.47), channel_id=1, source_target_pairs={{0,3},{1,2},{2,1},{3,0},{4,7},{5,6},{6,5},{7,4},{8,11},{9,10},{10,... | collective-permute-start | bytes 983048 | tf_op jit(solution)/shard_map/ppermute | solution.py:336
  11.6 34.9 %collective-permute-start.1 = (bf16[160,1024]{1,0:T(8,128)(2,1)}, bf16[160,1024]{1,0:T(8,128)(2,1)S(1)}, u32[]{:S(2)}, u32[]{:S(2)}) collective-permute-start(bf16[160,1024]{1,0:T(8,128)(2,1)} %get-tuple-element.46), channel_id=1, source_target_pairs={{0,16},{1,17},{2,18},{3,19},{4,20},{5,21},{6,22},{7,23},{8,24},{9,... | collective-permute-start | bytes 983048 | tf_op jit(solution)/shard_map/ppermute | solution.py:342
  12.9 33.9 %collective-permute-start.2 = (bf16[160,1024]{1,0:T(8,128)(2,1)}, bf16[160,1024]{1,0:T(8,128)(2,1)S(1)}, u32[]{:S(2)}, u32[]{:S(2)}) collective-permute-start(bf16[160,1024]{1,0:T(8,128)(2,1)} %get-tuple-element.46), channel_id=1, source_target_pairs={{0,17},{1,16},{2,19},{3,18},{4,21},{5,20},{6,23},{7,22},{8,25},{9,... | collective-permute-start | bytes 983048 | tf_op jit(solution)/shard_map/ppermute | solution.py:342
  19.9 26.9 %collective-permute-start = (bf16[160,1024]{1,0:T(8,128)(2,1)S(1)}, bf16[160,1024]{1,0:T(8,128)(2,1)S(1)}, u32[]{:S(2)}, u32[]{:S(2)}) collective-permute-start(bf16[160,1024]{1,0:T(8,128)(2,1)S(1)} %get-tuple-element.48.qo), channel_id=1, source_target_pairs={{0,1},{1,0},{2,3},{3,2},{4,5},{5,4},{6,7},{7,6},{8,9},{9,8},{10,11... | collective-permute-start | bytes 983048 | tf_op jit(solution)/shard_map/ppermute | solution.py:336
  30.3 2.2 %copy-start.1 = (bf16[1,2048,1024]{2,1,0:T(8,128)(2,1)S(1)}, bf16[1,2048,1024]{2,1,0:T(8,128)(2,1)}, u32[]{:S(2)}) copy-start(bf16[1,2048,1024]{2,1,0:T(8,128)(2,1)} %param.11) | copy-start | bytes 12582916
  32.5 2.2 %copy-start.3 = (bf16[1,2048,1024]{2,1,0:T(8,128)(2,1)S(1)}, bf16[1,2048,1024]{2,1,0:T(8,128)(2,1)}, u32[]{:S(2)}) copy-start(bf16[1,2048,1024]{2,1,0:T(8,128)(2,1)} %param.12) | copy-start | bytes 12582916
  34.7 2.2 %copy-start.4 = (bf16[1,2048,1024]{2,1,0:T(8,128)(2,1)S(1)}, bf16[1,2048,1024]{2,1,0:T(8,128)(2,1)}, u32[]{:S(2)}) copy-start(bf16[1,2048,1024]{2,1,0:T(8,128)(2,1)} %param.13) | copy-start | bytes 12582916
  36.9 9.9 %copy-start.2 = (bf16[1,2048,1024]{2,1,0:T(8,128)(2,1)S(1)}, bf16[1,2048,1024]{2,1,0:T(8,128)(2,1)}, u32[]{:S(2)}) copy-start(bf16[1,2048,1024]{2,1,0:T(8,128)(2,1)} %param.11) | copy-start | bytes 12582916
  42.5 17.8 %collective-permute-start.10 = (bf16[160,768]{1,0:T(8,128)(2,1)S(1)}, bf16[160,768]{1,0:T(8,128)(2,1)S(1)}, u32[]{:S(2)}, u32[]{:S(2)}) collective-permute-start(bf16[160,768]{1,0:T(8,128)(2,1)S(1)} %get-tuple-element.30), channel_id=1, source_target_pairs={{0,8},{2,10},{4,12},{6,14},{8,0},{10,2},{12,4},{14,6},{1,9},{3,11}... | collective-permute-start | bytes 737288 | tf_op jit(solution)/shard_map/ppermute | solution.py:345
  45.2 15.2 %collective-permute-start.12 = (bf16[160,768]{1,0:T(8,128)(2,1)S(1)}, bf16[160,768]{1,0:T(8,128)(2,1)S(1)}, u32[]{:S(2)}, u32[]{:S(2)}) collective-permute-start(bf16[160,768]{1,0:T(8,128)(2,1)S(1)} %get-tuple-element.32), channel_id=1, source_target_pairs={{0,12},{2,14},{4,8},{6,10},{8,4},{10,6},{12,0},{14,2},{1,13},{3,15... | collective-permute-start | bytes 737288 | tf_op jit(solution)/shard_map/ppermute | solution.py:345
  46.5 13.8 %copy-start.6 = (s32[1,2,2]{2,1,0:T(2,128)S(1)}, s32[1,2,2]{2,1,0:T(2,128)}, u32[]{:S(2)}) copy-start(s32[1,2,2]{2,1,0:T(2,128)} %param.17) | copy-start | bytes 52
  46.5 15.0 %collective-permute-start.8 = (bf16[160,768]{1,0:T(8,128)(2,1)S(1)}, bf16[160,768]{1,0:T(8,128)(2,1)S(1)}, u32[]{:S(2)}, u32[]{:S(2)}) collective-permute-start(bf16[160,768]{1,0:T(8,128)(2,1)S(1)} %get-tuple-element.28), channel_id=1, source_target_pairs={{0,4},{2,6},{4,0},{6,2},{8,12},{10,14},{12,8},{14,10},{1,5},{3,7},... | collective-permute-start | bytes 737288 | tf_op jit(solution)/shard_map/ppermute | solution.py:345
  53.3 14.9 %collective-permute-start.11 = (bf16[160,768]{1,0:T(8,128)(2,1)}, bf16[160,768]{1,0:T(8,128)(2,1)S(1)}, u32[]{:S(2)}, u32[]{:S(2)}) collective-permute-start(bf16[160,768]{1,0:T(8,128)(2,1)} %get-tuple-element.31), channel_id=1, source_target_pairs={{0,12},{2,14},{4,8},{6,10},{8,4},{10,6},{12,0},{14,2},{1,13},{3,15... | collective-permute-start | bytes 737288 | tf_op jit(solution)/shard_map/ppermute | solution.py:345
  56.1 12.9 %collective-permute-start.7 = (bf16[160,768]{1,0:T(8,128)(2,1)}, bf16[160,768]{1,0:T(8,128)(2,1)S(1)}, u32[]{:S(2)}, u32[]{:S(2)}) collective-permute-start(bf16[160,768]{1,0:T(8,128)(2,1)} %get-tuple-element.27), channel_id=1, source_target_pairs={{0,4},{2,6},{4,0},{6,2},{8,12},{10,14},{12,8},{14,10},{1,5},{3,7},... | collective-permute-start | bytes 737288 | tf_op jit(solution)/shard_map/ppermute | solution.py:345
  60.3 22.4 %collective-permute-start.9 = (bf16[160,768]{1,0:T(8,128)(2,1)}, bf16[160,768]{1,0:T(8,128)(2,1)S(1)}, u32[]{:S(2)}, u32[]{:S(2)}) collective-permute-start(bf16[160,768]{1,0:T(8,128)(2,1)} %get-tuple-element.29), channel_id=1, source_target_pairs={{0,8},{2,10},{4,12},{6,14},{8,0},{10,2},{12,4},{14,6},{1,9},{3,11}... | collective-permute-start | bytes 737288 | tf_op jit(solution)/shard_map/ppermute | solution.py:345
  92.3 24.7 %copy-start = (bf16[1,1024,2048]{2,1,0:T(8,128)(2,1)S(1)}, bf16[1,1024,2048]{2,1,0:T(8,128)(2,1)}, u32[]{:S(2)}) copy-start(bf16[1,1024,2048]{2,1,0:T(8,128)(2,1)} %param.14) | copy-start | bytes 12582916
  92.3 18.4 %collective-permute-start.14 = (bf16[320,128]{1,0:T(8,128)(2,1)S(1)}, bf16[320,128]{1,0:T(8,128)(2,1)S(1)}, u32[]{:S(2)}, u32[]{:S(2)}) collective-permute-start(bf16[320,128]{1,0:T(8,128)(2,1)S(1)} %get-tuple-element.36), channel_id=1, source_target_pairs={{0,4},{2,6},{4,0},{6,2},{8,12},{10,14},{12,8},{14,10},{1,5},{3,7},... | collective-permute-start | bytes 245768 | tf_op jit(solution)/shard_map/ppermute | solution.py:345
  93.2 17.9 %collective-permute-start.16 = (bf16[320,128]{1,0:T(8,128)(2,1)S(1)}, bf16[320,128]{1,0:T(8,128)(2,1)S(1)}, u32[]{:S(2)}, u32[]{:S(2)}) collective-permute-start(bf16[320,128]{1,0:T(8,128)(2,1)S(1)} %get-tuple-element.38), channel_id=1, source_target_pairs={{0,8},{2,10},{4,12},{6,14},{8,0},{10,2},{12,4},{14,6},{1,9},{3,11}... | collective-permute-start | bytes 245768 | tf_op jit(solution)/shard_map/ppermute | solution.py:345
  96.5 14.6 %collective-permute-start.18 = (bf16[320,128]{1,0:T(8,128)(2,1)S(1)}, bf16[320,128]{1,0:T(8,128)(2,1)S(1)}, u32[]{:S(2)}, u32[]{:S(2)}) collective-permute-start(bf16[320,128]{1,0:T(8,128)(2,1)S(1)} %get-tuple-element.40), channel_id=1, source_target_pairs={{0,12},{2,14},{4,8},{6,10},{8,4},{10,6},{12,0},{14,2},{1,13},{3,15... | collective-permute-start | bytes 245768 | tf_op jit(solution)/shard_map/ppermute | solution.py:345
  106.6 4.7 %collective-permute-start.13 = (bf16[320,128]{1,0:T(8,128)(2,1)S(1)}, bf16[320,128]{1,0:T(8,128)(2,1)S(1)}, u32[]{:S(2)}, u32[]{:S(2)}) collective-permute-start(bf16[320,128]{1,0:T(8,128)(2,1)S(1)} %get-tuple-element.35), channel_id=1, source_target_pairs={{0,4},{2,6},{4,0},{6,2},{8,12},{10,14},{12,8},{14,10},{1,5},{3,7},... | collective-permute-start | bytes 245768 | tf_op jit(solution)/shard_map/ppermute | solution.py:345
  107.0 8.0 %collective-permute-start.15 = (bf16[320,128]{1,0:T(8,128)(2,1)S(1)}, bf16[320,128]{1,0:T(8,128)(2,1)S(1)}, u32[]{:S(2)}, u32[]{:S(2)}) collective-permute-start(bf16[320,128]{1,0:T(8,128)(2,1)S(1)} %get-tuple-element.37), channel_id=1, source_target_pairs={{0,8},{2,10},{4,12},{6,14},{8,0},{10,2},{12,4},{14,6},{1,9},{3,11}... | collective-permute-start | bytes 245768 | tf_op jit(solution)/shard_map/ppermute | solution.py:345
  110.8 6.2 %collective-permute-start.17 = (bf16[320,128]{1,0:T(8,128)(2,1)S(1)}, bf16[320,128]{1,0:T(8,128)(2,1)S(1)}, u32[]{:S(2)}, u32[]{:S(2)}) collective-permute-start(bf16[320,128]{1,0:T(8,128)(2,1)S(1)} %get-tuple-element.39), channel_id=1, source_target_pairs={{0,12},{2,14},{4,8},{6,10},{8,4},{10,6},{12,0},{14,2},{1,13},{3,15... | collective-permute-start | bytes 245768 | tf_op jit(solution)/shard_map/ppermute | solution.py:345
  117.0 16.6 %copy-start.5 = (bf16[1,2,160,1024]{3,2,1,0:T(8,128)(2,1)S(1)}, bf16[1,2,160,1024]{3,2,1,0:T(8,128)(2,1)}, u32[]{:S(2)}) copy-start(bf16[1,2,160,1024]{3,2,1,0:T(8,128)(2,1)} %hidden.1) | copy-start | bytes 1966084
  118.6 13.8 %collective-permute-start.19 = (bf16[160,1024]{1,0:T(8,128)(2,1)S(1)}, bf16[160,1024]{1,0:T(8,128)(2,1)S(1)}, u32[]{:S(2)}, u32[]{:S(2)}) collective-permute-start(bf16[160,1024]{1,0:T(8,128)(2,1)S(1)} %get-tuple-element.42), channel_id=1, source_target_pairs={{0,1},{1,0},{2,3},{3,2},{4,5},{5,4},{6,7},{7,6},{8,9},{9,8},{10,11... | collective-permute-start | bytes 983048 | tf_op jit(solution)/shard_map/ppermute | solution.py:336
  120.2 12.1 %collective-permute-start.21 = (bf16[160,1024]{1,0:T(8,128)(2,1)S(1)}, bf16[160,1024]{1,0:T(8,128)(2,1)S(1)}, u32[]{:S(2)}, u32[]{:S(2)}) collective-permute-start(bf16[160,1024]{1,0:T(8,128)(2,1)S(1)} %get-tuple-element.44), channel_id=1, source_target_pairs={{0,3},{1,2},{2,1},{3,0},{4,7},{5,6},{6,5},{7,4},{8,11},{9,10},{10,... | collective-permute-start | bytes 983048 | tf_op jit(solution)/shard_map/ppermute | solution.py:336
  123.1 10.5 %collective-permute-start.20 = (bf16[160,1024]{1,0:T(8,128)(2,1)S(1)}, bf16[160,1024]{1,0:T(8,128)(2,1)S(1)}, u32[]{:S(2)}, u32[]{:S(2)}) collective-permute-start(bf16[160,1024]{1,0:T(8,128)(2,1)S(1)} %get-tuple-element.43), channel_id=1, source_target_pairs={{0,2},{1,3},{2,0},{3,1},{4,6},{5,7},{6,4},{7,5},{8,10},{9,11},{10,... | collective-permute-start | bytes 983048 | tf_op jit(solution)/shard_map/ppermute | solution.py:336

commit v2 on v1

v2 whole, which is shorter than its diff:
```python
import functools

import jax
import jax.numpy as jnp
from jax import lax
from jax.experimental import pallas as pl
from jax.experimental.pallas import tpu as pltpu
from jax.sharding import PartitionSpec as P

DH = 64
LANES = 128
SCALE = 0.25 * 1.4426950408889634
MIB = 1024 * 1024


def passed_along(value, axis, steps):
    count = lax.axis_size(axis)
    leading, last = (max(0, -steps), min(count, count - steps))
    return lax.ppermute(value, axis, [(source, source + steps) for source in range(leading, last)])


def normalize(values, gain_row):
    widened = values.astype(jnp.float32)
    square = jnp.mean(widened * widened, axis=-1, keepdims=True)
    return (widened * lax.rsqrt(square + 1e-06) * gain_row).astype(jnp.bfloat16)


def gathered_body(hidden, memory, w_query, w_key, w_value, w_out, norm_gain, final_gain, lengths):
    encoder_side = lax.axis_index("segment") == 0
    own_part = hidden[0]
    arrived = passed_along(memory[0], "segment", 1)
    source_part = jnp.where(encoder_side, own_part, arrived)
    query_rows, source_rows = (
        lax.all_gather(own_part, "mp", axis=2, tiled=True),
        lax.all_gather(source_part, "mp", axis=2, tiled=True),
    )
    batch = own_part.shape[0]
    row_count = own_part.shape[1]
    width = query_rows.shape[2]
    key_gain = jnp.where(encoder_side, norm_gain[0], final_gain)
    query_in = normalize(query_rows.reshape(batch * row_count, width), norm_gain[0])
    key_in = normalize(source_rows.reshape(batch * row_count, width), key_gain)
    head_cols = w_query.shape[2]
    local_heads = head_cols // DH
    queries = jnp.dot(query_in, w_query[0], preferred_element_type=jnp.float32).astype(jnp.bfloat16)
    keys = jnp.dot(key_in, w_key[0], preferred_element_type=jnp.float32).astype(jnp.bfloat16)
    values = jnp.dot(key_in, w_value[0], preferred_element_type=jnp.float32).astype(jnp.bfloat16)
    keys = keys.reshape(batch, row_count, head_cols)
    values = values.reshape(batch, row_count, head_cols)
    query_length = lengths[0, :, 0]
    key_length = lengths[0, :, 1]
    split_queries = queries.reshape(batch, row_count, local_heads, DH)
    key_piece = lax.all_gather(keys, "seq", axis=1, tiled=True)
    value_piece = lax.all_gather(values, "seq", axis=1, tiled=True)
    key_count = key_piece.shape[1]
    scores = (
        jnp.einsum(
            "bqhd,bkhd->bqhk",
            split_queries,
            key_piece.reshape(batch, key_count, local_heads, DH),
            preferred_element_type=jnp.float32,
        )
        * 0.25
    )
    visible = jnp.arange(key_count)[None, :] < key_length[:, None]
    mask = visible[:, None, None, :]
    scores = jnp.where(mask, scores, -1e30)
    largest = jnp.max(scores, axis=-1)
    exponent = jnp.where(mask, jnp.exp(scores - largest[..., None]), 0.0)
    totals = jnp.sum(exponent, axis=-1)
    weighted = jnp.einsum(
        "bqhk,bkhd->bqhd",
        exponent.astype(jnp.bfloat16),
        value_piece.reshape(batch, key_count, local_heads, DH),
        preferred_element_type=jnp.float32,
    )
    context = weighted / totals[..., None]
    positions = lax.axis_index("seq") * row_count + jnp.arange(row_count)
    live_rows = positions[None, :] < query_length[:, None]
    context = jnp.where(live_rows[:, :, None, None], context, 0.0)
    context = context.astype(jnp.bfloat16).reshape(batch * row_count, head_cols)
    partial_value = jnp.dot(context, w_out[0], preferred_element_type=jnp.float32)
    branch = lax.psum_scatter(
        partial_value.astype(jnp.bfloat16), "mp", scatter_dimension=1, tiled=True
    ).astype(jnp.float32)
    branch = branch.reshape(batch, row_count, branch.shape[1])
    return (own_part.astype(jnp.float32) + branch).astype(jnp.bfloat16)[None]


HEAD, SIDE, INNER, ENC = 0, 1, 2, 3
BLOCK = 4


def in_hbm(array):
    return pltpu.with_memory_space_constraint(array, pltpu.HBM)


def times_gain(values, gains, side, into):
    half = values.shape[1]
    wide = values.astype(jnp.float32)
    into[...] = (wide * gains[:, pl.ds(pl.multiple_of(side * half, half), half)]).astype(jnp.bfloat16)
    return jnp.sum(wide * wide, axis=-1, keepdims=True)


def start_weights(weights, halves, held, sems, parts):
    half = held.shape[2]
    size = half // parts
    copies = [[] for _ in weights]
    for n, weight in enumerate(weights):
        for h, side in enumerate(halves):
            for m in range(parts):
                source = pl.ds(pl.multiple_of(side * half + m * size, size), size)
                copy = pltpu.make_async_copy(
                    weight.at[0, source], held.at[n, h, pl.ds(m * size, size)], sems.at[n, h, m]
                )
                copy.start()
                copies[n].append(copy)
    return copies


def begin_kernel(parts, table, hidden, memory, gain, last_gain, wk, wv, wq, ak, av, aq, sk, sq, xk, xq, held, sems):
    side = table[SIDE]
    copies = start_weights((wk, wv, wq), (side,), held, sems, parts)
    encoder = table[ENC] == 1
    total = times_gain(hidden[...], gain, side, xq)
    sq[...] = jnp.broadcast_to(total, sq.shape)

    @pl.when(encoder)
    def _():
        xk[...] = xq[...]
        sk[...] = sq[...]

    @pl.when(jnp.logical_not(encoder))
    def _():
        total = times_gain(memory[0], last_gain, side, xk)
        sk[...] = jnp.broadcast_to(total, sk.shape)

    for n, (x, out) in enumerate(((xk, ak), (xk, av), (xq, aq))):
        for copy in copies[n]:
            copy.wait()
        out[...] = jnp.dot(x[...], held[n, 0], preferred_element_type=jnp.float32)


def begin(table, hidden, memory, gains, weights, parts=4):
    rows, half = hidden.shape
    columns = weights[0].shape[2]
    whole = lambda i, table: (0, 0)
    shares, squares = ((rows, columns), (rows, LANES))
    return pl.pallas_call(
        functools.partial(begin_kernel, parts),
        out_shape=[jax.ShapeDtypeStruct(shape, jnp.float32) for shape in [shares] * 3 + [squares] * 2],
        grid_spec=pltpu.PrefetchScalarGridSpec(
            num_scalar_prefetch=1,
            grid=(1,),
            in_specs=[
                pl.BlockSpec((rows, half), whole),
                pl.BlockSpec((1, rows, half), lambda i, table: (table[INNER], 0, 0)),
            ]
            + [pl.BlockSpec((1, 2 * half), whole)] * 2
            + [pl.BlockSpec(memory_space=pltpu.HBM)] * 3,
            out_specs=[pl.BlockSpec(shape, whole) for shape in [shares] * 3 + [squares] * 2],
            scratch_shapes=[pltpu.VMEM((rows, half), jnp.bfloat16)] * 2
            + [pltpu.VMEM((3, 1, half, columns), jnp.bfloat16), pltpu.SemaphoreType.DMA((3, 1, parts))],
        ),
        compiler_params=pltpu.CompilerParams(vmem_limit_bytes=24 * MIB),
        cost_estimate=pl.CostEstimate(
            flops=6 * rows * half * columns, bytes_accessed=6 * half * columns, transcendentals=0
        ),
    )(table, hidden, memory, *gains, *[in_hbm(w) for w in weights])


def end_kernel(parts, count, table, qn, kn, gain, last_gain, wk, wv, wq, ak, av, aq, sk, sq, *rest):
    outs, (xk, xq, fk, fq, held, sems) = rest[: 2 * count], rest[2 * count :]
    side = 1 - table[SIDE]
    features = 2 * qn.shape[1]
    width = outs[count].shape[1]
    copies = start_weights((wk, wv, wq), (side,), held, sems, parts)
    encoder = table[ENC] == 1

    def factor(total):
        return lax.rsqrt(total / features + 1e-06)

    fq[...] = factor(sq[...] + times_gain(qn[...], gain, side, xq))

    @pl.when(encoder)
    def _():
        xk[...] = xq[...]
        fk[...] = fq[...]

    @pl.when(jnp.logical_not(encoder))
    def _():
        fk[...] = factor(sk[...] + times_gain(kn[...], last_gain, side, xk))

    for n, (x, share, f) in enumerate(((xk, ak, fk), (xk, av, fk), (xq, aq, fq))):
        for copy in copies[n]:
            copy.wait()
        scale = f[:, :1] * SCALE if n == 2 else f[:, :1]
        for turn in range(count):
            columns = pl.ds(pl.multiple_of((table[HEAD] ^ turn) * width, width), width)
            total = share[:, columns] + jnp.dot(x[...], held[n, 0, :, columns], preferred_element_type=jnp.float32)
            total = (total * scale).astype(jnp.bfloat16)
            if n == 2:
                outs[count + turn][...] = total
            else:
                outs[turn][:, n * width : (n + 1) * width] = total


def end(table, qn, kn, gains, weights, shares, count, parts=4):
    rows, half = qn.shape
    columns = weights[0].shape[2]
    width = columns // count
    whole = lambda i, table: (0, 0)
    widths = [2 * width] * count + [width] * count
    return pl.pallas_call(
        functools.partial(end_kernel, parts, count),
        out_shape=[jax.ShapeDtypeStruct((rows, w), jnp.bfloat16) for w in widths],
        grid_spec=pltpu.PrefetchScalarGridSpec(
            num_scalar_prefetch=1,
            grid=(1,),
            in_specs=[pl.BlockSpec((rows, half), whole)] * 2
            + [pl.BlockSpec((1, 2 * half), whole)] * 2
            + [pl.BlockSpec(memory_space=pltpu.HBM)] * 3
            + [pl.BlockSpec((rows, columns), whole)] * 3
            + [pl.BlockSpec((rows, LANES), whole)] * 2,
            out_specs=[pl.BlockSpec((rows, w), whole) for w in widths],
            scratch_shapes=[pltpu.VMEM((rows, half), jnp.bfloat16)] * 2
            + [pltpu.VMEM((rows, LANES), jnp.float32)] * 2
            + [pltpu.VMEM((3, 1, half, columns), jnp.bfloat16), pltpu.SemaphoreType.DMA((3, 1, parts))],
        ),
        compiler_params=pltpu.CompilerParams(vmem_limit_bytes=24 * MIB),
        cost_estimate=pl.CostEstimate(
            flops=6 * rows * half * columns, bytes_accessed=6 * half * columns, transcendentals=0
        ),
    )(table, qn, kn, *gains, *[in_hbm(w) for w in weights], *shares)


def project_kernel(parts, count, table, qo, qn, ko, kn, gain, last_gain, wk, wv, wq, *rest):
    outs, (xk, xq, fk, fq, held, sems) = rest[:count], rest[count:]
    side = table[SIDE]
    features = 2 * qn.shape[1]
    width = outs[0].shape[1] // 3
    copies = start_weights((wk, wv, wq), (side, 1 - side), held, sems, parts)
    encoder = table[ENC] == 1

    def fill(own, other, gains, x, f):
        total = times_gain(own[...], gains, side, x.at[0]) + times_gain(other[...], gains, 1 - side, x.at[1])
        f[...] = jnp.broadcast_to(lax.rsqrt(total / features + 1e-06), f.shape)

    fill(qo, qn, gain, xq, fq)

    @pl.when(encoder)
    def _():
        xk[...] = xq[...]
        fk[...] = fq[...]

    @pl.when(jnp.logical_not(encoder))
    def _():
        fill(ko, kn, last_gain, xk, fk)

    for n, (x, f) in enumerate(((xk, fk), (xk, fk), (xq, fq))):
        for copy in copies[n]:
            copy.wait()
        scale = f[:, :1] * SCALE if n == 2 else f[:, :1]
        for turn in range(count):
            columns = pl.ds(pl.multiple_of((table[HEAD] ^ turn) * width, width), width)
            total = jnp.dot(x[0], held[n, 0, :, columns], preferred_element_type=jnp.float32)
            total += jnp.dot(x[1], held[n, 1, :, columns], preferred_element_type=jnp.float32)
            outs[turn][:, n * width : (n + 1) * width] = (total * scale).astype(jnp.bfloat16)


def project(table, qo, qn, ko, kn, gains, weights, count, parts=4):
    rows, half = qo.shape
    columns = weights[0].shape[2]
    width = 3 * columns // count
    whole = lambda i, table: (0, 0)
    return pl.pallas_call(
        functools.partial(project_kernel, parts, count),
        out_shape=[jax.ShapeDtypeStruct((rows, width), jnp.bfloat16)] * count,
        grid_spec=pltpu.PrefetchScalarGridSpec(
            num_scalar_prefetch=1,
            grid=(1,),
            in_specs=[pl.BlockSpec((rows, half), whole)] * 4
            + [pl.BlockSpec((1, 2 * half), whole)] * 2
            + [pl.BlockSpec(memory_space=pltpu.HBM)] * 3,
            out_specs=[pl.BlockSpec((rows, width), whole)] * count,
            scratch_shapes=[pltpu.VMEM((2, rows, half), jnp.bfloat16)] * 2
            + [pltpu.VMEM((rows, LANES), jnp.float32)] * 2
            + [pltpu.VMEM((3, 2, half, columns), jnp.bfloat16), pltpu.SemaphoreType.DMA((3, 2, parts))],
        ),
        compiler_params=pltpu.CompilerParams(vmem_limit_bytes=32 * MIB),
        cost_estimate=pl.CostEstimate(
            flops=12 * rows * half * columns, bytes_accessed=12 * half * columns, transcendentals=0
        ),
    )(table, qo, qn, ko, kn, *gains, *[in_hbm(w) for w in weights])


def attend_kernel(count, chunk, tile, table, lengths, *refs):
    q_refs, k_refs, v_refs = refs[:count], refs[count : 3 * count], refs[3 * count : 5 * count]
    outs, (qs, ks, vs, contexts) = refs[5 * count : 6 * count], refs[6 * count :]
    rows, width = q_refs[0].shape
    pairs = width // LANES
    query_length = lengths[2 * table[INNER]]
    key_length = lengths[2 * table[INNER] + 1]
    lane = lax.broadcasted_iota(jnp.int32, (rows, LANES), 1)
    row = lax.broadcasted_iota(jnp.int32, (rows, LANES), 0)
    low = lane < DH
    zero = jnp.zeros((rows, LANES), jnp.bfloat16)
    one = jnp.ones((rows, LANES), jnp.bfloat16)
    unit = jnp.where(lane == 0, one, zero)
    for j in range(2 * count):
        here = pl.ds(j * rows, rows)
        hides = jnp.logical_and(lane == 0, row + table[BLOCK + j] >= key_length)
        bias = jnp.where(hides, -1e30, 0.0).astype(jnp.bfloat16)
        for pair in range(pairs):
            columns = slice(pair * LANES, (pair + 1) * LANES)
            key = k_refs[j][:, columns]
            value = v_refs[j][:, columns]
            ks[pair, 0, here, :LANES] = jnp.where(low, key, zero)
            ks[pair, 1, here, :LANES] = jnp.where(low, zero, key)
            ks[pair, 0, here, LANES:] = bias
            ks[pair, 1, here, LANES:] = bias
            vs[pair, 0, here, :] = jnp.where(low, value, one)
            vs[pair, 1, here, :] = jnp.where(low, one, value)
    for j in range(count):
        here = pl.ds(j * rows, rows)
        for pair in range(pairs):
            qs[pair, here, :LANES] = q_refs[j][:, pair * LANES : (pair + 1) * LANES]
            qs[pair, here, LANES:] = unit

    low = lax.broadcasted_iota(jnp.int32, (tile, LANES), 1) < DH
    for pair in range(pairs):
        for t in range(count * rows // tile):
            query = qs[pair, pl.ds(t * tile, tile), :]
            sums = []
            for head in range(2):
                scores = lax.dot_general(
                    query, ks[pair, head], (((1,), (1,)), ((), ())), preferred_element_type=jnp.float32
                )
                largest = jnp.max(scores, axis=-1, keepdims=True)
                weights = jnp.exp2(scores - largest).astype(jnp.bfloat16)
                sums.append(jnp.dot(weights, vs[pair, head], preferred_element_type=jnp.float32))
            weighted = jnp.where(low, sums[0], sums[1])
            totals = jnp.where(low, pltpu.roll(sums[0], DH, 1), pltpu.roll(sums[1], DH, 1))
            contexts[pl.ds(t * tile, tile), pair * LANES : (pair + 1) * LANES] = (weighted / totals).astype(
                jnp.bfloat16
            )

    for j in range(count):
        live = row + table[BLOCK + 2 * j + chunk] < query_length
        for pair in range(pairs):
            columns = slice(pair * LANES, (pair + 1) * LANES)
            outs[j][:, columns] = jnp.where(live, contexts[pl.ds(j * rows, rows), columns], zero)


def attend(table, lengths, queries, keyed, chunk, width):
    count = len(queries)
    rows = queries[0][0].shape[0]
    total = 2 * count * rows

    def column(place):
        return pl.BlockSpec((rows, width), lambda i, table, lengths: (0, place))

    return pl.pallas_call(
        functools.partial(attend_kernel, count, chunk, 2 * rows if count % 2 == 0 else rows),
        out_shape=[jax.ShapeDtypeStruct((rows, width), jnp.bfloat16)] * count,
        grid_spec=pltpu.PrefetchScalarGridSpec(
            num_scalar_prefetch=2,
            grid=(1,),
            in_specs=[column(place) for _, place in queries] + [column(0)] * (2 * count) + [column(1)] * (2 * count),
            out_specs=[column(0)] * count,
            scratch_shapes=[
                pltpu.VMEM((width // LANES, count * rows, 2 * LANES), jnp.bfloat16),
                pltpu.VMEM((width // LANES, 2, total, 2 * LANES), jnp.bfloat16),
                pltpu.VMEM((width // LANES, 2, total, LANES), jnp.bfloat16),
                pltpu.VMEM((count * rows, width), jnp.bfloat16),
            ],
        ),
        compiler_params=pltpu.CompilerParams(vmem_limit_bytes=32 * MIB),
        cost_estimate=pl.CostEstimate(
            flops=4 * count * rows * total * 2 * width,
            bytes_accessed=6 * total * width,
            transcendentals=count * rows * total * (width // DH),
        ),
    )(table, lengths, *[array for array, _ in queries], *keyed, *keyed)


def output_kernel(count, table, w, *refs):
    pieces, outs, x = refs[:count], refs[count : count + 2], refs[-1]
    step = pl.program_id(0)
    width = pieces[0].shape[1]

    @pl.when(step == 0)
    def _():
        for turn in range(count):
            place = pl.multiple_of((table[HEAD] ^ turn) * width, width)
            x[:, pl.ds(place, width)] = pieces[turn][...]

    total = jnp.dot(x[...], w[...], preferred_element_type=jnp.float32).astype(jnp.bfloat16)
    for i in range(2):

        @pl.when(step == i)
        def _(i=i):
            outs[i][...] = total


def output_parts(table, pieces, w_out):
    rows, width = pieces[0].shape
    depth, half = w_out.shape[0], w_out.shape[1] // 2
    whole = lambda i, table: (0, 0)
    return pl.pallas_call(
        functools.partial(output_kernel, len(pieces)),
        out_shape=[jax.ShapeDtypeStruct((rows, half), jnp.bfloat16)] * 2,
        grid_spec=pltpu.PrefetchScalarGridSpec(
            num_scalar_prefetch=1,
            grid=(2,),
            in_specs=[pl.BlockSpec((depth, half), lambda i, table: (0, 1 - (table[SIDE] ^ i)))]
            + [pl.BlockSpec((rows, width), whole)] * len(pieces),
            out_specs=[pl.BlockSpec((rows, half), whole)] * 2,
            scratch_shapes=[pltpu.VMEM((rows, depth), jnp.bfloat16)],
        ),
        compiler_params=pltpu.CompilerParams(vmem_limit_bytes=24 * MIB),
        cost_estimate=pl.CostEstimate(
            flops=4 * rows * depth * half,
            bytes_accessed=2 * (2 * depth * half + rows * depth + 2 * rows * half),
            transcendentals=0,
        ),
    )(table, w_out, *pieces)


def add_kernel(table, hidden, own, beside, across, corner, out):
    def total(a, b):
        out[0, 0] = (
            hidden[0, 0].astype(jnp.float32) + (a[...].astype(jnp.float32) + b[...].astype(jnp.float32))
        ).astype(jnp.bfloat16)

    @pl.when(pl.program_id(0) == 0)
    def _():
        total(own, beside)

    @pl.when(pl.program_id(0) == 1)
    def _():
        total(across, corner)


def add_all(table, hidden, own, beside, across, corner):
    rows, half = own.shape
    block = pl.BlockSpec((1, 1, rows, half), lambda i, table: (0, table[INNER] ^ i, 0, 0))
    part = pl.BlockSpec((rows, half), lambda i, table: (0, 0))
    return pl.pallas_call(
        add_kernel,
        out_shape=jax.ShapeDtypeStruct(hidden.shape, jnp.bfloat16),
        grid_spec=pltpu.PrefetchScalarGridSpec(
            num_scalar_prefetch=1,
            grid=(2,),
            in_specs=[block, part, part, part, part],
            out_specs=block,
        ),
        compiler_params=pltpu.CompilerParams(vmem_limit_bytes=16 * MIB),
    )(table, hidden, own, beside, across, corner)


def body(hidden, memory, w_query, w_key, w_value, w_out, norm_gain, final_gain, lengths):
    seq, mp = lax.axis_size("seq"), lax.axis_size("mp")
    count = seq // 2
    rows, half = hidden.shape[2:]
    width = w_query.shape[2] // count

    place, side = lax.axis_index("seq"), lax.axis_index("mp")
    outer, inner = place // 2, place % 2
    encoder = (lax.axis_index("segment") == 0).astype(jnp.int32)
    starts = [
        (2 * (outer ^ turn) + (inner ^ chunk)) * rows for turn in range(count) for chunk in range(2)
    ]
    table = jnp.stack([outer, side, inner, encoder] + starts).astype(jnp.int32)

    def moved(value, swap_seq, swap_mp):
        pairs = [
            (s * mp + m, (s ^ swap_seq) * mp + (m ^ swap_mp)) for s in range(seq) for m in range(mp)
        ]
        return lax.ppermute(value, ("seq", "mp"), pairs)

    def handed(value, swap_seq, swap_mp):
        pairs = [
            (s * mp + m, seq * mp + (s ^ swap_seq) * mp + (m ^ swap_mp)) for s in range(seq) for m in range(mp)
        ]
        return lax.ppermute(value, ("segment", "seq", "mp"), pairs)

    def turned(value, turn):
        return lax.ppermute(value, "seq", [(s, s ^ (2 * turn)) for s in range(seq)]) if turn else value

    def chosen(array, index):
        return lax.dynamic_index_in_dim(array, index, 0, keepdims=False)

    source_here = handed(memory[0], 0, 0)
    hidden_own = chosen(hidden[0], inner)
    query_beside = moved(hidden_own, 0, 1)
    memory_own = chosen(memory[0], inner)
    source_beside = handed(memory_own, 0, 1)
    hidden_later, memory_later, _, _ = lax.optimization_barrier((hidden[0], memory[0], hidden_own, memory_own))
    hidden_away = chosen(hidden_later, 1 - inner)
    query_across = moved(hidden_away, 1, 0)
    memory_away = chosen(memory_later, 1 - inner)
    source_across = handed(memory_away, 1, 0)

    gains = (in_hbm(norm_gain), in_hbm(final_gain.reshape(1, -1)))
    weights = (w_key, w_value, w_query)
    shares = begin(table, hidden_own, source_here, gains, weights)
    hidden_away, memory_away, shares = lax.optimization_barrier((hidden_away, memory_away, shares))
    query_corner = moved(hidden_away, 1, 1)
    source_corner = handed(memory_away, 1, 1)

    turns = range(count - 1, -1, -1)
    products = end(table, query_beside, source_beside, gains, weights, shares, count)
    first = {t: turned(products[t], t) for t in turns}
    second = project(table, query_across, query_corner, source_across, source_corner, gains, weights, count)
    first_queries, second = lax.optimization_barrier((products[count:], second))
    second = {t: turned(second[t], t) for t in turns}
    first_queries = {t: turned(first_queries[t], t) for t in turns}
    keyed = [part[t] for t in range(count) for part in (first, second)]

    lengths = lengths.reshape(-1)
    context = attend(table, lengths, [(second[t], 2) for t in range(count)], keyed, 1, width)
    context = [turned(context[t], t) for t in range(count)]
    corner, across = output_parts(table, context, w_out[0])
    corner = moved(corner, 1, 1)
    across = moved(across, 1, 0)

    context = attend(table, lengths, [(first_queries[t], 0) for t in range(count)], keyed, 0, width)
    context = [turned(context[t], t) for t in range(count)]
    beside, own = output_parts(table, context, w_out[0])
    beside = moved(beside, 0, 1)
    return add_all(table, hidden, own, beside, across, corner)


def solution(mesh):
    seq, mp = mesh.shape["seq"], mesh.shape["mp"]

    def chosen(*arrays):
        batch, columns = arrays[0].shape[1], arrays[2].shape[2]
        count = seq // 2
        fits = (
            batch == 2
            and mp == 2
            and seq % 2 == 0
            and count & (count - 1) == 0
            and (columns // mp) % (count * LANES) == 0
            and (arrays[0].shape[2] // seq) % 16 == 0
        )
        return jax.shard_map(
            body if fits else gathered_body,
            mesh=mesh,
            in_specs=(
                P("segment", None, "seq", "mp"),
                P("segment", None, "seq", "mp"),
                P("segment", None, "mp"),
                P("segment", None, "mp"),
                P("segment", None, "mp"),
                P("segment", "mp", None),
                P("segment", None),
                P(),
                P("segment", None, None),
            ),
            out_specs=P("segment", None, "seq", "mp"),
            check_vma=False,
        )(*arrays)

    return chosen
```

time: 136 us -> 115 us (0.85)
  waiting for transfers between devices: 51.4 us -> 34.9 us
  starting transfers between devices: 35.3 us -> 41.2 us
  local copies, waits for them, and re-layouts: 10.9 us -> 5.62 us
  Pallas kernels: 36.1 us -> 33 us
    ppermute x12 -> x15, waiting for transfers between devices: 32 us -> 21.8 us  [turned(): lax.ppermute(value, 'seq', [(s, s ^ 2 * turn) for s in range(seq)])]
    ppermute x12 -> x15, starting transfers between devices: 16.5 us -> 26.5 us  [turned(): lax.ppermute(value, 'seq', [(s, s ^ 2 * turn) for s in range(seq)])]
    unnamed x15 -> x6, local copies, waits for them, and re-layouts: 7.06 us -> 0.02 us
    ppermute x4, starting transfers between devices: 11.6 us -> 6.63 us  [handed(): return lax.ppermute(value, ('segment', 'seq', 'mp'), pairs)]
    ppermute x6, waiting for transfers between devices: 16.3 us -> 12.7 us  [moved(): return lax.ppermute(value, ('seq', 'mp'), pairs)]
    pallas_call x6 -> x7, Pallas kernels: 34.6 us -> 31.5 us  [the longest x2 10.8 us: attend(): pl.pallas_call(functools.partial(attend_kernel, count, chunk, 2 * rows if...]
    ppermute x4, waiting for transfers between devices: 3.22 us -> 0.43 us  [handed(): return lax.ppermute(value, ('segment', 'seq', 'mp'), pairs)]
    squeeze x2 -> x4, local copies, waits for them, and re-layouts: 2.96 us -> 5.44 us  [chosen(): return lax.dynamic_index_in_dim(array, index, 0, keepdims=False)]
  transfers between devices with their start and end apart: 22 -> 25, of which waited for: 13 -> 8; matrix products, arithmetic and copies ran while one was open for 3% -> 5% of each run, Pallas kernels for 17% -> 23%
where the time goes in v2:
time: 115 us
  starting transfers between devices  41.2 us (36%)
  waiting for transfers between devices  34.9 us (30%)
  Pallas kernels  33 us (29%)
  local copies, waits for them, and re-layouts  5.62 us (5%)
    ppermute x15, starting transfers between devices, turned(): lax.ppermute(value, 'seq', [(s, s ^ 2 * turn) for s in range(seq)])  26.5 us
    ppermute x15, waiting for transfers between devices, turned(): lax.ppermute(value, 'seq', [(s, s ^ 2 * turn) for s in range(seq)])  21.8 us
    ppermute x6, waiting for transfers between devices, moved(): return lax.ppermute(value, ('seq', 'mp'), pairs)  12.7 us
    pallas_call x2, Pallas kernels, attend(): pl.pallas_call(functools.partial(attend_kernel, count, chunk, 2 * rows if...  10.8 us
    ppermute x6, starting transfers between devices, moved(): return lax.ppermute(value, ('seq', 'mp'), pairs)  8.09 us
    pallas_call x1, Pallas kernels, project(): pl.pallas_call(functools.partial(project_kernel, parts, count), out_shape...  7.12 us
    ppermute x4, starting transfers between devices, handed(): return lax.ppermute(value, ('segment', 'seq', 'mp'), pairs)  6.63 us
    squeeze x4, local copies, waits for them, and re-layouts, chosen(): return lax.dynamic_index_in_dim(array, index, 0, keepdims=False)  5.44 us
  transfers between devices with their start and end apart: 25, of which 8 were waited for; matrix products, arithmetic and copies ran while one was open for 5% of the time, Pallas kernels for 23%

profile of v2, /device:TPU:0, one launch (start us, length us, event | category | flops | bytes accessed | tf_op | source)
XLA Modules:
  0.0 115.0 jit_solution(13639269457088054450)
XLA Ops:
  0.0 2.4 %collective-permute-start.2 = (bf16[2,160,1024]{2,1,0:T(8,128)(2,1)}, bf16[2,160,1024]{2,1,0:T(8,128)(2,1)S(1)}, u32[]{:S(2)}, u32[]{:S(2)}) collective-permute-start(bf16[2,160,1024]{2,1,0:T(8,128)(2,1)} %bitcast.27), channel_id=1, source_target_pairs={{0,16},{1,17},{2,18},{3,19},{4,20},{5,21},{6,22},{7,23},{8,24},{9,... | collective-permute-start | bytes 1966088 | tf_op jit(solution)/shard_map/ppermute | solution.py:486
  2.4 1.0 dynamic-slice_bitcast_fusion.3.hidden
  3.4 2.4 %collective-permute-start = (bf16[160,1024]{1,0:T(8,128)(2,1)S(1)}, bf16[160,1024]{1,0:T(8,128)(2,1)S(1)}, u32[]{:S(2)}, u32[]{:S(2)}) collective-permute-start(bf16[160,1024]{1,0:T(8,128)(2,1)S(1)} %dynamic-slice_bitcast_fusion.3.hidden), channel_id=1, source_target_pairs={{0,1},{1,0},{2,3},{3,2},{4,5},{5,4},{6,7},{7,6},{8,9},{9,8},{10,11... | collective-permute-start | bytes 983048 | tf_op jit(solution)/shard_map/ppermute | solution.py:480
  5.8 1.0 dynamic-slice_bitcast_fusion.2
  6.8 1.3 %collective-permute-start.1 = (bf16[160,1024]{1,0:T(8,128)(2,1)S(1)}, bf16[160,1024]{1,0:T(8,128)(2,1)S(1)}, u32[]{:S(2)}, u32[]{:S(2)}) collective-permute-start(bf16[160,1024]{1,0:T(8,128)(2,1)S(1)} %dynamic-slice_bitcast_fusion.2), channel_id=1, source_target_pairs={{0,17},{1,16},{2,19},{3,18},{4,21},{5,20},{6,23},{7,22},{8,25},{9,... | collective-permute-start | bytes 983048 | tf_op jit(solution)/shard_map/ppermute | solution.py:486
  8.2 1.7 %dynamic-slice_bitcast_fusion.1 = bf16[160,1024]{1,0:T(8,128)(2,1)} fusion(bf16[2,160,1024]{2,1,0:T(8,128)(2,1)} %bitcast.26, s32[]{:T(128)S(6)} %select_n.23), kind=kLoop, calls=%fused_computation.1 | loop fusion | bytes 655364 | tf_op jit(solution)/shard_map/jit(dynamic_index_in_dim)/squeeze | solution.py:492
  9.9 1.5 %collective-permute-start.3 = (bf16[160,1024]{1,0:T(8,128)(2,1)}, bf16[160,1024]{1,0:T(8,128)(2,1)S(1)}, u32[]{:S(2)}, u32[]{:S(2)}) collective-permute-start(bf16[160,1024]{1,0:T(8,128)(2,1)} %dynamic-slice_bitcast_fusion.1), channel_id=1, source_target_pairs={{0,2},{1,3},{2,0},{3,1},{4,6},{5,7},{6,4},{7,5},{8,10},{9,11},{10,... | collective-permute-start | bytes 983048 | tf_op jit(solution)/shard_map/ppermute | solution.py:480
  11.4 1.7 %dynamic-slice_bitcast_fusion = bf16[160,1024]{1,0:T(8,128)(2,1)} fusion(bf16[2,160,1024]{2,1,0:T(8,128)(2,1)} %bitcast.28, s32[]{:T(128)S(6)} %select_n.23), kind=kLoop, calls=%fused_computation | loop fusion | bytes 655364 | tf_op jit(solution)/shard_map/jit(dynamic_index_in_dim)/squeeze | solution.py:492
  13.1 1.3 %collective-permute-start.5 = (bf16[160,1024]{1,0:T(8,128)(2,1)}, bf16[160,1024]{1,0:T(8,128)(2,1)S(1)}, u32[]{:S(2)}, u32[]{:S(2)}) collective-permute-start(bf16[160,1024]{1,0:T(8,128)(2,1)} %dynamic-slice_bitcast_fusion), channel_id=1, source_target_pairs={{0,18},{1,19},{2,16},{3,17},{4,22},{5,23},{6,20},{7,21},{8,26},{9,... | collective-permute-start | bytes 983048 | tf_op jit(solution)/shard_map/ppermute | solution.py:486
  14.4 0.1 stack.55.table
  14.5 0.0 collective-permute-done.2.memory
  14.5 4.7 %shard_map.91 = (f32[160,1024]{1,0:T(8,128)S(1)}, f32[160,1024]{1,0:T(8,128)S(1)}, f32[160,1024]{1,0:T(8,128)S(1)}, f32[160,128]{1,0:T(8,128)S(1)}, f32[160,128]{1,0:T(8,128)S(1)}) custom-call(s32[12]{0:T(128)S(1)} %stack.55.table, bf16[160,1024]{1,0:T(8,128)(2,1)S(1)} %dynamic-slice_bitcast_fusion.3.hidden, ...), custom_call_target="tpu_custom_call" | custom-call | flops 1006632960 | bytes 6291456 | tf_op jit(solution)/shard_map/pallas_call | solution.py:149
  19.2 1.3 %collective-permute-start.4 = (bf16[160,1024]{1,0:T(8,128)(2,1)}, bf16[160,1024]{1,0:T(8,128)(2,1)S(1)}, u32[]{:S(2)}, u32[]{:S(2)}) collective-permute-start(bf16[160,1024]{1,0:T(8,128)(2,1)} %dynamic-slice_bitcast_fusion.1), channel_id=1, source_target_pairs={{0,3},{1,2},{2,1},{3,0},{4,7},{5,6},{6,5},{7,4},{8,11},{9,10},{10,... | collective-permute-start | bytes 983048 | tf_op jit(solution)/shard_map/ppermute | solution.py:480
  20.6 0.0 collective-permute-done.qn
  20.6 1.6 %collective-permute-start.6 = (bf16[160,1024]{1,0:T(8,128)(2,1)}, bf16[160,1024]{1,0:T(8,128)(2,1)S(1)}, u32[]{:S(2)}, u32[]{:S(2)}) collective-permute-start(bf16[160,1024]{1,0:T(8,128)(2,1)} %dynamic-slice_bitcast_fusion), channel_id=1, source_target_pairs={{0,19},{1,18},{2,17},{3,16},{4,23},{5,22},{6,21},{7,20},{8,27},{9,... | collective-permute-start | bytes 983048 | tf_op jit(solution)/shard_map/ppermute | solution.py:486
  22.2 0.0 collective-permute-done.1.kn
  22.2 4.8 %shard_map.92 = (bf16[160,512]{1,0:T(8,128)(2,1)S(1)}, bf16[160,512]{1,0:T(8,128)(2,1)S(1)}, bf16[160,512]{1,0:T(8,128)(2,1)S(1)}, bf16[160,512]{1,0:T(8,128)(2,...) custom-call(s32[12]{0:T(128)S(1)} %stack.55.table, ...), custom_call_target="tpu_custom_call" | custom-call | flops 1006632960 | bytes 6291456 | tf_op jit(solution)/shard_map/pallas_call | solution.py:214
  27.0 1.6 %collective-permute-start.10 = (bf16[160,512]{1,0:T(8,128)(2,1)S(1)}, bf16[160,512]{1,0:T(8,128)(2,1)S(1)}, u32[]{:S(2)}, u32[]{:S(2)}) collective-permute-start(bf16[160,512]{1,0:T(8,128)(2,1)S(1)} %get-tuple-element.79), channel_id=1, source_target_pairs={{0,4},{2,6},{4,0},{6,2},{8,12},{10,14},{12,8},{14,10},{1,5},{3,7},... | collective-permute-start | bytes 491528 | tf_op jit(solution)/shard_map/ppermute | solution.py:489
  28.6 0.0 collective-permute-done.3.qo
  28.6 2.6 %collective-permute-start.12 = (bf16[160,512]{1,0:T(8,128)(2,1)S(1)}, bf16[160,512]{1,0:T(8,128)(2,1)S(1)}, u32[]{:S(2)}, u32[]{:S(2)}) collective-permute-start(bf16[160,512]{1,0:T(8,128)(2,1)S(1)} %get-tuple-element.81), channel_id=1, source_target_pairs={{0,8},{2,10},{4,12},{6,14},{8,0},{10,2},{12,4},{14,6},{1,9},{3,11}... | collective-permute-start | bytes 491528 | tf_op jit(solution)/shard_map/ppermute | solution.py:489
  31.2 0.0 collective-permute-done.5.ko
  31.2 0.2 collective-permute-start.14
  31.5 0.0 collective-permute-done.4.qn
  31.5 0.4 collective-permute-done.6.kn
  31.9 7.1 %shard_map.93 = (bf16[160,768]{1,0:T(8,128)(2,1)S(1)}, bf16[160,768]{1,0:T(8,128)(2,1)S(1)}, bf16[160,768]{1,0:T(8,128)(2,1)S(1)}, bf16[160,768]{1,0:T(8,128)(2,1)S(1)}) custom-call(s32[12]{0:T(128)S(1)} %stack.55.table, bf16[160,1024]{1,0:T(8,128)(2,1)S(1)} %collective-permute-done.3.qo, bf16[160,1024]{1,0:T(8,128)(2,1)S(1)} %collective-permute-done.4.qn, ...), custom_call_target="tpu_custom_call" | custom-call | flops 2013265920 | bytes 12582912 | tf_op jit(solution)/shard_map/pallas_call | solution.py:276
  39.0 1.6 %collective-permute-start.11 = (bf16[160,768]{1,0:T(8,128)(2,1)S(1)}, bf16[160,768]{1,0:T(8,128)(2,1)S(1)}, u32[]{:S(2)}, u32[]{:S(2)}) collective-permute-start(bf16[160,768]{1,0:T(8,128)(2,1)S(1)} %get-tuple-element.80), channel_id=1, source_target_pairs={{0,4},{2,6},{4,0},{6,2},{8,12},{10,14},{12,8},{14,10},{1,5},{3,7},... | collective-permute-start | bytes 737288 | tf_op jit(solution)/shard_map/ppermute | solution.py:489
  40.7 2.6 %collective-permute-start.13 = (bf16[160,768]{1,0:T(8,128)(2,1)S(1)}, bf16[160,768]{1,0:T(8,128)(2,1)S(1)}, u32[]{:S(2)}, u32[]{:S(2)}) collective-permute-start(bf16[160,768]{1,0:T(8,128)(2,1)S(1)} %get-tuple-element.82), channel_id=1, source_target_pairs={{0,8},{2,10},{4,12},{6,14},{8,0},{10,2},{12,4},{14,6},{1,9},{3,11}... | collective-permute-start | bytes 737288 | tf_op jit(solution)/shard_map/ppermute | solution.py:489
  43.2 0.0 collective-permute-done.10.refs_6_.refs_14_
  43.2 0.2 collective-permute-start.15
  43.5 0.0 collective-permute-done.12.refs_8_.refs_16_
  43.5 0.7 collective-permute-start.7
  44.2 0.0 collective-permute-done.14.refs_10_.refs_18_
  44.2 3.5 %collective-permute-start.8 = (bf16[160,256]{1,0:T(8,128)(2,1)S(1)}, bf16[160,256]{1,0:T(8,128)(2,1)S(1)}, u32[]{:S(2)}, u32[]{:S(2)}) collective-permute-start(bf16[160,256]{1,0:T(8,128)(2,1)S(1)} %get-tuple-element.75), channel_id=1, source_target_pairs={{0,8},{2,10},{4,12},{6,14},{8,0},{10,2},{12,4},{14,6},{1,9},{3,11}... | collective-permute-start | bytes 245768 | tf_op jit(solution)/shard_map/ppermute | solution.py:489
  47.7 11.7 %collective-permute-done.7.refs_1_ = bf16[160,256]{1,0:T(8,128)(2,1)S(1)} collective-permute-done((bf16[160,256]{1,0:T(8,128)(2,1)S(1)}, bf16[160,256]{1,0:T(8,128)(2,1)S(1)}, u32[]{:S(2)}, u32[]{:S(2)}) %collective-permute-start.7) | collective-permute-done | bytes 81952 | tf_op jit(solution)/shard_map/ppermute | solution.py:489
  59.4 4.4 %collective-permute-start.9 = (bf16[160,256]{1,0:T(8,128)(2,1)S(1)}, bf16[160,256]{1,0:T(8,128)(2,1)S(1)}, u32[]{:S(2)}, u32[]{:S(2)}) collective-permute-start(bf16[160,256]{1,0:T(8,128)(2,1)S(1)} %get-tuple-element.76), channel_id=1, source_target_pairs={{0,12},{2,14},{4,8},{6,10},{8,4},{10,6},{12,0},{14,2},{1,13},{3,15... | collective-permute-start | bytes 245768 | tf_op jit(solution)/shard_map/ppermute | solution.py:489
  63.8 0.1 reshape.10.lengths
  63.9 7.6 %collective-permute-done.8.refs_2_ = bf16[160,256]{1,0:T(8,128)(2,1)S(1)} collective-permute-done((bf16[160,256]{1,0:T(8,128)(2,1)S(1)}, bf16[160,256]{1,0:T(8,128)(2,1)S(1)}, u32[]{:S(2)}, u32[]{:S(2)}) %collective-permute-start.8) | collective-permute-done | bytes 81952 | tf_op jit(solution)/shard_map/ppermute | solution.py:489
  71.4 0.0 collective-permute-done.9.refs_3_
  71.4 0.0 collective-permute-done.11.refs_7_.refs_15_.refs_1_
  71.4 0.0 collective-permute-done.15.refs_11_.refs_19_.refs_3_
  71.4 5.4 %shard_map.94 = (bf16[160,256]{1,0:T(8,128)(2,1)S(1)}, bf16[160,256]{1,0:T(8,128)(2,1)S(1)}, bf16[160,256]{1,0:T(8,128)(2,1)S(1)}, bf16[160,256]{1,0:T(8,128)(2,1)S(1)}) custom-call(s32[12]{0:T(128)S(1)} %stack.55.table, s32[4]{0:T(128)S(1)} %reshape.10.lengths, bf16[160,256]{1,0:T(8,128)(2,1)S(1)} %get-tuple-element.73.refs_0_, ...), custom_call_target="tpu_custom_call" | custom-call | flops 1677721600 | bytes 1966080 | tf_op jit(solution)/shard_map/pallas_call | solution.py:363
  76.9 0.0 copy-start
  76.9 2.1 %collective-permute-start.16 = (bf16[160,256]{1,0:T(8,128)(2,1)S(1)}, bf16[160,256]{1,0:T(8,128)(2,1)S(1)}, u32[]{:S(2)}, u32[]{:S(2)}) collective-permute-start(bf16[160,256]{1,0:T(8,128)(2,1)S(1)} %get-tuple-element.86), channel_id=1, source_target_pairs={{0,4},{2,6},{4,0},{6,2},{8,12},{10,14},{12,8},{14,10},{1,5},{3,7},... | collective-permute-start | bytes 245768 | tf_op jit(solution)/shard_map/ppermute | solution.py:489
  79.0 1.1 collective-permute-start.17
  80.1 1.4 %collective-permute-start.18 = (bf16[160,256]{1,0:T(8,128)(2,1)S(1)}, bf16[160,256]{1,0:T(8,128)(2,1)S(1)}, u32[]{:S(2)}, u32[]{:S(2)}) collective-permute-start(bf16[160,256]{1,0:T(8,128)(2,1)S(1)} %get-tuple-element.88), channel_id=1, source_target_pairs={{0,12},{2,14},{4,8},{6,10},{8,4},{10,6},{12,0},{14,2},{1,13},{3,15... | collective-permute-start | bytes 245768 | tf_op jit(solution)/shard_map/ppermute | solution.py:489
  81.5 5.4 %shard_map.96 = (bf16[160,256]{1,0:T(8,128)(2,1)S(1)}, bf16[160,256]{1,0:T(8,128)(2,1)S(1)}, bf16[160,256]{1,0:T(8,128)(2,1)S(1)}, bf16[160,256]{1,0:T(8,128)(2,1)S(1)}) custom-call(s32[12]{0:T(128)S(1)} %stack.55.table, s32[4]{0:T(128)S(1)} %reshape.10.lengths, bf16[160,768]{1,0:T(8,128)(2,1)S(1)} %get-tuple-element.78.refs_5_.refs_13_.refs_0_, ...), custom_call_target="tpu_custom_call" | custom-call | flops 1677721600 | bytes 1966080 | tf_op jit(solution)/shard_map/pallas_call | solution.py:363
  86.9 1.1 collective-permute-start.20
  88.0 2.0 %collective-permute-start.21 = (bf16[160,256]{1,0:T(8,128)(2,1)S(1)}, bf16[160,256]{1,0:T(8,128)(2,1)S(1)}, u32[]{:S(2)}, u32[]{:S(2)}) collective-permute-start(bf16[160,256]{1,0:T(8,128)(2,1)S(1)} %get-tuple-element.93), channel_id=1, source_target_pairs={{0,8},{2,10},{4,12},{6,14},{8,0},{10,2},{12,4},{14,6},{1,9},{3,11}... | collective-permute-start | bytes 245768 | tf_op jit(solution)/shard_map/ppermute | solution.py:489
  90.0 0.0 collective-permute-done.16.refs_1_
  90.0 1.4 %collective-permute-start.22 = (bf16[160,256]{1,0:T(8,128)(2,1)S(1)}, bf16[160,256]{1,0:T(8,128)(2,1)S(1)}, u32[]{:S(2)}, u32[]{:S(2)}) collective-permute-start(bf16[160,256]{1,0:T(8,128)(2,1)S(1)} %get-tuple-element.94), channel_id=1, source_target_pairs={{0,12},{2,14},{4,8},{6,10},{8,4},{10,6},{12,0},{14,2},{1,13},{3,15... | collective-permute-start | bytes 245768 | tf_op jit(solution)/shard_map/ppermute | solution.py:489
  91.3 0.0 collective-permute-done.17.refs_2_
  91.4 0.0 collective-permute-done.18.refs_3_
  91.4 0.0 copy-start.1
  91.4 2.0 %shard_map.95 = (bf16[160,1024]{1,0:T(8,128)(2,1)S(1)}, bf16[160,1024]{1,0:T(8,128)(2,1)S(1)}) custom-call(s32[12]{0:T(128)S(1)} %stack.55.table, bf16[1024,2048]{1,0:T(8,128)(2,1)S(1)} %bitcast.24, bf16[160,256]{1,0:T(8,128)(2,1)S(1)} %get-tuple-element.85.refs_0_, bf16[160,256]{1,0:T(8,128)(2,1)S(1)} %collective-permute-done.16.refs_1_, ...), custom_call_target="tpu_custom_call" | custom-call | flops 671088640 | bytes 5177344 | tf_op jit(solution)/shard_map/pallas_call | solution.py:410
  93.4 0.4 collective-permute-start.19
  93.8 1.6 %collective-permute-done.21.refs_2_ = bf16[160,256]{1,0:T(8,128)(2,1)S(1)} collective-permute-done((bf16[160,256]{1,0:T(8,128)(2,1)S(1)}, bf16[160,256]{1,0:T(8,128)(2,1)S(1)}, u32[]{:S(2)}, u32[]{:S(2)}) %collective-permute-start.21) | collective-permute-done | bytes 81952 | tf_op jit(solution)/shard_map/ppermute | solution.py:489
  95.4 0.9 collective-permute-done.22.refs_3_
  96.3 2.0 %shard_map.97 = (bf16[160,1024]{1,0:T(8,128)(2,1)S(1)}, bf16[160,1024]{1,0:T(8,128)(2,1)S(1)}) custom-call(s32[12]{0:T(128)S(1)} %stack.55.table, bf16[1024,2048]{1,0:T(8,128)(2,1)S(1)} %bitcast.25, bf16[160,256]{1,0:T(8,128)(2,1)S(1)} %get-tuple-element.91.refs_0_, bf16[160,256]{1,0:T(8,128)(2,1)S(1)} %collective-permute-done.20.refs_1_, ...), custom_call_target="tpu_custom_call" | custom-call | flops 671088640 | bytes 5177344 | tf_op jit(solution)/shard_map/pallas_call | solution.py:410
  98.3 1.0 collective-permute-start.23
  99.3 1.4 %collective-permute-start.24 = (bf16[160,1024]{1,0:T(8,128)(2,1)S(1)}, bf16[160,1024]{1,0:T(8,128)(2,1)S(1)}, u32[]{:S(2)}, u32[]{:S(2)}) collective-permute-start(bf16[160,1024]{1,0:T(8,128)(2,1)S(1)} %get-tuple-element.96), channel_id=1, source_target_pairs={{0,3},{1,2},{2,1},{3,0},{4,7},{5,6},{6,5},{7,4},{8,11},{9,10},{10,... | collective-permute-start | bytes 983048 | tf_op jit(solution)/shard_map/ppermute | solution.py:480
  100.7 0.7 collective-permute-done.19.beside
  101.5 7.6 %collective-permute-done.23.across = bf16[160,1024]{1,0:T(8,128)(2,1)S(1)} collective-permute-done((bf16[160,1024]{1,0:T(8,128)(2,1)S(1)}, bf16[160,1024]{1,0:T(8,128)(2,1)S(1)}, u32[]{:S(2)}, u32[]{:S(2)}) %collective-permute-start.23) | collective-permute-done | bytes 327712 | tf_op jit(solution)/shard_map/ppermute | solution.py:480
  109.0 4.4 %collective-permute-done.24.corner = bf16[160,1024]{1,0:T(8,128)(2,1)S(1)} collective-permute-done((bf16[160,1024]{1,0:T(8,128)(2,1)S(1)}, bf16[160,1024]{1,0:T(8,128)(2,1)S(1)}, u32[]{:S(2)}, u32[]{:S(2)}) %collective-permute-start.24) | collective-permute-done | bytes 327712 | tf_op jit(solution)/shard_map/ppermute | solution.py:480
  113.4 1.6 %shard_map.98 = bf16[1,2,160,1024]{3,2,1,0:T(8,128)(2,1)} custom-call(s32[12]{0:T(128)S(1)} %stack.55.table, bf16[1,2,160,1024]{3,2,1,0:T(8,128)(2,1)S(1)} %copy-done.1, bf16[160,1024]{1,0:T(8,128)(2,1)S(1)} %get-tuple-element.89.own, bf16[160,1024]{1,0:T(8,128)(2,1)S(1)} %collective-permute-done.19.beside, ...), custom_call_target="tpu_custom_call" | custom-call | tf_op jit(solution)/shard_map/pallas_call | solution.py:449
  (6 shorter events, 0.0 us)
Async XLA Ops:
  0.0 14.5 %collective-permute-start.2 = (bf16[2,160,1024]{2,1,0:T(8,128)(2,1)}, bf16[2,160,1024]{2,1,0:T(8,128)(2,1)S(1)}, u32[]{:S(2)}, u32[]{:S(2)}) collective-permute-start(bf16[2,160,1024]{2,1,0:T(8,128)(2,1)} %bitcast.27), channel_id=1, source_target_pairs={{0,16},{1,17},{2,18},{3,19},{4,20},{5,21},{6,22},{7,23},{8,24},{9,... | collective-permute-start | bytes 1966088 | tf_op jit(solution)/shard_map/ppermute | solution.py:486
  3.4 17.2 %collective-permute-start = (bf16[160,1024]{1,0:T(8,128)(2,1)S(1)}, bf16[160,1024]{1,0:T(8,128)(2,1)S(1)}, u32[]{:S(2)}, u32[]{:S(2)}) collective-permute-start(bf16[160,1024]{1,0:T(8,128)(2,1)S(1)} %dynamic-slice_bitcast_fusion.3.hidden), channel_id=1, source_target_pairs={{0,1},{1,0},{2,3},{3,2},{4,5},{5,4},{6,7},{7,6},{8,9},{9,8},{10,11... | collective-permute-start | bytes 983048 | tf_op jit(solution)/shard_map/ppermute | solution.py:480
  6.8 15.4 %collective-permute-start.1 = (bf16[160,1024]{1,0:T(8,128)(2,1)S(1)}, bf16[160,1024]{1,0:T(8,128)(2,1)S(1)}, u32[]{:S(2)}, u32[]{:S(2)}) collective-permute-start(bf16[160,1024]{1,0:T(8,128)(2,1)S(1)} %dynamic-slice_bitcast_fusion.2), channel_id=1, source_target_pairs={{0,17},{1,16},{2,19},{3,18},{4,21},{5,20},{6,23},{7,22},{8,25},{9,... | collective-permute-start | bytes 983048 | tf_op jit(solution)/shard_map/ppermute | solution.py:486
  9.9 18.8 %collective-permute-start.3 = (bf16[160,1024]{1,0:T(8,128)(2,1)}, bf16[160,1024]{1,0:T(8,128)(2,1)S(1)}, u32[]{:S(2)}, u32[]{:S(2)}) collective-permute-start(bf16[160,1024]{1,0:T(8,128)(2,1)} %dynamic-slice_bitcast_fusion.1), channel_id=1, source_target_pairs={{0,2},{1,3},{2,0},{3,1},{4,6},{5,7},{6,4},{7,5},{8,10},{9,11},{10,... | collective-permute-start | bytes 983048 | tf_op jit(solution)/shard_map/ppermute | solution.py:480
  13.1 18.1 %collective-permute-start.5 = (bf16[160,1024]{1,0:T(8,128)(2,1)}, bf16[160,1024]{1,0:T(8,128)(2,1)S(1)}, u32[]{:S(2)}, u32[]{:S(2)}) collective-permute-start(bf16[160,1024]{1,0:T(8,128)(2,1)} %dynamic-slice_bitcast_fusion), channel_id=1, source_target_pairs={{0,18},{1,19},{2,16},{3,17},{4,22},{5,23},{6,20},{7,21},{8,26},{9,... | collective-permute-start | bytes 983048 | tf_op jit(solution)/shard_map/ppermute | solution.py:486
  19.2 12.3 %collective-permute-start.4 = (bf16[160,1024]{1,0:T(8,128)(2,1)}, bf16[160,1024]{1,0:T(8,128)(2,1)S(1)}, u32[]{:S(2)}, u32[]{:S(2)}) collective-permute-start(bf16[160,1024]{1,0:T(8,128)(2,1)} %dynamic-slice_bitcast_fusion.1), channel_id=1, source_target_pairs={{0,3},{1,2},{2,1},{3,0},{4,7},{5,6},{6,5},{7,4},{8,11},{9,10},{10,... | collective-permute-start | bytes 983048 | tf_op jit(solution)/shard_map/ppermute | solution.py:480
  20.6 11.3 %collective-permute-start.6 = (bf16[160,1024]{1,0:T(8,128)(2,1)}, bf16[160,1024]{1,0:T(8,128)(2,1)S(1)}, u32[]{:S(2)}, u32[]{:S(2)}) collective-permute-start(bf16[160,1024]{1,0:T(8,128)(2,1)} %dynamic-slice_bitcast_fusion), channel_id=1, source_target_pairs={{0,19},{1,18},{2,17},{3,16},{4,23},{5,22},{6,21},{7,20},{8,27},{9,... | collective-permute-start | bytes 983048 | tf_op jit(solution)/shard_map/ppermute | solution.py:486
  27.0 16.2 %collective-permute-start.10 = (bf16[160,512]{1,0:T(8,128)(2,1)S(1)}, bf16[160,512]{1,0:T(8,128)(2,1)S(1)}, u32[]{:S(2)}, u32[]{:S(2)}) collective-permute-start(bf16[160,512]{1,0:T(8,128)(2,1)S(1)} %get-tuple-element.79), channel_id=1, source_target_pairs={{0,4},{2,6},{4,0},{6,2},{8,12},{10,14},{12,8},{14,10},{1,5},{3,7},... | collective-permute-start | bytes 491528 | tf_op jit(solution)/shard_map/ppermute | solution.py:489
  28.6 14.8 %collective-permute-start.12 = (bf16[160,512]{1,0:T(8,128)(2,1)S(1)}, bf16[160,512]{1,0:T(8,128)(2,1)S(1)}, u32[]{:S(2)}, u32[]{:S(2)}) collective-permute-start(bf16[160,512]{1,0:T(8,128)(2,1)S(1)} %get-tuple-element.81), channel_id=1, source_target_pairs={{0,8},{2,10},{4,12},{6,14},{8,0},{10,2},{12,4},{14,6},{1,9},{3,11}... | collective-permute-start | bytes 491528 | tf_op jit(solution)/shard_map/ppermute | solution.py:489
  31.2 32.5 %copy-start.2 = (s32[1,2,2]{2,1,0:T(2,128)S(1)}, s32[1,2,2]{2,1,0:T(2,128)}, u32[]{:S(2)}) copy-start(s32[1,2,2]{2,1,0:T(2,128)} %param.17) | copy-start | bytes 52
  31.2 12.9 %collective-permute-start.14 = (bf16[160,512]{1,0:T(8,128)(2,1)S(1)}, bf16[160,512]{1,0:T(8,128)(2,1)S(1)}, u32[]{:S(2)}, u32[]{:S(2)}) collective-permute-start(bf16[160,512]{1,0:T(8,128)(2,1)S(1)} %get-tuple-element.83), channel_id=1, source_target_pairs={{0,12},{2,14},{4,8},{6,10},{8,4},{10,6},{12,0},{14,2},{1,13},{3,15... | collective-permute-start | bytes 491528 | tf_op jit(solution)/shard_map/ppermute | solution.py:489
  39.0 32.4 %collective-permute-start.11 = (bf16[160,768]{1,0:T(8,128)(2,1)S(1)}, bf16[160,768]{1,0:T(8,128)(2,1)S(1)}, u32[]{:S(2)}, u32[]{:S(2)}) collective-permute-start(bf16[160,768]{1,0:T(8,128)(2,1)S(1)} %get-tuple-element.80), channel_id=1, source_target_pairs={{0,4},{2,6},{4,0},{6,2},{8,12},{10,14},{12,8},{14,10},{1,5},{3,7},... | collective-permute-start | bytes 737288 | tf_op jit(solution)/shard_map/ppermute | solution.py:489
  40.7 30.8 %collective-permute-start.13 = (bf16[160,768]{1,0:T(8,128)(2,1)S(1)}, bf16[160,768]{1,0:T(8,128)(2,1)S(1)}, u32[]{:S(2)}, u32[]{:S(2)}) collective-permute-start(bf16[160,768]{1,0:T(8,128)(2,1)S(1)} %get-tuple-element.82), channel_id=1, source_target_pairs={{0,8},{2,10},{4,12},{6,14},{8,0},{10,2},{12,4},{14,6},{1,9},{3,11}... | collective-permute-start | bytes 737288 | tf_op jit(solution)/shard_map/ppermute | solution.py:489
  43.2 28.2 %collective-permute-start.15 = (bf16[160,768]{1,0:T(8,128)(2,1)S(1)}, bf16[160,768]{1,0:T(8,128)(2,1)S(1)}, u32[]{:S(2)}, u32[]{:S(2)}) collective-permute-start(bf16[160,768]{1,0:T(8,128)(2,1)S(1)} %get-tuple-element.84), channel_id=1, source_target_pairs={{0,12},{2,14},{4,8},{6,10},{8,4},{10,6},{12,0},{14,2},{1,13},{3,15... | collective-permute-start | bytes 737288 | tf_op jit(solution)/shard_map/ppermute | solution.py:489
  43.5 15.9 %collective-permute-start.7 = (bf16[160,256]{1,0:T(8,128)(2,1)S(1)}, bf16[160,256]{1,0:T(8,128)(2,1)S(1)}, u32[]{:S(2)}, u32[]{:S(2)}) collective-permute-start(bf16[160,256]{1,0:T(8,128)(2,1)S(1)} %get-tuple-element.74), channel_id=1, source_target_pairs={{0,4},{2,6},{4,0},{6,2},{8,12},{10,14},{12,8},{14,10},{1,5},{3,7},... | collective-permute-start | bytes 245768 | tf_op jit(solution)/shard_map/ppermute | solution.py:489
  44.2 27.3 %collective-permute-start.8 = (bf16[160,256]{1,0:T(8,128)(2,1)S(1)}, bf16[160,256]{1,0:T(8,128)(2,1)S(1)}, u32[]{:S(2)}, u32[]{:S(2)}) collective-permute-start(bf16[160,256]{1,0:T(8,128)(2,1)S(1)} %get-tuple-element.75), channel_id=1, source_target_pairs={{0,8},{2,10},{4,12},{6,14},{8,0},{10,2},{12,4},{14,6},{1,9},{3,11}... | collective-permute-start | bytes 245768 | tf_op jit(solution)/shard_map/ppermute | solution.py:489
  59.4 12.0 %collective-permute-start.9 = (bf16[160,256]{1,0:T(8,128)(2,1)S(1)}, bf16[160,256]{1,0:T(8,128)(2,1)S(1)}, u32[]{:S(2)}, u32[]{:S(2)}) collective-permute-start(bf16[160,256]{1,0:T(8,128)(2,1)S(1)} %get-tuple-element.76), channel_id=1, source_target_pairs={{0,12},{2,14},{4,8},{6,10},{8,4},{10,6},{12,0},{14,2},{1,13},{3,15... | collective-permute-start | bytes 245768 | tf_op jit(solution)/shard_map/ppermute | solution.py:489
  76.9 14.5 %copy-start = (bf16[1,1024,2048]{2,1,0:T(8,128)(2,1)S(1)}, bf16[1,1024,2048]{2,1,0:T(8,128)(2,1)}, u32[]{:S(2)}) copy-start(bf16[1,1024,2048]{2,1,0:T(8,128)(2,1)} %param.14) | copy-start | bytes 12582916
  76.9 13.1 %collective-permute-start.16 = (bf16[160,256]{1,0:T(8,128)(2,1)S(1)}, bf16[160,256]{1,0:T(8,128)(2,1)S(1)}, u32[]{:S(2)}, u32[]{:S(2)}) collective-permute-start(bf16[160,256]{1,0:T(8,128)(2,1)S(1)} %get-tuple-element.86), channel_id=1, source_target_pairs={{0,4},{2,6},{4,0},{6,2},{8,12},{10,14},{12,8},{14,10},{1,5},{3,7},... | collective-permute-start | bytes 245768 | tf_op jit(solution)/shard_map/ppermute | solution.py:489
  79.0 12.4 %collective-permute-start.17 = (bf16[160,256]{1,0:T(8,128)(2,1)S(1)}, bf16[160,256]{1,0:T(8,128)(2,1)S(1)}, u32[]{:S(2)}, u32[]{:S(2)}) collective-permute-start(bf16[160,256]{1,0:T(8,128)(2,1)S(1)} %get-tuple-element.87), channel_id=1, source_target_pairs={{0,8},{2,10},{4,12},{6,14},{8,0},{10,2},{12,4},{14,6},{1,9},{3,11}... | collective-permute-start | bytes 245768 | tf_op jit(solution)/shard_map/ppermute | solution.py:489
  80.1 11.3 %collective-permute-start.18 = (bf16[160,256]{1,0:T(8,128)(2,1)S(1)}, bf16[160,256]{1,0:T(8,128)(2,1)S(1)}, u32[]{:S(2)}, u32[]{:S(2)}) collective-permute-start(bf16[160,256]{1,0:T(8,128)(2,1)S(1)} %get-tuple-element.88), channel_id=1, source_target_pairs={{0,12},{2,14},{4,8},{6,10},{8,4},{10,6},{12,0},{14,2},{1,13},{3,15... | collective-permute-start | bytes 245768 | tf_op jit(solution)/shard_map/ppermute | solution.py:489
  86.9 7.0 %collective-permute-start.20 = (bf16[160,256]{1,0:T(8,128)(2,1)S(1)}, bf16[160,256]{1,0:T(8,128)(2,1)S(1)}, u32[]{:S(2)}, u32[]{:S(2)}) collective-permute-start(bf16[160,256]{1,0:T(8,128)(2,1)S(1)} %get-tuple-element.92), channel_id=1, source_target_pairs={{0,4},{2,6},{4,0},{6,2},{8,12},{10,14},{12,8},{14,10},{1,5},{3,7},... | collective-permute-start | bytes 245768 | tf_op jit(solution)/shard_map/ppermute | solution.py:489
  88.0 7.5 %collective-permute-start.21 = (bf16[160,256]{1,0:T(8,128)(2,1)S(1)}, bf16[160,256]{1,0:T(8,128)(2,1)S(1)}, u32[]{:S(2)}, u32[]{:S(2)}) collective-permute-start(bf16[160,256]{1,0:T(8,128)(2,1)S(1)} %get-tuple-element.93), channel_id=1, source_target_pairs={{0,8},{2,10},{4,12},{6,14},{8,0},{10,2},{12,4},{14,6},{1,9},{3,11}... | collective-permute-start | bytes 245768 | tf_op jit(solution)/shard_map/ppermute | solution.py:489
  90.0 6.3 %collective-permute-start.22 = (bf16[160,256]{1,0:T(8,128)(2,1)S(1)}, bf16[160,256]{1,0:T(8,128)(2,1)S(1)}, u32[]{:S(2)}, u32[]{:S(2)}) collective-permute-start(bf16[160,256]{1,0:T(8,128)(2,1)S(1)} %get-tuple-element.94), channel_id=1, source_target_pairs={{0,12},{2,14},{4,8},{6,10},{8,4},{10,6},{12,0},{14,2},{1,13},{3,15... | collective-permute-start | bytes 245768 | tf_op jit(solution)/shard_map/ppermute | solution.py:489
  91.4 22.0 %copy-start.1 = (bf16[1,2,160,1024]{3,2,1,0:T(8,128)(2,1)S(1)}, bf16[1,2,160,1024]{3,2,1,0:T(8,128)(2,1)}, u32[]{:S(2)}) copy-start(bf16[1,2,160,1024]{3,2,1,0:T(8,128)(2,1)} %hidden.1) | copy-start | bytes 1966084
  93.4 8.1 %collective-permute-start.19 = (bf16[160,1024]{1,0:T(8,128)(2,1)S(1)}, bf16[160,1024]{1,0:T(8,128)(2,1)S(1)}, u32[]{:S(2)}, u32[]{:S(2)}) collective-permute-start(bf16[160,1024]{1,0:T(8,128)(2,1)S(1)} %get-tuple-element.90), channel_id=1, source_target_pairs={{0,1},{1,0},{2,3},{3,2},{4,5},{5,4},{6,7},{7,6},{8,9},{9,8},{10,11... | collective-permute-start | bytes 983048 | tf_op jit(solution)/shard_map/ppermute | solution.py:480
  98.3 10.7 %collective-permute-start.23 = (bf16[160,1024]{1,0:T(8,128)(2,1)S(1)}, bf16[160,1024]{1,0:T(8,128)(2,1)S(1)}, u32[]{:S(2)}, u32[]{:S(2)}) collective-permute-start(bf16[160,1024]{1,0:T(8,128)(2,1)S(1)} %get-tuple-element.95), channel_id=1, source_target_pairs={{0,2},{1,3},{2,0},{3,1},{4,6},{5,7},{6,4},{7,5},{8,10},{9,11},{10,... | collective-permute-start | bytes 983048 | tf_op jit(solution)/shard_map/ppermute | solution.py:480
  99.3 14.1 %collective-permute-start.24 = (bf16[160,1024]{1,0:T(8,128)(2,1)S(1)}, bf16[160,1024]{1,0:T(8,128)(2,1)S(1)}, u32[]{:S(2)}, u32[]{:S(2)}) collective-permute-start(bf16[160,1024]{1,0:T(8,128)(2,1)S(1)} %get-tuple-element.96), channel_id=1, source_target_pairs={{0,3},{1,2},{2,1},{3,0},{4,7},{5,6},{6,5},{7,4},{8,11},{9,10},{10,... | collective-permute-start | bytes 983048 | tf_op jit(solution)/shard_map/ppermute | solution.py:480

commit v3 on v2

v3 whole, which is shorter than its diff:
```python
import functools

import jax
import jax.numpy as jnp
from jax import lax
from jax.experimental import pallas as pl
from jax.experimental.pallas import tpu as pltpu
from jax.sharding import PartitionSpec as P

DH = 64
LANES = 128
SCALE = 0.25 * 1.4426950408889634
MIB = 1024 * 1024
SMALL = pl.CostEstimate(flops=1, bytes_accessed=1, transcendentals=0)
IN_VMEM = pl.BlockSpec(memory_space=pltpu.VMEM)


def passed_along(value, axis, steps):
    count = lax.axis_size(axis)
    leading, last = (max(0, -steps), min(count, count - steps))
    return lax.ppermute(value, axis, [(source, source + steps) for source in range(leading, last)])


def normalize(values, gain_row):
    widened = values.astype(jnp.float32)
    square = jnp.mean(widened * widened, axis=-1, keepdims=True)
    return (widened * lax.rsqrt(square + 1e-06) * gain_row).astype(jnp.bfloat16)


def gathered_body(hidden, memory, w_query, w_key, w_value, w_out, norm_gain, final_gain, lengths):
    encoder_side = lax.axis_index("segment") == 0
    own_part = hidden[0]
    arrived = passed_along(memory[0], "segment", 1)
    source_part = jnp.where(encoder_side, own_part, arrived)
    query_rows, source_rows = (
        lax.all_gather(own_part, "mp", axis=2, tiled=True),
        lax.all_gather(source_part, "mp", axis=2, tiled=True),
    )
    batch = own_part.shape[0]
    row_count = own_part.shape[1]
    width = query_rows.shape[2]
    key_gain = jnp.where(encoder_side, norm_gain[0], final_gain)
    query_in = normalize(query_rows.reshape(batch * row_count, width), norm_gain[0])
    key_in = normalize(source_rows.reshape(batch * row_count, width), key_gain)
    head_cols = w_query.shape[2]
    local_heads = head_cols // DH
    queries = jnp.dot(query_in, w_query[0], preferred_element_type=jnp.float32).astype(jnp.bfloat16)
    keys = jnp.dot(key_in, w_key[0], preferred_element_type=jnp.float32).astype(jnp.bfloat16)
    values = jnp.dot(key_in, w_value[0], preferred_element_type=jnp.float32).astype(jnp.bfloat16)
    keys = keys.reshape(batch, row_count, head_cols)
    values = values.reshape(batch, row_count, head_cols)
    query_length = lengths[0, :, 0]
    key_length = lengths[0, :, 1]
    split_queries = queries.reshape(batch, row_count, local_heads, DH)
    key_piece = lax.all_gather(keys, "seq", axis=1, tiled=True)
    value_piece = lax.all_gather(values, "seq", axis=1, tiled=True)
    key_count = key_piece.shape[1]
    scores = (
        jnp.einsum(
            "bqhd,bkhd->bqhk",
            split_queries,
            key_piece.reshape(batch, key_count, local_heads, DH),
            preferred_element_type=jnp.float32,
        )
        * 0.25
    )
    visible = jnp.arange(key_count)[None, :] < key_length[:, None]
    mask = visible[:, None, None, :]
    scores = jnp.where(mask, scores, -1e30)
    largest = jnp.max(scores, axis=-1)
    exponent = jnp.where(mask, jnp.exp(scores - largest[..., None]), 0.0)
    totals = jnp.sum(exponent, axis=-1)
    weighted = jnp.einsum(
        "bqhk,bkhd->bqhd",
        exponent.astype(jnp.bfloat16),
        value_piece.reshape(batch, key_count, local_heads, DH),
        preferred_element_type=jnp.float32,
    )
    context = weighted / totals[..., None]
    positions = lax.axis_index("seq") * row_count + jnp.arange(row_count)
    live_rows = positions[None, :] < query_length[:, None]
    context = jnp.where(live_rows[:, :, None, None], context, 0.0)
    context = context.astype(jnp.bfloat16).reshape(batch * row_count, head_cols)
    partial_value = jnp.dot(context, w_out[0], preferred_element_type=jnp.float32)
    branch = lax.psum_scatter(
        partial_value.astype(jnp.bfloat16), "mp", scatter_dimension=1, tiled=True
    ).astype(jnp.float32)
    branch = branch.reshape(batch, row_count, branch.shape[1])
    return (own_part.astype(jnp.float32) + branch).astype(jnp.bfloat16)[None]


HEAD, SIDE, INNER, ENC = 0, 1, 2, 3
BLOCK = 4


def in_hbm(array):
    return pltpu.with_memory_space_constraint(array, pltpu.HBM)


def split_kernel(table, hidden, memory, hidden_own, memory_own, hidden_away, memory_away, sems):
    inner = table[INNER]
    copies = [
        pltpu.make_async_copy(hidden.at[0, inner], hidden_own, sems.at[0]),
        pltpu.make_async_copy(memory.at[0, inner], memory_own, sems.at[1]),
        pltpu.make_async_copy(hidden.at[0, 1 - inner], hidden_away, sems.at[2]),
        pltpu.make_async_copy(memory.at[0, 1 - inner], memory_away, sems.at[3]),
    ]
    for copy in copies:
        copy.start()
    for copy in copies:
        copy.wait()


def split(table, hidden, memory):
    return pl.pallas_call(
        split_kernel,
        out_shape=[jax.ShapeDtypeStruct(hidden.shape[2:], jnp.bfloat16)] * 4,
        in_specs=[pl.BlockSpec(memory_space=pltpu.SMEM)] + [pl.BlockSpec(memory_space=pltpu.HBM)] * 2,
        out_specs=[pl.BlockSpec(memory_space=pltpu.VMEM)] * 4,
        scratch_shapes=[pltpu.SemaphoreType.DMA((4,))],
        compiler_params=pltpu.CompilerParams(vmem_limit_bytes=4 * MIB),
        cost_estimate=SMALL,
    )(table, in_hbm(hidden), in_hbm(memory))


def times_gain(values, gains, side, into):
    half = values.shape[1]
    wide = values.astype(jnp.float32)
    into[...] = (wide * gains[:, pl.ds(pl.multiple_of(side * half, half), half)]).astype(jnp.bfloat16)
    return jnp.sum(wide * wide, axis=-1, keepdims=True)


def start_weights(weights, halves, held, sems, parts):
    half = held.shape[2]
    size = half // parts
    copies = [[] for _ in weights]
    for n, weight in enumerate(weights):
        for h, side in enumerate(halves):
            for m in range(parts):
                source = pl.ds(pl.multiple_of(side * half + m * size, size), size)
                copy = pltpu.make_async_copy(
                    weight.at[0, source], held.at[n, h, pl.ds(m * size, size)], sems.at[n, h, m]
                )
                copy.start()
                copies[n].append(copy)
    return copies


def row_factor(total, features):
    return lax.rsqrt(total / features + 1e-06)


def fetch_kernel(parts, *refs):
    half = len(refs) // 2
    ins, outs, sems = refs[:half], refs[half:-1], refs[-1]
    copies = []
    for n, (source, target) in enumerate(zip(ins, outs)):
        size = target.shape[0] // parts
        for m in range(parts):
            rows = pl.ds(m * size, size)
            copies.append(pltpu.make_async_copy(source.at[0, rows], target.at[rows], sems.at[n, m]))
            copies[-1].start()
    for copy in copies:
        copy.wait()


def fetch(weights, parts=4):
    shape = weights[0].shape[1:]
    return pl.pallas_call(
        functools.partial(fetch_kernel, parts),
        out_shape=[pltpu.VMEM(shape, jnp.bfloat16)] * len(weights),
        in_specs=[pl.BlockSpec(memory_space=pltpu.HBM)] * len(weights),
        out_specs=[IN_VMEM] * len(weights),
        scratch_shapes=[pltpu.SemaphoreType.DMA((len(weights), parts))],
        compiler_params=pltpu.CompilerParams(vmem_limit_bytes=2 * MIB),
        cost_estimate=SMALL,
    )(*[in_hbm(w) for w in weights])


def first_kernel(count, table, qo, qn, ko, kn, gain, last_gain, wk, wv, wq, *rest):
    outs, (xk, xq, fk, fq) = rest[:count], rest[count:]
    side = table[SIDE]
    rows, half = qo.shape
    width = outs[0].shape[1] // 3

    def fill(own, other, gains, x, f):
        total = times_gain(own, gains, side, x.at[0]) + times_gain(other, gains, 1 - side, x.at[1])
        f[...] = jnp.broadcast_to(row_factor(total, 2 * half), f.shape)

    fill(qo[...], qn[...], gain, xq, fq)

    @pl.when(table[ENC] == 1)
    def _():
        xk[...] = xq[...]
        fk[...] = fq[...]

    @pl.when(table[ENC] == 0)
    def _():
        fill(ko[table[INNER]], kn[...], last_gain, xk, fk)

    def part(s):
        return pl.ds(pl.multiple_of(s * half, half), half)

    for turn in range(count - 1, -1, -1):
        columns = pl.ds(pl.multiple_of((table[HEAD] ^ turn) * width, width), width)
        for n, (x, f, w) in enumerate(((xk, fk, wk), (xk, fk, wv), (xq, fq, wq))):
            total = jnp.dot(x[0], w[part(side), columns], preferred_element_type=jnp.float32)
            total += jnp.dot(x[1], w[part(1 - side), columns], preferred_element_type=jnp.float32)
            scale = f[:, :1] * SCALE if n == 2 else f[:, :1]
            outs[turn][:, n * width : (n + 1) * width] = (total * scale).astype(jnp.bfloat16)


def project_first(table, qo, qn, ko, kn, gains, weights, count):
    rows, half = qo.shape
    width = 3 * weights[0].shape[1] // count
    return pl.pallas_call(
        functools.partial(first_kernel, count),
        out_shape=[jax.ShapeDtypeStruct((rows, width), jnp.bfloat16)] * count,
        grid_spec=pltpu.PrefetchScalarGridSpec(
            num_scalar_prefetch=1,
            grid=(1,),
            in_specs=[IN_VMEM] * (6 + len(weights)),
            out_specs=[IN_VMEM] * count,
            scratch_shapes=[pltpu.VMEM((2, rows, half), jnp.bfloat16)] * 2
            + [pltpu.VMEM((rows, LANES), jnp.float32)] * 2,
        ),
        compiler_params=pltpu.CompilerParams(vmem_limit_bytes=8 * MIB),
        cost_estimate=SMALL,
    )(table, qo, qn, ko, kn, *gains, *weights)


def project_kernel(parts, count, table, qo, qn, ko, kn, gain, last_gain, wk, wv, wq, *rest):
    outs, (xk, xq, fk, fq, held, sems) = rest[:-6], rest[-6:]
    side = table[SIDE]
    rows, half = qo.shape
    width = held.shape[3] // count
    copies = start_weights((wk, wv, wq), (side, 1 - side), held, sems, parts)

    def fill(own, other, gains, x, f):
        total = times_gain(own, gains, side, x.at[0]) + times_gain(other, gains, 1 - side, x.at[1])
        f[...] = jnp.broadcast_to(row_factor(total, 2 * half), (rows, LANES))

    fill(qo[...], qn[...], gain, xq, fq)

    @pl.when(table[ENC] == 1)
    def _():
        xk[...] = xq[...]
        fk[...] = fq[...]

    @pl.when(table[ENC] == 0)
    def _():
        fill(ko[...], kn[...], last_gain, xk, fk)

    for n, (x, f) in enumerate(((xk, fk), (xk, fk), (xq, fq))):
        for copy in copies[n]:
            copy.wait()
        scale = f[:, :1] * SCALE if n == 2 else f[:, :1]
        for turn in range(count):
            columns = pl.ds(pl.multiple_of((table[HEAD] ^ turn) * width, width), width)
            total = jnp.dot(x[0], held[n, 0, :, columns], preferred_element_type=jnp.float32)
            total += jnp.dot(x[1], held[n, 1, :, columns], preferred_element_type=jnp.float32)
            total = (total * scale).astype(jnp.bfloat16)
            outs[turn][:, n * width : (n + 1) * width] = total


def project(table, qo, qn, ko, kn, gains, weights, count, parts=4):
    rows, half = qo.shape
    columns = weights[0].shape[2]
    width = columns // count
    return pl.pallas_call(
        functools.partial(project_kernel, parts, count),
        out_shape=[jax.ShapeDtypeStruct((rows, 3 * width), jnp.bfloat16)] * count,
        grid_spec=pltpu.PrefetchScalarGridSpec(
            num_scalar_prefetch=1,
            grid=(1,),
            in_specs=[IN_VMEM] * 6 + [pl.BlockSpec(memory_space=pltpu.HBM)] * 3,
            out_specs=[IN_VMEM] * count,
            scratch_shapes=[pltpu.VMEM((2, rows, half), jnp.bfloat16)] * 2
            + [pltpu.VMEM((rows, LANES), jnp.float32)] * 2
            + [pltpu.VMEM((3, 2, half, columns), jnp.bfloat16), pltpu.SemaphoreType.DMA((3, 2, parts))],
        ),
        compiler_params=pltpu.CompilerParams(vmem_limit_bytes=32 * MIB),
        cost_estimate=SMALL,
    )(table, qo, qn, ko, kn, *gains, *[in_hbm(w) for w in weights])


def attend_kernel(count, chunk, tile, places, table, lengths, *refs):
    q_refs, keyed = refs[:count], refs[count : 3 * count]
    outs, (qs, ks, vs, contexts) = refs[3 * count : 4 * count], refs[4 * count :]
    rows, width = outs[0].shape
    pairs = width // LANES
    query_length = lengths[2 * table[INNER]]
    key_length = lengths[2 * table[INNER] + 1]
    lane = lax.broadcasted_iota(jnp.int32, (rows, LANES), 1)
    row = lax.broadcasted_iota(jnp.int32, (rows, LANES), 0)
    low = lane < DH
    zero = jnp.zeros((rows, LANES), jnp.bfloat16)
    one = jnp.ones((rows, LANES), jnp.bfloat16)
    unit = jnp.where(lane == 0, one, zero)
    for j in range(2 * count):
        here = pl.ds(j * rows, rows)
        hides = jnp.logical_and(lane == 0, row + table[BLOCK + j] >= key_length)
        bias = jnp.where(hides, -1e30, 0.0).astype(jnp.bfloat16)
        for pair in range(pairs):
            columns = slice(pair * LANES, (pair + 1) * LANES)
            key = keyed[j][:, columns]
            value = keyed[j][:, width + pair * LANES : width + (pair + 1) * LANES]
            ks[pair, 0, here, :LANES] = jnp.where(low, key, zero)
            ks[pair, 1, here, :LANES] = jnp.where(low, zero, key)
            ks[pair, 0, here, LANES:] = bias
            ks[pair, 1, here, LANES:] = bias
            vs[pair, 0, here, :] = jnp.where(low, value, one)
            vs[pair, 1, here, :] = jnp.where(low, one, value)
    for j in range(count):
        here = pl.ds(j * rows, rows)
        for pair in range(pairs):
            start = places[j] * width + pair * LANES
            qs[pair, here, :LANES] = q_refs[j][:, start : start + LANES]
            qs[pair, here, LANES:] = unit

    low = lax.broadcasted_iota(jnp.int32, (tile, LANES), 1) < DH
    for pair in range(pairs):
        for t in range(count * rows // tile):
            query = qs[pair, pl.ds(t * tile, tile), :]
            sums = []
            for head in range(2):
                scores = lax.dot_general(
                    query, ks[pair, head], (((1,), (1,)), ((), ())), preferred_element_type=jnp.float32
                )
                largest = jnp.max(scores, axis=-1, keepdims=True)
                weights = jnp.exp2(scores - largest).astype(jnp.bfloat16)
                sums.append(jnp.dot(weights, vs[pair, head], preferred_element_type=jnp.float32))
            weighted = jnp.where(low, sums[0], sums[1])
            totals = jnp.where(low, pltpu.roll(sums[0], DH, 1), pltpu.roll(sums[1], DH, 1))
            contexts[pl.ds(t * tile, tile), pair * LANES : (pair + 1) * LANES] = (weighted / totals).astype(
                jnp.bfloat16
            )

    for j in range(count):
        live = row + table[BLOCK + 2 * j + chunk] < query_length
        for pair in range(pairs):
            columns = slice(pair * LANES, (pair + 1) * LANES)
            outs[j][:, columns] = jnp.where(live, contexts[pl.ds(j * rows, rows), columns], zero)


def attend(table, lengths, queries, keyed, chunk, width):
    count = len(queries)
    rows = queries[0][0].shape[0]
    total = 2 * count * rows

    return pl.pallas_call(
        functools.partial(
            attend_kernel, count, chunk, 2 * rows if count % 2 == 0 else rows, [place for _, place in queries]
        ),
        out_shape=[jax.ShapeDtypeStruct((rows, width), jnp.bfloat16)] * count,
        grid_spec=pltpu.PrefetchScalarGridSpec(
            num_scalar_prefetch=2,
            grid=(1,),
            in_specs=[IN_VMEM] * (3 * count),
            out_specs=[IN_VMEM] * count,
            scratch_shapes=[
                pltpu.VMEM((width // LANES, count * rows, 2 * LANES), jnp.bfloat16),
                pltpu.VMEM((width // LANES, 2, total, 2 * LANES), jnp.bfloat16),
                pltpu.VMEM((width // LANES, 2, total, LANES), jnp.bfloat16),
                pltpu.VMEM((count * rows, width), jnp.bfloat16),
            ],
        ),
        compiler_params=pltpu.CompilerParams(vmem_limit_bytes=32 * MIB),
        cost_estimate=SMALL,
    )(table, lengths, *[array for array, _ in queries], *keyed)


def output_kernel(count, table, w, *refs):
    pieces, outs, x = refs[:count], refs[count : count + 2], refs[-1]
    width = pieces[0].shape[1]
    half = outs[0].shape[1]
    for turn in range(count):
        place = pl.multiple_of((table[HEAD] ^ turn) * width, width)
        x[:, pl.ds(place, width)] = pieces[turn][...]
    for i in range(2):
        columns = pl.ds(pl.multiple_of((1 - (table[SIDE] ^ i)) * half, half), half)
        outs[i][...] = jnp.dot(x[...], w[:, columns], preferred_element_type=jnp.float32).astype(jnp.bfloat16)


def output_parts(table, pieces, w_out):
    rows, width = pieces[0].shape
    depth, half = w_out.shape[0], w_out.shape[1] // 2
    return pl.pallas_call(
        functools.partial(output_kernel, len(pieces)),
        out_shape=[jax.ShapeDtypeStruct((rows, half), jnp.bfloat16)] * 2,
        grid_spec=pltpu.PrefetchScalarGridSpec(
            num_scalar_prefetch=1,
            grid=(1,),
            in_specs=[IN_VMEM] * (1 + len(pieces)),
            out_specs=[IN_VMEM] * 2,
            scratch_shapes=[pltpu.VMEM((rows, depth), jnp.bfloat16)],
        ),
        compiler_params=pltpu.CompilerParams(vmem_limit_bytes=16 * MIB),
        cost_estimate=SMALL,
    )(table, w_out, *pieces)


def add_kernel(table, hidden, own, beside, across, corner, out):
    def total(a, b):
        out[0, 0] = (
            hidden[0, 0].astype(jnp.float32) + (a[...].astype(jnp.float32) + b[...].astype(jnp.float32))
        ).astype(jnp.bfloat16)

    @pl.when(pl.program_id(0) == 0)
    def _():
        total(own, beside)

    @pl.when(pl.program_id(0) == 1)
    def _():
        total(across, corner)


def add_all(table, hidden, own, beside, across, corner):
    rows, half = own.shape
    block = pl.BlockSpec((1, 1, rows, half), lambda i, table: (0, table[INNER] ^ i, 0, 0))
    part = pl.BlockSpec((rows, half), lambda i, table: (0, 0))
    return pl.pallas_call(
        add_kernel,
        out_shape=jax.ShapeDtypeStruct(hidden.shape, jnp.bfloat16),
        grid_spec=pltpu.PrefetchScalarGridSpec(
            num_scalar_prefetch=1,
            grid=(2,),
            in_specs=[block, part, part, part, part],
            out_specs=block,
        ),
        compiler_params=pltpu.CompilerParams(vmem_limit_bytes=16 * MIB),
    )(table, hidden, own, beside, across, corner)


def body(hidden, memory, w_query, w_key, w_value, w_out, norm_gain, final_gain, lengths):
    seq, mp = lax.axis_size("seq"), lax.axis_size("mp")
    count = seq // 2
    rows, half = hidden.shape[2:]
    width = w_query.shape[2] // count

    place, side = lax.axis_index("seq"), lax.axis_index("mp")
    outer, inner = place // 2, place % 2
    encoder = (lax.axis_index("segment") == 0).astype(jnp.int32)
    starts = [
        (2 * (outer ^ turn) + (inner ^ chunk)) * rows for turn in range(count) for chunk in range(2)
    ]
    table = jnp.stack([outer, side, inner, encoder] + starts).astype(jnp.int32)

    def moved(value, swap_seq, swap_mp, segments=(0, 1)):
        pairs = [
            ((g * seq + s) * mp + m, (g * seq + (s ^ swap_seq)) * mp + (m ^ swap_mp))
            for g in segments
            for s in range(seq)
            for m in range(mp)
        ]
        return lax.ppermute(value, ("segment", "seq", "mp"), pairs)

    def handed(value, swap_seq, swap_mp):
        pairs = [
            (s * mp + m, seq * mp + (s ^ swap_seq) * mp + (m ^ swap_mp)) for s in range(seq) for m in range(mp)
        ]
        return lax.ppermute(value, ("segment", "seq", "mp"), pairs)

    def turned(value, turn):
        return moved(value, 2 * turn, 0) if turn else value

    def after(value, *others):
        return lax.optimization_barrier((value, *others))[0]

    hidden_own, memory_own, hidden_away, memory_away = split(table, hidden, memory)
    query_beside = moved(hidden_own, 0, 1)
    source_beside = handed(memory_own, 0, 1)
    source_here = handed(after(memory[0], hidden_own), 0, 0)
    query_across = moved(hidden_away, 1, 0)
    source_across = handed(memory_away, 1, 0)
    weights = (w_key, w_value, w_query)
    fetched = fetch([after(w, query_beside) for w in weights])

    gains = (in_hbm(norm_gain), in_hbm(final_gain.reshape(1, -1)))
    turns = range(count - 1, -1, -1)
    products = project_first(table, hidden_own, query_beside, source_here, source_beside, gains, fetched, count)
    first = {t: turned(products[t], t) for t in turns}
    query_corner = moved(after(query_across, fetched), 0, 1)
    source_corner = moved(after(source_across, fetched), 0, 1, (1,))
    query_across = after(query_across, products)
    products = project(table, query_across, query_corner, source_across, source_corner, gains, weights, count)
    second = {t: turned(after(products[t], first[1]) if t == 1 else products[t], t) for t in turns}
    keyed = [part[t] for t in range(count) for part in (first, second)]

    lengths = lengths.reshape(-1)
    context = attend(table, lengths, [(second[t], 2) for t in range(count)], keyed, 1, width)
    second_context = [moved(context[t], 2 * t + 1, 0) for t in range(count)]
    queries = [(after(first[t], context), 2) for t in range(count)]
    context = attend(table, lengths, queries, keyed, 0, width)
    first_context = [moved(after(context[t], second_context), 2 * t, 0) if t else context[t] for t in range(count)]
    away, second_own = output_parts(table, second_context, w_out[0])
    second_beside = moved(away, 0, 1)
    away, own = output_parts(table, first_context, w_out[0])
    first_beside = moved(away, 0, 1)
    return add_all(table, hidden, own, first_beside, second_own, second_beside)


def solution(mesh):
    seq, mp = mesh.shape["seq"], mesh.shape["mp"]

    def chosen(*arrays):
        batch, columns = arrays[0].shape[1], arrays[2].shape[2]
        count = seq // 2
        fits = (
            batch == 2
            and mp == 2
            and seq % 2 == 0
            and count & (count - 1) == 0
            and (columns // mp) % (count * LANES) == 0
            and (arrays[0].shape[2] // seq) % 16 == 0
        )
        return jax.shard_map(
            body if fits else gathered_body,
            mesh=mesh,
            in_specs=(
                P("segment", None, "seq", "mp"),
                P("segment", None, "seq", "mp"),
                P("segment", None, "mp"),
                P("segment", None, "mp"),
                P("segment", None, "mp"),
                P("segment", "mp", None),
                P("segment", None),
                P(),
                P("segment", None, None),
            ),
            out_specs=P("segment", None, "seq", "mp"),
            check_vma=False,
        )(*arrays)

    return chosen
```

time: 115 us -> 110 us (0.957)
  waiting for transfers between devices: 34.9 us -> 41.7 us
  starting transfers between devices: 41.2 us -> 35.2 us
  local copies, waits for them, and re-layouts: 5.62 us -> 0.18 us
    ppermute x21 -> x19, waiting for transfers between devices: 34.4 us -> 41.7 us  [moved(): return lax.ppermute(value, ('segment', 'seq', 'mp'), pairs)]
    squeeze x4 -> x0, local copies, waits for them, and re-layouts: 5.44 us -> none  [chosen(): return lax.dynamic_index_in_dim(array, index, 0, keepdims=False)]
    ppermute x21 -> x19, starting transfers between devices: 34.6 us -> 29.5 us  [moved(): return lax.ppermute(value, ('segment', 'seq', 'mp'), pairs)]
    pallas_call x2, Pallas kernels: 4.03 us -> 2.84 us  [output_parts(): pl.pallas_call(functools.partial(output_kernel, len(pieces)), out_shape=[...]
    pallas_call x2 -> x3, Pallas kernels: 9.47 us -> 10.5 us  [the longest x1 4.7 us: fetch(): pl.pallas_call(functools.partial(fetch_kernel, parts), out_shape=[pltpu.V...]
    ppermute x4 -> x3, starting transfers between devices: 6.63 us -> 5.77 us  [handed(): return lax.ppermute(value, ('segment', 'seq', 'mp'), pairs)]
  transfers between devices with their start and end apart: 25 -> 22, of which waited for: 8 -> 8; matrix products, arithmetic and copies ran while one was open for 5% -> 0% of each run, Pallas kernels for 23% -> 22%
where the time goes in v3:
time: 110 us
  waiting for transfers between devices  41.7 us (38%)
  starting transfers between devices  35.2 us (32%)
  Pallas kernels  32.4 us (29%)
    ppermute x19, waiting for transfers between devices, moved(): return lax.ppermute(value, ('segment', 'seq', 'mp'), pairs)  41.7 us
    ppermute x19, starting transfers between devices, moved(): return lax.ppermute(value, ('segment', 'seq', 'mp'), pairs)  29.5 us
    pallas_call x2, Pallas kernels, attend(): pl.pallas_call(functools.partial(attend_kernel, count, chunk, 2 * rows if...  10.4 us
    pallas_call x1, Pallas kernels, project(): pl.pallas_call(functools.partial(project_kernel, parts, count), out_shape...  7.11 us
    ppermute x3, starting transfers between devices, handed(): return lax.ppermute(value, ('segment', 'seq', 'mp'), pairs)  5.77 us
    pallas_call x1, Pallas kernels, fetch(): pl.pallas_call(functools.partial(fetch_kernel, parts), out_shape=[pltpu.V...  4.7 us
    pallas_call x1, Pallas kernels, project_first(): pl.pallas_call(functools.partial(first_kernel, count), out_shape=[jax.Sha...  3.93 us
    pallas_call x2, Pallas kernels, output_parts(): pl.pallas_call(functools.partial(output_kernel, len(pieces)), out_shape=[...  2.84 us
  transfers between devices with their start and end apart: 22, of which 8 were waited for; matrix products, arithmetic and copies ran while one was open for 0% of the time, Pallas kernels for 22%

profile of v3, /device:TPU:0, one launch (start us, length us, event | category | flops | bytes accessed | tf_op | source)
XLA Modules:
  0.0 109.6 jit_solution(7660580104310528144)
XLA Ops:
  0.0 0.1 stack.55.table
  0.1 1.9 %shard_map.91 = (bf16[160,1024]{1,0:T(8,128)(2,1)S(1)}, bf16[160,1024]{1,0:T(8,128)(2,1)S(1)}, bf16[160,1024]{1,0:T(8,128)(2,1)S(1)}, bf16[160,1024]{1,0:T(8,128)(2,1)S(1)}) custom-call(s32[12]{0:T(128)S(1)} %stack.55.table, bf16[1,2,160,1024]{3,2,1,0:T(8,128)(2,1)} %hidden.3, bf16[1,2,160,1024]{3,2,1,0:T(8,128)(2,1)} %memory.1), custom_call_target="tpu_custom_call" | custom-call | flops 1 | bytes 1 | tf_op jit(solution)/shard_map/pallas_call | solution.py:115
  1.9 2.4 %collective-permute-start.1 = (bf16[2,160,1024]{2,1,0:T(8,128)(2,1)}, bf16[2,160,1024]{2,1,0:T(8,128)(2,1)S(1)}, u32[]{:S(2)}, u32[]{:S(2)}) collective-permute-start(bf16[2,160,1024]{2,1,0:T(8,128)(2,1)} %bitcast.17), channel_id=1, source_target_pairs={{0,16},{1,17},{2,18},{3,19},{4,20},{5,21},{6,22},{7,23},{8,24},{9,... | collective-permute-start | bytes 1966088 | tf_op jit(solution)/shard_map/ppermute | solution.py:462
  4.4 2.4 %collective-permute-start = (bf16[160,1024]{1,0:T(8,128)(2,1)S(1)}, bf16[160,1024]{1,0:T(8,128)(2,1)S(1)}, u32[]{:S(2)}, u32[]{:S(2)}) collective-permute-start(bf16[160,1024]{1,0:T(8,128)(2,1)S(1)} %get-tuple-element.47.qo), channel_id=1, source_target_pairs={{0,1},{1,0},{2,3},{3,2},{4,5},{5,4},{6,7},{7,6},{8,9},{9,8},{10,11... | collective-permute-start | bytes 983048 | tf_op jit(solution)/shard_map/ppermute | solution.py:456
  6.8 2.1 %collective-permute-start.5 = (bf16[160,1024]{1,0:T(8,128)(2,1)S(1)}, bf16[160,1024]{1,0:T(8,128)(2,1)S(1)}, u32[]{:S(2)}, u32[]{:S(2)}) collective-permute-start(bf16[160,1024]{1,0:T(8,128)(2,1)S(1)} %get-tuple-element.63), channel_id=1, source_target_pairs={{0,18},{1,19},{2,16},{3,17},{4,22},{5,23},{6,20},{7,21},{8,26},{9,... | collective-permute-start | bytes 983048 | tf_op jit(solution)/shard_map/ppermute | solution.py:462
  8.9 0.8 collective-permute-start.3
  9.6 1.3 %collective-permute-start.2 = (bf16[160,1024]{1,0:T(8,128)(2,1)S(1)}, bf16[160,1024]{1,0:T(8,128)(2,1)S(1)}, u32[]{:S(2)}, u32[]{:S(2)}) collective-permute-start(bf16[160,1024]{1,0:T(8,128)(2,1)S(1)} %get-tuple-element.49), channel_id=1, source_target_pairs={{0,17},{1,16},{2,19},{3,18},{4,21},{5,20},{6,23},{7,22},{8,25},{9,... | collective-permute-start | bytes 983048 | tf_op jit(solution)/shard_map/ppermute | solution.py:462
  10.9 3.1 %collective-permute-done.qn = bf16[160,1024]{1,0:T(8,128)(2,1)S(1)} collective-permute-done((bf16[160,1024]{1,0:T(8,128)(2,1)S(1)}, bf16[160,1024]{1,0:T(8,128)(2,1)S(1)}, u32[]{:S(2)}, u32[]{:S(2)}) %collective-permute-start) | collective-permute-done | bytes 327712 | tf_op jit(solution)/shard_map/ppermute | solution.py:456
  14.0 4.7 %shard_map.92 = (bf16[2048,1024]{1,0:T(8,128)(2,1)S(1)}, bf16[2048,1024]{1,0:T(8,128)(2,1)S(1)}, bf16[2048,1024]{1,0:T(8,128)(2,1)S(1)}) custom-call(bf16[1,2048,1024]{2,1,0:T(8,128)(2,1)} %wk.1, bf16[1,2048,1024]{2,1,0:T(8,128)(2,1)} %wv.1, bf16[1,2048,1024]{2,1,0:T(8,128)(2,1)} %wq.1), custom_call_target="tpu_custom_call" | custom-call | flops 1 | bytes 1 | tf_op jit(solution)/shard_map/pallas_call | solution.py:169
  18.7 0.0 collective-permute-done.5.ko
  18.7 1.6 %collective-permute-done.3.qo = bf16[160,1024]{1,0:T(8,128)(2,1)S(1)} collective-permute-done((bf16[160,1024]{1,0:T(8,128)(2,1)S(1)}, bf16[160,1024]{1,0:T(8,128)(2,1)S(1)}, u32[]{:S(2)}, u32[]{:S(2)}) %collective-permute-start.3) | collective-permute-done | bytes 327712 | tf_op jit(solution)/shard_map/ppermute | solution.py:456
  20.3 0.3 collective-permute-start.4
  20.6 0.7 collective-permute-start.6
  21.3 0.0 collective-permute-done.2.kn
  21.3 0.0 collective-permute-done.1.ko
  21.3 3.9 %shard_map.93 = (bf16[160,768]{1,0:T(8,128)(2,1)S(1)}, bf16[160,768]{1,0:T(8,128)(2,1)S(1)}, bf16[160,768]{1,0:T(8,128)(2,1)S(1)}, bf16[160,768]{1,0:T(8,128)(2,1)S(1)}) custom-call(s32[12]{0:T(128)S(1)} %stack.55.table, bf16[160,1024]{1,0:T(8,128)(2,1)S(1)} %get-tuple-element.47.qo, bf16[160,1024]{1,0:T(8,128)(2,1)S(1)} %collective-permute-done.qn, ...), custom_call_target="tpu_custom_call" | custom-call | flops 1 | bytes 1 | tf_op jit(solution)/shard_map/pallas_call | solution.py:216
  25.3 1.8 %collective-permute-start.7 = (bf16[160,768]{1,0:T(8,128)(2,1)S(1)}, bf16[160,768]{1,0:T(8,128)(2,1)S(1)}, u32[]{:S(2)}, u32[]{:S(2)}) collective-permute-start(bf16[160,768]{1,0:T(8,128)(2,1)S(1)} %get-tuple-element.58), channel_id=1, source_target_pairs={{0,4},{1,5},{2,6},{3,7},{4,0},{5,1},{6,2},{7,3},{8,12},{9,13},{10,... | collective-permute-start | bytes 737288 | tf_op jit(solution)/shard_map/ppermute | solution.py:456
  27.1 2.6 %collective-permute-start.11 = (bf16[160,768]{1,0:T(8,128)(2,1)S(1)}, bf16[160,768]{1,0:T(8,128)(2,1)S(1)}, u32[]{:S(2)}, u32[]{:S(2)}) collective-permute-start(bf16[160,768]{1,0:T(8,128)(2,1)S(1)} %get-tuple-element.59), channel_id=1, source_target_pairs={{0,8},{1,9},{2,10},{3,11},{4,12},{5,13},{6,14},{7,15},{8,0},{9,1},... | collective-permute-start | bytes 737288 | tf_op jit(solution)/shard_map/ppermute | solution.py:456
  29.7 0.0 collective-permute-start.12
  29.7 0.0 copy-start.2
  29.7 0.9 collective-permute-done.4.qn
  30.6 0.0 collective-permute-done.6.kn
  30.6 7.1 %shard_map.94 = (bf16[160,768]{1,0:T(8,128)(2,1)S(1)}, bf16[160,768]{1,0:T(8,128)(2,1)S(1)}, bf16[160,768]{1,0:T(8,128)(2,1)S(1)}, bf16[160,768]{1,0:T(8,128)(2,1)S(1)}) custom-call(s32[12]{0:T(128)S(1)} %stack.55.table, bf16[160,1024]{1,0:T(8,128)(2,1)S(1)} %collective-permute-done.3.qo, bf16[160,1024]{1,0:T(8,128)(2,1)S(1)} %collective-permute-done.4.qn, ...), custom_call_target="tpu_custom_call" | custom-call | flops 1 | bytes 1 | tf_op jit(solution)/shard_map/pallas_call | solution.py:270
  37.8 2.6 %collective-permute-start.9 = (bf16[160,768]{1,0:T(8,128)(2,1)S(1)}, bf16[160,768]{1,0:T(8,128)(2,1)S(1)}, u32[]{:S(2)}, u32[]{:S(2)}) collective-permute-start(bf16[160,768]{1,0:T(8,128)(2,1)S(1)} %get-tuple-element.68), channel_id=1, source_target_pairs={{0,8},{1,9},{2,10},{3,11},{4,12},{5,13},{6,14},{7,15},{8,0},{9,1},... | collective-permute-start | bytes 737288 | tf_op jit(solution)/shard_map/ppermute | solution.py:456
  40.3 1.3 %collective-permute-start.10 = (bf16[160,768]{1,0:T(8,128)(2,1)S(1)}, bf16[160,768]{1,0:T(8,128)(2,1)S(1)}, u32[]{:S(2)}, u32[]{:S(2)}) collective-permute-start(bf16[160,768]{1,0:T(8,128)(2,1)S(1)} %get-tuple-element.69), channel_id=1, source_target_pairs={{0,12},{1,13},{2,14},{3,15},{4,8},{5,9},{6,10},{7,11},{8,4},{9,5},... | collective-permute-start | bytes 737288 | tf_op jit(solution)/shard_map/ppermute | solution.py:456
  41.7 0.0 collective-permute-done.7.refs_6_.refs_1_
  41.7 0.2 collective-permute-start.8
  41.9 0.0 copy-done.2
  41.9 0.1 reshape.6.lengths
  42.0 0.0 copy-start
  42.0 15.9 %collective-permute-done.11.refs_8_.refs_2_ = bf16[160,768]{1,0:T(8,128)(2,1)S(1)} collective-permute-done((bf16[160,768]{1,0:T(8,128)(2,1)S(1)}, bf16[160,768]{1,0:T(8,128)(2,1)S(1)}, u32[]{:S(2)}, u32[]{:S(2)}) %collective-permute-start.11) | collective-permute-done | bytes 245792 | tf_op jit(solution)/shard_map/ppermute | solution.py:456
  57.9 0.0 collective-permute-done.12.refs_10_.refs_3_
  57.9 10.5 %collective-permute-done.9.refs_2_.refs_9_ = bf16[160,768]{1,0:T(8,128)(2,1)S(1)} collective-permute-done((bf16[160,768]{1,0:T(8,128)(2,1)S(1)}, bf16[160,768]{1,0:T(8,128)(2,1)S(1)}, u32[]{:S(2)}, u32[]{:S(2)}) %collective-permute-start.9) | collective-permute-done | bytes 245792 | tf_op jit(solution)/shard_map/ppermute | solution.py:456
  68.5 0.0 collective-permute-done.10.refs_3_.refs_11_
  68.5 0.0 collective-permute-done.8.refs_1_.refs_7_
  68.5 5.2 %shard_map.95 = (bf16[160,256]{1,0:T(8,128)(2,1)S(1)}, bf16[160,256]{1,0:T(8,128)(2,1)S(1)}, bf16[160,256]{1,0:T(8,128)(2,1)S(1)}, bf16[160,256]{1,0:T(8,128)(2,1)S(1)}) custom-call(s32[12]{0:T(128)S(1)} %stack.55.table, s32[4]{0:T(128)S(1)} %reshape.6.lengths, bf16[160,768]{1,0:T(8,128)(2,1)S(1)} %get-tuple-element.65.refs_0_.refs_5_, ...), custom_call_target="tpu_custom_call" | custom-call | flops 1 | bytes 1 | tf_op jit(solution)/shard_map/pallas_call | solution.py:351
  73.7 1.5 %collective-permute-start.13 = (bf16[160,256]{1,0:T(8,128)(2,1)S(1)}, bf16[160,256]{1,0:T(8,128)(2,1)S(1)}, u32[]{:S(2)}, u32[]{:S(2)}) collective-permute-start(bf16[160,256]{1,0:T(8,128)(2,1)S(1)} %get-tuple-element.70), channel_id=1, source_target_pairs={{0,2},{1,3},{2,0},{3,1},{4,6},{5,7},{6,4},{7,5},{8,10},{9,11},{10,... | collective-permute-start | bytes 245768 | tf_op jit(solution)/shard_map/ppermute | solution.py:456
  75.2 4.1 %collective-permute-start.14 = (bf16[160,256]{1,0:T(8,128)(2,1)S(1)}, bf16[160,256]{1,0:T(8,128)(2,1)S(1)}, u32[]{:S(2)}, u32[]{:S(2)}) collective-permute-start(bf16[160,256]{1,0:T(8,128)(2,1)S(1)} %get-tuple-element.71), channel_id=1, source_target_pairs={{0,6},{1,7},{2,4},{3,5},{4,2},{5,3},{6,0},{7,1},{8,14},{9,15},{10,... | collective-permute-start | bytes 245768 | tf_op jit(solution)/shard_map/ppermute | solution.py:456
  79.3 1.1 collective-permute-start.15
  80.4 2.4 %collective-permute-start.16 = (bf16[160,256]{1,0:T(8,128)(2,1)S(1)}, bf16[160,256]{1,0:T(8,128)(2,1)S(1)}, u32[]{:S(2)}, u32[]{:S(2)}) collective-permute-start(bf16[160,256]{1,0:T(8,128)(2,1)S(1)} %get-tuple-element.73), channel_id=1, source_target_pairs={{0,14},{1,15},{2,12},{3,13},{4,10},{5,11},{6,8},{7,9},{8,6},{9,7},... | collective-permute-start | bytes 245768 | tf_op jit(solution)/shard_map/ppermute | solution.py:456
  82.8 5.2 %shard_map.96 = (bf16[160,256]{1,0:T(8,128)(2,1)S(1)}, bf16[160,256]{1,0:T(8,128)(2,1)S(1)}, bf16[160,256]{1,0:T(8,128)(2,1)S(1)}, bf16[160,256]{1,0:T(8,128)(2,1)S(1)}) custom-call(s32[12]{0:T(128)S(1)} %stack.55.table, s32[4]{0:T(128)S(1)} %reshape.6.lengths, bf16[160,768]{1,0:T(8,128)(2,1)S(1)} %get-tuple-element.74.refs_4_.refs_0_, ...), custom_call_target="tpu_custom_call" | custom-call | flops 1 | bytes 1 | tf_op jit(solution)/shard_map/pallas_call | solution.py:351
  88.0 0.0 collective-permute-done.13.refs_0_
  88.0 0.0 collective-permute-done.14.refs_1_
  88.0 0.0 collective-permute-done.15.refs_2_
  88.0 0.0 collective-permute-done.16.refs_3_
  88.0 1.4 %collective-permute-start.17 = (bf16[160,256]{1,0:T(8,128)(2,1)S(1)}, bf16[160,256]{1,0:T(8,128)(2,1)S(1)}, u32[]{:S(2)}, u32[]{:S(2)}) collective-permute-start(bf16[160,256]{1,0:T(8,128)(2,1)S(1)} %get-tuple-element.80), channel_id=1, source_target_pairs={{0,4},{1,5},{2,6},{3,7},{4,0},{5,1},{6,2},{7,3},{8,12},{9,13},{10,... | collective-permute-start | bytes 245768 | tf_op jit(solution)/shard_map/ppermute | solution.py:456
  89.4 1.6 %collective-permute-start.18 = (bf16[160,256]{1,0:T(8,128)(2,1)S(1)}, bf16[160,256]{1,0:T(8,128)(2,1)S(1)}, u32[]{:S(2)}, u32[]{:S(2)}) collective-permute-start(bf16[160,256]{1,0:T(8,128)(2,1)S(1)} %get-tuple-element.82), channel_id=1, source_target_pairs={{0,8},{1,9},{2,10},{3,11},{4,12},{5,13},{6,14},{7,15},{8,0},{9,1},... | collective-permute-start | bytes 245768 | tf_op jit(solution)/shard_map/ppermute | solution.py:456
  91.0 1.5 %collective-permute-start.19 = (bf16[160,256]{1,0:T(8,128)(2,1)S(1)}, bf16[160,256]{1,0:T(8,128)(2,1)S(1)}, u32[]{:S(2)}, u32[]{:S(2)}) collective-permute-start(bf16[160,256]{1,0:T(8,128)(2,1)S(1)} %get-tuple-element.84), channel_id=1, source_target_pairs={{0,12},{1,13},{2,14},{3,15},{4,8},{5,9},{6,10},{7,11},{8,4},{9,5},... | collective-permute-start | bytes 245768 | tf_op jit(solution)/shard_map/ppermute | solution.py:456
  92.5 0.0 copy-done
  92.5 0.0 copy-start.1
  92.5 1.4 %shard_map.98 = (bf16[160,1024]{1,0:T(8,128)(2,1)S(1)}, bf16[160,1024]{1,0:T(8,128)(2,1)S(1)}) custom-call(s32[12]{0:T(128)S(1)} %stack.55.table, bf16[1024,2048]{1,0:T(8,128)(2,1)S(1)} %bitcast.15, bf16[160,256]{1,0:T(8,128)(2,1)S(1)} %collective-permute-done.13.refs_0_, bf16[160,256]{1,0:T(8,128)(2,1)S(1)} %collective-permute-done.14.refs_1_, ...), custom_call_target="tpu_custom_call" | custom-call | flops 1 | bytes 1 | tf_op jit(solution)/shard_map/pallas_call | solution.py:388
  93.9 1.6 %collective-permute-start.21 = (bf16[160,1024]{1,0:T(8,128)(2,1)S(1)}, bf16[160,1024]{1,0:T(8,128)(2,1)S(1)}, u32[]{:S(2)}, u32[]{:S(2)}) collective-permute-start(bf16[160,1024]{1,0:T(8,128)(2,1)S(1)} %get-tuple-element.88), channel_id=1, source_target_pairs={{0,1},{1,0},{2,3},{3,2},{4,5},{5,4},{6,7},{7,6},{8,9},{9,8},{10,11... | collective-permute-start | bytes 983048 | tf_op jit(solution)/shard_map/ppermute | solution.py:456
  95.5 0.0 collective-permute-done.17.refs_1_
  95.5 1.9 %collective-permute-done.18.refs_2_ = bf16[160,256]{1,0:T(8,128)(2,1)S(1)} collective-permute-done((bf16[160,256]{1,0:T(8,128)(2,1)S(1)}, bf16[160,256]{1,0:T(8,128)(2,1)S(1)}, u32[]{:S(2)}, u32[]{:S(2)}) %collective-permute-start.18) | collective-permute-done | bytes 81952 | tf_op jit(solution)/shard_map/ppermute | solution.py:456
  97.4 0.0 collective-permute-done.19.refs_3_
  97.4 1.4 %shard_map.97 = (bf16[160,1024]{1,0:T(8,128)(2,1)S(1)}, bf16[160,1024]{1,0:T(8,128)(2,1)S(1)}) custom-call(s32[12]{0:T(128)S(1)} %stack.55.table, bf16[1024,2048]{1,0:T(8,128)(2,1)S(1)} %bitcast.16, bf16[160,256]{1,0:T(8,128)(2,1)S(1)} %get-tuple-element.78.refs_0_, bf16[160,256]{1,0:T(8,128)(2,1)S(1)} %collective-permute-done.17.refs_1_, ...), custom_call_target="tpu_custom_call" | custom-call | flops 1 | bytes 1 | tf_op jit(solution)/shard_map/pallas_call | solution.py:388
  98.8 1.6 %collective-permute-start.20 = (bf16[160,1024]{1,0:T(8,128)(2,1)S(1)}, bf16[160,1024]{1,0:T(8,128)(2,1)S(1)}, u32[]{:S(2)}, u32[]{:S(2)}) collective-permute-start(bf16[160,1024]{1,0:T(8,128)(2,1)S(1)} %get-tuple-element.86), channel_id=1, source_target_pairs={{0,1},{1,0},{2,3},{3,2},{4,5},{5,4},{6,7},{7,6},{8,9},{9,8},{10,11... | collective-permute-start | bytes 983048 | tf_op jit(solution)/shard_map/ppermute | solution.py:456
  100.4 3.5 %collective-permute-done.21.corner = bf16[160,1024]{1,0:T(8,128)(2,1)S(1)} collective-permute-done((bf16[160,1024]{1,0:T(8,128)(2,1)S(1)}, bf16[160,1024]{1,0:T(8,128)(2,1)S(1)}, u32[]{:S(2)}, u32[]{:S(2)}) %collective-permute-start.21) | collective-permute-done | bytes 327712 | tf_op jit(solution)/shard_map/ppermute | solution.py:456
  103.9 4.1 %collective-permute-done.20.beside = bf16[160,1024]{1,0:T(8,128)(2,1)S(1)} collective-permute-done((bf16[160,1024]{1,0:T(8,128)(2,1)S(1)}, bf16[160,1024]{1,0:T(8,128)(2,1)S(1)}, u32[]{:S(2)}, u32[]{:S(2)}) %collective-permute-start.20) | collective-permute-done | bytes 327712 | tf_op jit(solution)/shard_map/ppermute | solution.py:456
  108.1 0.0 copy-done.1
  108.1 1.6 %shard_map.99 = bf16[1,2,160,1024]{3,2,1,0:T(8,128)(2,1)} custom-call(s32[12]{0:T(128)S(1)} %stack.55.table, bf16[1,2,160,1024]{3,2,1,0:T(8,128)(2,1)S(1)} %copy-done.1, bf16[160,1024]{1,0:T(8,128)(2,1)S(1)} %get-tuple-element.85.own, bf16[160,1024]{1,0:T(8,128)(2,1)S(1)} %collective-permute-done.20.beside, bf16[160,1024]{1,0:T(8,128)(2,1)S(1)} %get-tuple-element.87.across, ...), custom_call_target="tpu_custom_call" | custom-call | tf_op jit(solution)/shard_map/pallas_call | solution.py:422
Async XLA Ops:
  1.9 19.4 %collective-permute-start.1 = (bf16[2,160,1024]{2,1,0:T(8,128)(2,1)}, bf16[2,160,1024]{2,1,0:T(8,128)(2,1)S(1)}, u32[]{:S(2)}, u32[]{:S(2)}) collective-permute-start(bf16[2,160,1024]{2,1,0:T(8,128)(2,1)} %bitcast.17), channel_id=1, source_target_pairs={{0,16},{1,17},{2,18},{3,19},{4,20},{5,21},{6,22},{7,23},{8,24},{9,... | collective-permute-start | bytes 1966088 | tf_op jit(solution)/shard_map/ppermute | solution.py:462
  4.4 9.6 %collective-permute-start = (bf16[160,1024]{1,0:T(8,128)(2,1)S(1)}, bf16[160,1024]{1,0:T(8,128)(2,1)S(1)}, u32[]{:S(2)}, u32[]{:S(2)}) collective-permute-start(bf16[160,1024]{1,0:T(8,128)(2,1)S(1)} %get-tuple-element.47.qo), channel_id=1, source_target_pairs={{0,1},{1,0},{2,3},{3,2},{4,5},{5,4},{6,7},{7,6},{8,9},{9,8},{10,11... | collective-permute-start | bytes 983048 | tf_op jit(solution)/shard_map/ppermute | solution.py:456
  6.8 11.9 %collective-permute-start.5 = (bf16[160,1024]{1,0:T(8,128)(2,1)S(1)}, bf16[160,1024]{1,0:T(8,128)(2,1)S(1)}, u32[]{:S(2)}, u32[]{:S(2)}) collective-permute-start(bf16[160,1024]{1,0:T(8,128)(2,1)S(1)} %get-tuple-element.63), channel_id=1, source_target_pairs={{0,18},{1,19},{2,16},{3,17},{4,22},{5,23},{6,20},{7,21},{8,26},{9,... | collective-permute-start | bytes 983048 | tf_op jit(solution)/shard_map/ppermute | solution.py:462
  8.9 11.5 %collective-permute-start.3 = (bf16[160,1024]{1,0:T(8,128)(2,1)S(1)}, bf16[160,1024]{1,0:T(8,128)(2,1)S(1)}, u32[]{:S(2)}, u32[]{:S(2)}) collective-permute-start(bf16[160,1024]{1,0:T(8,128)(2,1)S(1)} %get-tuple-element.57), channel_id=1, source_target_pairs={{0,2},{1,3},{2,0},{3,1},{4,6},{5,7},{6,4},{7,5},{8,10},{9,11},{10,... | collective-permute-start | bytes 983048 | tf_op jit(solution)/shard_map/ppermute | solution.py:456
  9.6 11.7 %collective-permute-start.2 = (bf16[160,1024]{1,0:T(8,128)(2,1)S(1)}, bf16[160,1024]{1,0:T(8,128)(2,1)S(1)}, u32[]{:S(2)}, u32[]{:S(2)}) collective-permute-start(bf16[160,1024]{1,0:T(8,128)(2,1)S(1)} %get-tuple-element.49), channel_id=1, source_target_pairs={{0,17},{1,16},{2,19},{3,18},{4,21},{5,20},{6,23},{7,22},{8,25},{9,... | collective-permute-start | bytes 983048 | tf_op jit(solution)/shard_map/ppermute | solution.py:462
  20.3 10.3 %collective-permute-start.4 = (bf16[160,1024]{1,0:T(8,128)(2,1)S(1)}, bf16[160,1024]{1,0:T(8,128)(2,1)S(1)}, u32[]{:S(2)}, u32[]{:S(2)}) collective-permute-start(bf16[160,1024]{1,0:T(8,128)(2,1)S(1)} %collective-permute-done.3.qo), channel_id=1, source_target_pairs={{0,1},{1,0},{2,3},{3,2},{4,5},{5,4},{6,7},{7,6},{8,9},{9,8},{10,11... | collective-permute-start | bytes 983048 | tf_op jit(solution)/shard_map/ppermute | solution.py:456
  20.6 10.0 %collective-permute-start.6 = (bf16[160,1024]{1,0:T(8,128)(2,1)S(1)}, bf16[160,1024]{1,0:T(8,128)(2,1)S(1)}, u32[]{:S(2)}, u32[]{:S(2)}) collective-permute-start(bf16[160,1024]{1,0:T(8,128)(2,1)S(1)} %collective-permute-done.5.ko), channel_id=1, source_target_pairs={{16,17},{17,16},{18,19},{19,18},{20,21},{21,20},{22,23},{23,22},{2... | collective-permute-start | bytes 983048 | tf_op jit(solution)/shard_map/ppermute | solution.py:456
  25.3 16.4 %collective-permute-start.7 = (bf16[160,768]{1,0:T(8,128)(2,1)S(1)}, bf16[160,768]{1,0:T(8,128)(2,1)S(1)}, u32[]{:S(2)}, u32[]{:S(2)}) collective-permute-start(bf16[160,768]{1,0:T(8,128)(2,1)S(1)} %get-tuple-element.58), channel_id=1, source_target_pairs={{0,4},{1,5},{2,6},{3,7},{4,0},{5,1},{6,2},{7,3},{8,12},{9,13},{10,... | collective-permute-start | bytes 737288 | tf_op jit(solution)/shard_map/ppermute | solution.py:456
  27.1 30.9 %collective-permute-start.11 = (bf16[160,768]{1,0:T(8,128)(2,1)S(1)}, bf16[160,768]{1,0:T(8,128)(2,1)S(1)}, u32[]{:S(2)}, u32[]{:S(2)}) collective-permute-start(bf16[160,768]{1,0:T(8,128)(2,1)S(1)} %get-tuple-element.59), channel_id=1, source_target_pairs={{0,8},{1,9},{2,10},{3,11},{4,12},{5,13},{6,14},{7,15},{8,0},{9,1},... | collective-permute-start | bytes 737288 | tf_op jit(solution)/shard_map/ppermute | solution.py:456
  29.7 28.3 %collective-permute-start.12 = (bf16[160,768]{1,0:T(8,128)(2,1)S(1)}, bf16[160,768]{1,0:T(8,128)(2,1)S(1)}, u32[]{:S(2)}, u32[]{:S(2)}) collective-permute-start(bf16[160,768]{1,0:T(8,128)(2,1)S(1)} %get-tuple-element.60), channel_id=1, source_target_pairs={{0,12},{1,13},{2,14},{3,15},{4,8},{5,9},{6,10},{7,11},{8,4},{9,5},... | collective-permute-start | bytes 737288 | tf_op jit(solution)/shard_map/ppermute | solution.py:456
  29.7 12.2 %copy-start.2 = (s32[1,2,2]{2,1,0:T(2,128)S(1)}, s32[1,2,2]{2,1,0:T(2,128)}, u32[]{:S(2)}) copy-start(s32[1,2,2]{2,1,0:T(2,128)} %param.17) | copy-start | bytes 52
  37.8 30.7 %collective-permute-start.9 = (bf16[160,768]{1,0:T(8,128)(2,1)S(1)}, bf16[160,768]{1,0:T(8,128)(2,1)S(1)}, u32[]{:S(2)}, u32[]{:S(2)}) collective-permute-start(bf16[160,768]{1,0:T(8,128)(2,1)S(1)} %get-tuple-element.68), channel_id=1, source_target_pairs={{0,8},{1,9},{2,10},{3,11},{4,12},{5,13},{6,14},{7,15},{8,0},{9,1},... | collective-permute-start | bytes 737288 | tf_op jit(solution)/shard_map/ppermute | solution.py:456
  40.3 28.1 %collective-permute-start.10 = (bf16[160,768]{1,0:T(8,128)(2,1)S(1)}, bf16[160,768]{1,0:T(8,128)(2,1)S(1)}, u32[]{:S(2)}, u32[]{:S(2)}) collective-permute-start(bf16[160,768]{1,0:T(8,128)(2,1)S(1)} %get-tuple-element.69), channel_id=1, source_target_pairs={{0,12},{1,13},{2,14},{3,15},{4,8},{5,9},{6,10},{7,11},{8,4},{9,5},... | collective-permute-start | bytes 737288 | tf_op jit(solution)/shard_map/ppermute | solution.py:456
  41.7 26.8 %collective-permute-start.8 = (bf16[160,768]{1,0:T(8,128)(2,1)S(1)}, bf16[160,768]{1,0:T(8,128)(2,1)S(1)}, u32[]{:S(2)}, u32[]{:S(2)}) collective-permute-start(bf16[160,768]{1,0:T(8,128)(2,1)S(1)} %get-tuple-element.67), channel_id=1, source_target_pairs={{0,4},{1,5},{2,6},{3,7},{4,0},{5,1},{6,2},{7,3},{8,12},{9,13},{10,... | collective-permute-start | bytes 737288 | tf_op jit(solution)/shard_map/ppermute | solution.py:456
  42.0 50.5 %copy-start = (bf16[1,1024,2048]{2,1,0:T(8,128)(2,1)S(1)}, bf16[1,1024,2048]{2,1,0:T(8,128)(2,1)}, u32[]{:S(2)}) copy-start(bf16[1,1024,2048]{2,1,0:T(8,128)(2,1)} %param.14) | copy-start | bytes 12582916
  73.7 14.3 %collective-permute-start.13 = (bf16[160,256]{1,0:T(8,128)(2,1)S(1)}, bf16[160,256]{1,0:T(8,128)(2,1)S(1)}, u32[]{:S(2)}, u32[]{:S(2)}) collective-permute-start(bf16[160,256]{1,0:T(8,128)(2,1)S(1)} %get-tuple-element.70), channel_id=1, source_target_pairs={{0,2},{1,3},{2,0},{3,1},{4,6},{5,7},{6,4},{7,5},{8,10},{9,11},{10,... | collective-permute-start | bytes 245768 | tf_op jit(solution)/shard_map/ppermute | solution.py:456
  75.2 12.8 %collective-permute-start.14 = (bf16[160,256]{1,0:T(8,128)(2,1)S(1)}, bf16[160,256]{1,0:T(8,128)(2,1)S(1)}, u32[]{:S(2)}, u32[]{:S(2)}) collective-permute-start(bf16[160,256]{1,0:T(8,128)(2,1)S(1)} %get-tuple-element.71), channel_id=1, source_target_pairs={{0,6},{1,7},{2,4},{3,5},{4,2},{5,3},{6,0},{7,1},{8,14},{9,15},{10,... | collective-permute-start | bytes 245768 | tf_op jit(solution)/shard_map/ppermute | solution.py:456
  79.3 8.7 %collective-permute-start.15 = (bf16[160,256]{1,0:T(8,128)(2,1)S(1)}, bf16[160,256]{1,0:T(8,128)(2,1)S(1)}, u32[]{:S(2)}, u32[]{:S(2)}) collective-permute-start(bf16[160,256]{1,0:T(8,128)(2,1)S(1)} %get-tuple-element.72), channel_id=1, source_target_pairs={{0,10},{1,11},{2,8},{3,9},{4,14},{5,15},{6,12},{7,13},{8,2},{9,3},... | collective-permute-start | bytes 245768 | tf_op jit(solution)/shard_map/ppermute | solution.py:456
  80.4 7.6 %collective-permute-start.16 = (bf16[160,256]{1,0:T(8,128)(2,1)S(1)}, bf16[160,256]{1,0:T(8,128)(2,1)S(1)}, u32[]{:S(2)}, u32[]{:S(2)}) collective-permute-start(bf16[160,256]{1,0:T(8,128)(2,1)S(1)} %get-tuple-element.73), channel_id=1, source_target_pairs={{0,14},{1,15},{2,12},{3,13},{4,10},{5,11},{6,8},{7,9},{8,6},{9,7},... | collective-permute-start | bytes 245768 | tf_op jit(solution)/shard_map/ppermute | solution.py:456
  88.0 7.5 %collective-permute-start.17 = (bf16[160,256]{1,0:T(8,128)(2,1)S(1)}, bf16[160,256]{1,0:T(8,128)(2,1)S(1)}, u32[]{:S(2)}, u32[]{:S(2)}) collective-permute-start(bf16[160,256]{1,0:T(8,128)(2,1)S(1)} %get-tuple-element.80), channel_id=1, source_target_pairs={{0,4},{1,5},{2,6},{3,7},{4,0},{5,1},{6,2},{7,3},{8,12},{9,13},{10,... | collective-permute-start | bytes 245768 | tf_op jit(solution)/shard_map/ppermute | solution.py:456
  89.4 8.0 %collective-permute-start.18 = (bf16[160,256]{1,0:T(8,128)(2,1)S(1)}, bf16[160,256]{1,0:T(8,128)(2,1)S(1)}, u32[]{:S(2)}, u32[]{:S(2)}) collective-permute-start(bf16[160,256]{1,0:T(8,128)(2,1)S(1)} %get-tuple-element.82), channel_id=1, source_target_pairs={{0,8},{1,9},{2,10},{3,11},{4,12},{5,13},{6,14},{7,15},{8,0},{9,1},... | collective-permute-start | bytes 245768 | tf_op jit(solution)/shard_map/ppermute | solution.py:456
  91.0 6.4 %collective-permute-start.19 = (bf16[160,256]{1,0:T(8,128)(2,1)S(1)}, bf16[160,256]{1,0:T(8,128)(2,1)S(1)}, u32[]{:S(2)}, u32[]{:S(2)}) collective-permute-start(bf16[160,256]{1,0:T(8,128)(2,1)S(1)} %get-tuple-element.84), channel_id=1, source_target_pairs={{0,12},{1,13},{2,14},{3,15},{4,8},{5,9},{6,10},{7,11},{8,4},{9,5},... | collective-permute-start | bytes 245768 | tf_op jit(solution)/shard_map/ppermute | solution.py:456
  92.5 15.6 %copy-start.1 = (bf16[1,2,160,1024]{3,2,1,0:T(8,128)(2,1)S(1)}, bf16[1,2,160,1024]{3,2,1,0:T(8,128)(2,1)}, u32[]{:S(2)}) copy-start(bf16[1,2,160,1024]{3,2,1,0:T(8,128)(2,1)} %hidden.3) | copy-start | bytes 1966084
  93.9 10.0 %collective-permute-start.21 = (bf16[160,1024]{1,0:T(8,128)(2,1)S(1)}, bf16[160,1024]{1,0:T(8,128)(2,1)S(1)}, u32[]{:S(2)}, u32[]{:S(2)}) collective-permute-start(bf16[160,1024]{1,0:T(8,128)(2,1)S(1)} %get-tuple-element.88), channel_id=1, source_target_pairs={{0,1},{1,0},{2,3},{3,2},{4,5},{5,4},{6,7},{7,6},{8,9},{9,8},{10,11... | collective-permute-start | bytes 983048 | tf_op jit(solution)/shard_map/ppermute | solution.py:456
  98.8 9.2 %collective-permute-start.20 = (bf16[160,1024]{1,0:T(8,128)(2,1)S(1)}, bf16[160,1024]{1,0:T(8,128)(2,1)S(1)}, u32[]{:S(2)}, u32[]{:S(2)}) collective-permute-start(bf16[160,1024]{1,0:T(8,128)(2,1)S(1)} %get-tuple-element.86), channel_id=1, source_target_pairs={{0,1},{1,0},{2,3},{3,2},{4,5},{5,4},{6,7},{7,6},{8,9},{9,8},{10,11... | collective-permute-start | bytes 983048 | tf_op jit(solution)/shard_map/ppermute | solution.py:456

commit v4 on v3

v4 whole, which is shorter than its diff:
```python
import functools

import jax
import jax.numpy as jnp
from jax import lax
from jax.experimental import pallas as pl
from jax.experimental.pallas import tpu as pltpu
from jax.sharding import PartitionSpec as P

DH = 64
LANES = 128
SCALE = 0.25 * 1.4426950408889634
MIB = 1024 * 1024
SMALL = pl.CostEstimate(flops=1, bytes_accessed=1, transcendentals=0)
IN_VMEM = pl.BlockSpec(memory_space=pltpu.VMEM)


def passed_along(value, axis, steps):
    count = lax.axis_size(axis)
    leading, last = (max(0, -steps), min(count, count - steps))
    return lax.ppermute(value, axis, [(source, source + steps) for source in range(leading, last)])


def normalize(values, gain_row):
    widened = values.astype(jnp.float32)
    square = jnp.mean(widened * widened, axis=-1, keepdims=True)
    return (widened * lax.rsqrt(square + 1e-06) * gain_row).astype(jnp.bfloat16)


def gathered_body(hidden, memory, w_query, w_key, w_value, w_out, norm_gain, final_gain, lengths):
    encoder_side = lax.axis_index("segment") == 0
    own_part = hidden[0]
    arrived = passed_along(memory[0], "segment", 1)
    source_part = jnp.where(encoder_side, own_part, arrived)
    query_rows, source_rows = (
        lax.all_gather(own_part, "mp", axis=2, tiled=True),
        lax.all_gather(source_part, "mp", axis=2, tiled=True),
    )
    batch = own_part.shape[0]
    row_count = own_part.shape[1]
    width = query_rows.shape[2]
    key_gain = jnp.where(encoder_side, norm_gain[0], final_gain)
    query_in = normalize(query_rows.reshape(batch * row_count, width), norm_gain[0])
    key_in = normalize(source_rows.reshape(batch * row_count, width), key_gain)
    head_cols = w_query.shape[2]
    local_heads = head_cols // DH
    queries = jnp.dot(query_in, w_query[0], preferred_element_type=jnp.float32).astype(jnp.bfloat16)
    keys = jnp.dot(key_in, w_key[0], preferred_element_type=jnp.float32).astype(jnp.bfloat16)
    values = jnp.dot(key_in, w_value[0], preferred_element_type=jnp.float32).astype(jnp.bfloat16)
    keys = keys.reshape(batch, row_count, head_cols)
    values = values.reshape(batch, row_count, head_cols)
    query_length = lengths[0, :, 0]
    key_length = lengths[0, :, 1]
    split_queries = queries.reshape(batch, row_count, local_heads, DH)
    key_piece = lax.all_gather(keys, "seq", axis=1, tiled=True)
    value_piece = lax.all_gather(values, "seq", axis=1, tiled=True)
    key_count = key_piece.shape[1]
    scores = (
        jnp.einsum(
            "bqhd,bkhd->bqhk",
            split_queries,
            key_piece.reshape(batch, key_count, local_heads, DH),
            preferred_element_type=jnp.float32,
        )
        * 0.25
    )
    visible = jnp.arange(key_count)[None, :] < key_length[:, None]
    mask = visible[:, None, None, :]
    scores = jnp.where(mask, scores, -1e30)
    largest = jnp.max(scores, axis=-1)
    exponent = jnp.where(mask, jnp.exp(scores - largest[..., None]), 0.0)
    totals = jnp.sum(exponent, axis=-1)
    weighted = jnp.einsum(
        "bqhk,bkhd->bqhd",
        exponent.astype(jnp.bfloat16),
        value_piece.reshape(batch, key_count, local_heads, DH),
        preferred_element_type=jnp.float32,
    )
    context = weighted / totals[..., None]
    positions = lax.axis_index("seq") * row_count + jnp.arange(row_count)
    live_rows = positions[None, :] < query_length[:, None]
    context = jnp.where(live_rows[:, :, None, None], context, 0.0)
    context = context.astype(jnp.bfloat16).reshape(batch * row_count, head_cols)
    partial_value = jnp.dot(context, w_out[0], preferred_element_type=jnp.float32)
    branch = lax.psum_scatter(
        partial_value.astype(jnp.bfloat16), "mp", scatter_dimension=1, tiled=True
    ).astype(jnp.float32)
    branch = branch.reshape(batch, row_count, branch.shape[1])
    return (own_part.astype(jnp.float32) + branch).astype(jnp.bfloat16)[None]


HEAD, SIDE, INNER, ENC = 0, 1, 2, 3
BLOCK = 4


def in_hbm(array):
    return pltpu.with_memory_space_constraint(array, pltpu.HBM)


def split_kernel(table, hidden, memory, own, away, sems):
    inner = table[INNER]

    def copied(array):
        copies = [
            pltpu.make_async_copy(array.at[0, inner], own, sems.at[0]),
            pltpu.make_async_copy(array.at[0, 1 - inner], away, sems.at[1]),
        ]
        for copy in copies:
            copy.start()
        for copy in copies:
            copy.wait()

    if memory is None:
        copied(hidden)
    else:
        pl.when(table[ENC] == 1)(lambda: copied(hidden))
        pl.when(table[ENC] == 0)(lambda: copied(memory))


def split(table, hidden, memory=None):
    arrays = [hidden] if memory is None else [hidden, memory]

    def kernel(table, hidden, *rest):
        split_kernel(table, hidden, *([None] if memory is None else []), *rest)

    return pl.pallas_call(
        kernel,
        out_shape=[jax.ShapeDtypeStruct(hidden.shape[2:], jnp.bfloat16)] * 2,
        in_specs=[pl.BlockSpec(memory_space=pltpu.SMEM)] + [pl.BlockSpec(memory_space=pltpu.HBM)] * len(arrays),
        out_specs=[IN_VMEM] * 2,
        scratch_shapes=[pltpu.SemaphoreType.DMA((2,))],
        compiler_params=pltpu.CompilerParams(vmem_limit_bytes=4 * MIB),
        cost_estimate=SMALL,
    )(table, *[in_hbm(array) for array in arrays])


def mark(array):
    def kernel(array, out):
        out[...] = jnp.zeros(out.shape, out.dtype)

    return pl.pallas_call(
        kernel,
        out_shape=jax.ShapeDtypeStruct((8, LANES), jnp.float32),
        in_specs=[pl.BlockSpec(memory_space=pl.ANY)],
        out_specs=IN_VMEM,
        compiler_params=pltpu.CompilerParams(vmem_limit_bytes=MIB),
        cost_estimate=pl.CostEstimate(flops=0, bytes_accessed=8 * MIB, transcendentals=0),
    )(array)


def times_gain(values, gains, side, into):
    half = values.shape[1]
    wide = values.astype(jnp.float32)
    into[...] = (wide * gains[:, pl.ds(pl.multiple_of(side * half, half), half)]).astype(jnp.bfloat16)
    return jnp.sum(wide * wide, axis=-1, keepdims=True)


def row_factor(total, features):
    return lax.rsqrt(total / features + 1e-06)


def project_kernel(parts, count, queried, table, *refs):
    size = 4 if queried else 2
    rest = refs[size:]
    (gain, last_gain), weights, rest = rest[:2], rest[2 : 2 + size // 2 + 1], rest[2 + size // 2 + 1 :]
    outs, (xk, xq, fk, fq, held, sems) = rest[:count], rest[count:]
    side = table[SIDE]
    rows, half = refs[0].shape
    width = held.shape[2] // count
    copies = []
    piece = 2 * half // parts
    for n, weight in enumerate(weights):
        for m in range(parts):
            here = pl.ds(m * piece, piece)
            copies.append(pltpu.make_async_copy(weight.at[0, here], held.at[n, here], sems.at[n, m]))
    ahead = len(copies)
    for copy in copies[:ahead]:
        copy.start()

    def fill(own, other, gains, x, f):
        total = times_gain(own, gains, side, x.at[0]) + times_gain(other, gains, 1 - side, x.at[1])
        f[...] = jnp.broadcast_to(row_factor(total, 2 * half), (rows, LANES))

    if queried:
        qo, qn, ko, kn = refs[:4]
        fill(qo[...], qn[...], gain, xq, fq)

        @pl.when(table[ENC] == 1)
        def _():
            xk[...] = xq[...]
            fk[...] = fq[...]

    else:
        ko, kn = refs[:2]

        @pl.when(table[ENC] == 1)
        def _():
            fill(ko[...], kn[...], gain, xk, fk)

    @pl.when(table[ENC] == 0)
    def _():
        fill(ko[...], kn[...], last_gain, xk, fk)

    def part(s):
        return pl.ds(pl.multiple_of(s * half, half), half)

    for n in range(len(weights)):
        for m in range(n * parts, (n + 1) * parts):
            copies[m].wait()
            if m + ahead < len(copies):
                copies[m + ahead].start()
        x, f = (xq, fq) if n == 2 else (xk, fk)
        scale = f[:, :1] * SCALE if n == 2 else f[:, :1]
        for turn in range(count - 1, -1, -1):
            columns = pl.ds(pl.multiple_of((table[HEAD] ^ turn) * width, width), width)
            total = jnp.dot(x[0], held[n, part(side), columns], preferred_element_type=jnp.float32)
            total += jnp.dot(x[1], held[n, part(1 - side), columns], preferred_element_type=jnp.float32)
            outs[turn][:, n * width : (n + 1) * width] = (total * scale).astype(jnp.bfloat16)


def project(table, arrays, gains, weights, count, parts=1):
    rows, half = arrays[0].shape
    columns = weights[0].shape[2]
    queried = len(arrays) == 4
    weights = weights[: 3 if queried else 2]
    width = len(weights) * columns // count
    return pl.pallas_call(
        functools.partial(project_kernel, parts, count, queried),
        out_shape=[jax.ShapeDtypeStruct((rows, width), jnp.bfloat16)] * count,
        grid_spec=pltpu.PrefetchScalarGridSpec(
            num_scalar_prefetch=1,
            grid=(1,),
            in_specs=[IN_VMEM] * (len(arrays) + 2) + [pl.BlockSpec(memory_space=pltpu.HBM)] * len(weights),
            out_specs=[IN_VMEM] * count,
            scratch_shapes=[pltpu.VMEM((2, rows, half), jnp.bfloat16)] * 2
            + [pltpu.VMEM((rows, LANES), jnp.float32)] * 2
            + [
                pltpu.VMEM((len(weights), 2 * half, columns), jnp.bfloat16),
                pltpu.SemaphoreType.DMA((len(weights), parts)),
            ],
        ),
        compiler_params=pltpu.CompilerParams(vmem_limit_bytes=24 * MIB),
        cost_estimate=SMALL,
    )(table, *arrays, *gains, *[in_hbm(w) for w in weights])


def attend_kernel(chosen, tile, blocks, table, lengths, *refs):
    arrays, outs, (qs, ks, vs, contexts) = refs[:blocks], refs[blocks:-4], refs[-4:]
    rows, width = outs[0].shape
    pairs = width // LANES
    query_length = lengths[2 * table[INNER]]
    key_length = lengths[2 * table[INNER] + 1]
    lane = lax.broadcasted_iota(jnp.int32, (rows, LANES), 1)
    row = lax.broadcasted_iota(jnp.int32, (rows, LANES), 0)
    low = lane < DH
    zero = jnp.zeros((rows, LANES), jnp.bfloat16)
    one = jnp.ones((rows, LANES), jnp.bfloat16)
    unit = jnp.where(lane == 0, one, zero)

    def lanes(block):
        return slice(block * LANES, (block + 1) * LANES)

    for j in range(blocks):
        here = pl.ds(j * rows, rows)
        hides = jnp.logical_and(lane == 0, row + table[BLOCK + j] >= key_length)
        bias = jnp.where(hides, -1e30, 0.0).astype(jnp.bfloat16)
        for pair in range(pairs):
            key = arrays[j][:, lanes(pair)]
            value = arrays[j][:, lanes(pairs + pair)]
            ks[pair, 0, here, :LANES] = jnp.where(low, key, zero)
            ks[pair, 1, here, :LANES] = jnp.where(low, zero, key)
            ks[pair, 0, here, LANES:] = bias
            ks[pair, 1, here, LANES:] = bias
            vs[pair, 0, here, :] = jnp.where(low, value, one)
            vs[pair, 1, here, :] = jnp.where(low, one, value)
    for i, j in enumerate(chosen):
        here = pl.ds(i * rows, rows)
        for pair in range(pairs):
            qs[pair, here, :LANES] = arrays[j][:, lanes(2 * pairs + pair)]
            qs[pair, here, LANES:] = unit

    low = lax.broadcasted_iota(jnp.int32, (tile, LANES), 1) < DH
    for pair in range(pairs):
        for t in range(len(chosen) * rows // tile):
            here = pl.ds(t * tile, tile)
            sums = []
            for head in range(2):
                scores = lax.dot_general(
                    qs[pair, here, :], ks[pair, head], (((1,), (1,)), ((), ())), preferred_element_type=jnp.float32
                )
                largest = jnp.max(scores, axis=-1, keepdims=True)
                weights = jnp.exp2(scores - largest).astype(jnp.bfloat16)
                sums.append(jnp.dot(weights, vs[pair, head], preferred_element_type=jnp.float32))
            weighted = jnp.where(low, sums[0], sums[1])
            totals = jnp.where(low, pltpu.roll(sums[0], DH, 1), pltpu.roll(sums[1], DH, 1))
            contexts[here, lanes(pair)] = (weighted / totals).astype(jnp.bfloat16)

    for i, j in enumerate(chosen):
        live = row + table[BLOCK + j] < query_length
        for pair in range(pairs):
            outs[i][:, lanes(pair)] = jnp.where(live, contexts[pl.ds(i * rows, rows), lanes(pair)], zero)


def attend(table, lengths, arrays, chosen, width):
    rows = arrays[0].shape[0]
    total = len(arrays) * rows
    size = len(chosen) * rows
    pairs = width // LANES
    return pl.pallas_call(
        functools.partial(attend_kernel, chosen, size, len(arrays)),
        out_shape=[jax.ShapeDtypeStruct((rows, width), jnp.bfloat16)] * len(chosen),
        grid_spec=pltpu.PrefetchScalarGridSpec(
            num_scalar_prefetch=2,
            grid=(1,),
            in_specs=[IN_VMEM] * len(arrays),
            out_specs=[IN_VMEM] * len(chosen),
            scratch_shapes=[
                pltpu.VMEM((pairs, size, 2 * LANES), jnp.bfloat16),
                pltpu.VMEM((pairs, 2, total, 2 * LANES), jnp.bfloat16),
                pltpu.VMEM((pairs, 2, total, LANES), jnp.bfloat16),
                pltpu.VMEM((size, width), jnp.bfloat16),
            ],
        ),
        compiler_params=pltpu.CompilerParams(vmem_limit_bytes=32 * MIB),
        cost_estimate=SMALL,
    )(table, lengths, *arrays)


def output_kernel(count, table, w, *refs):
    pieces, outs, x = refs[:count], refs[count : count + 2], refs[-1]
    width = pieces[0].shape[1]
    half = outs[0].shape[1]
    for turn in range(count):
        place = pl.multiple_of((table[HEAD] ^ turn) * width, width)
        x[:, pl.ds(place, width)] = pieces[turn][...]
    for i in range(2):
        columns = pl.ds(pl.multiple_of((1 - (table[SIDE] ^ i)) * half, half), half)
        outs[i][...] = jnp.dot(x[...], w[:, columns], preferred_element_type=jnp.float32).astype(jnp.bfloat16)


def output_parts(table, pieces, w_out):
    rows, width = pieces[0].shape
    depth, half = w_out.shape[0], w_out.shape[1] // 2
    return pl.pallas_call(
        functools.partial(output_kernel, len(pieces)),
        out_shape=[jax.ShapeDtypeStruct((rows, half), jnp.bfloat16)] * 2,
        grid_spec=pltpu.PrefetchScalarGridSpec(
            num_scalar_prefetch=1,
            grid=(1,),
            in_specs=[IN_VMEM] * (1 + len(pieces)),
            out_specs=[IN_VMEM] * 2,
            scratch_shapes=[pltpu.VMEM((rows, depth), jnp.bfloat16)],
        ),
        compiler_params=pltpu.CompilerParams(vmem_limit_bytes=16 * MIB),
        cost_estimate=SMALL,
    )(table, w_out, *pieces)


def add_kernel(table, hidden, own, beside, across, corner, out):
    def total(a, b):
        out[0, 0] = (
            hidden[0, 0].astype(jnp.float32) + (a[...].astype(jnp.float32) + b[...].astype(jnp.float32))
        ).astype(jnp.bfloat16)

    @pl.when(pl.program_id(0) == 0)
    def _():
        total(own, beside)

    @pl.when(pl.program_id(0) == 1)
    def _():
        total(across, corner)


def add_all(table, hidden, own, beside, across, corner):
    rows, half = own.shape
    block = pl.BlockSpec((1, 1, rows, half), lambda i, table: (0, table[INNER] ^ i, 0, 0))
    part = pl.BlockSpec((rows, half), lambda i, table: (0, 0))
    return pl.pallas_call(
        add_kernel,
        out_shape=jax.ShapeDtypeStruct(hidden.shape, jnp.bfloat16),
        grid_spec=pltpu.PrefetchScalarGridSpec(
            num_scalar_prefetch=1,
            grid=(2,),
            in_specs=[block, part, part, part, part],
            out_specs=block,
        ),
        compiler_params=pltpu.CompilerParams(vmem_limit_bytes=16 * MIB),
    )(table, hidden, own, beside, across, corner)


def body(hidden, memory, w_query, w_key, w_value, w_out, norm_gain, final_gain, lengths):
    seq, mp = lax.axis_size("seq"), lax.axis_size("mp")
    width = w_query.shape[2] // 2
    rows = hidden.shape[2]

    place, side = lax.axis_index("seq"), lax.axis_index("mp")
    encoder = (lax.axis_index("segment") == 0).astype(jnp.int32)
    chunks = range(0, seq, 2)
    starts = [(place ^ (chunk + turn)) * rows for chunk in chunks for turn in range(2)]
    table = jnp.stack([place % 2, side, place // 2 % 2, encoder] + starts).astype(jnp.int32)

    def moved(value, swap_seq, swap_mp, segments=(0, 1)):
        pairs = [
            ((g * seq + s) * mp + m, (g * seq + (s ^ swap_seq)) * mp + (m ^ swap_mp))
            for g in segments
            for s in range(seq)
            for m in range(mp)
        ]
        return lax.ppermute(value, ("segment", "seq", "mp"), pairs)

    def after(value, *others):
        return lax.optimization_barrier((value, *others))[0]

    gains = (in_hbm(norm_gain), in_hbm(final_gain.reshape(1, -1)))
    weights = (w_key, w_value, w_query)

    arrived = passed_along(memory[0], "segment", 1)
    hidden_own, hidden_away = split(table, hidden)
    query = {0: hidden_own}
    query_other = {0: moved(hidden_own, 0, 1)}
    query[2] = moved(hidden_away, 2, 0)
    source_own, source_away = split(table, hidden, after(arrived, hidden_own)[None])
    source = {0: source_own}
    source_other = {0: moved(source_own, 0, 1, (1,))}
    source[2] = moved(source_away, 2, 0, (1,))
    if seq > 4:
        source[4] = moved(source_own, 4, 0)
    query_other[2] = moved(query[2], 0, 1)
    source_other[2] = moved(source[2], 0, 1, (1,))

    def projected(chunk, *others):
        parts = [source[chunk], source_other[chunk]]
        if chunk < 4:
            parts = [query[chunk], query_other[chunk]] + parts
        parts[0] = after(parts[0], *others)
        kept, sent = project(table, parts, gains, weights, 2)
        return kept, moved(sent, 1, 0)

    done = {0: projected(0, query[2], source[2])}
    before = done[0][0]
    if seq > 4:
        source[4] = after(source[4], before)
        source_other[4] = moved(source[4], 0, 1)
        before = [before, mark(source[4])]
    last = before
    for chunk in chunks[3:]:
        source[chunk] = moved(after(source_away if chunk & 2 else source_own, last), chunk, 0)
        last = source[chunk]
    done[2] = projected(2, before)
    before = done[2][0]
    for chunk in chunks[2:]:
        if chunk > 4:
            source_other[chunk] = moved(after(source[chunk], done[2][0]), 0, 1)
        done[chunk] = projected(chunk, before, done[chunk - 4][1])
        before = done[chunk][0]
    arrays = [array for chunk in chunks for array in done[chunk]]

    lengths = lengths.reshape(-1)
    context = attend(table, lengths, arrays, (2, 3), width)
    second_context = [moved(context[turn], 2 + turn, 0) for turn in range(2)]
    context = attend(table, lengths, after(arrays, context), (0, 1), width)
    first_context = [context[0], moved(after(context[1], second_context), 1, 0)]
    away, second_own = output_parts(table, second_context, w_out[0])
    second_beside = moved(away, 0, 1)
    away, own = output_parts(table, first_context, w_out[0])
    first_beside = moved(away, 0, 1)
    return add_all(table, hidden, own, first_beside, second_own, second_beside)


def solution(mesh):
    seq, mp = mesh.shape["seq"], mesh.shape["mp"]

    def chosen(*arrays):
        batch, columns = arrays[0].shape[1], arrays[2].shape[2]
        fits = (
            batch == 2
            and mp == 2
            and seq >= 4
            and seq & (seq - 1) == 0
            and (columns // mp) % (2 * LANES) == 0
            and (arrays[0].shape[2] // seq) % 16 == 0
        )
        return jax.shard_map(
            body if fits else gathered_body,
            mesh=mesh,
            in_specs=(
                P("segment", None, "seq", "mp"),
                P("segment", None, "seq", "mp"),
                P("segment", None, "mp"),
                P("segment", None, "mp"),
                P("segment", None, "mp"),
                P("segment", "mp", None),
                P("segment", None),
                P(),
                P("segment", None, None),
            ),
            out_specs=P("segment", None, "seq", "mp"),
            check_vma=False,
        )(*arrays)

    return chosen
```

time: 110 us -> 106 us (0.964)
  Pallas kernels: 32.4 us -> 44.7 us
  waiting for transfers between devices: 41.7 us -> 32.6 us
  starting transfers between devices: 35.2 us -> 27.3 us
    pallas_call x6 -> x8, Pallas kernels: 27.9 us -> 40.3 us  [the longest x4 26 us: project(): pl.pallas_call(functools.partial(project_kernel, parts, count, queried),...]
    ppermute x19, waiting for transfers between devices: 41.7 us -> 32.6 us  [moved(): return lax.ppermute(value, ('segment', 'seq', 'mp'), pairs)]
    ppermute x19, starting transfers between devices: 29.5 us -> 24.9 us  [moved(): return lax.ppermute(value, ('segment', 'seq', 'mp'), pairs)]
    ppermute x3 -> x1, starting transfers between devices: 5.77 us -> 2.39 us  [passed_along(): lax.ppermute(value, axis, [(source, source + steps) for source in range(l...]
  transfers between devices with their start and end apart: 22 -> 20, of which waited for: 8 -> 10; matrix products, arithmetic and copies ran while one was open for 0% -> 0% of each run, Pallas kernels for 22% -> 36%
where the time goes in v4:
time: 106 us
  Pallas kernels  44.7 us (42%)
  waiting for transfers between devices  32.6 us (31%)
  starting transfers between devices  27.3 us (26%)
    ppermute x19, waiting for transfers between devices, moved(): return lax.ppermute(value, ('segment', 'seq', 'mp'), pairs)  32.6 us
    pallas_call x4, Pallas kernels, project(): pl.pallas_call(functools.partial(project_kernel, parts, count, queried),...  26 us
    ppermute x19, starting transfers between devices, moved(): return lax.ppermute(value, ('segment', 'seq', 'mp'), pairs)  24.9 us
    pallas_call x2, Pallas kernels, attend(): pl.pallas_call(functools.partial(attend_kernel, chosen, size, len(arrays)...  11 us
    pallas_call x2, Pallas kernels, split(): pl.pallas_call(kernel, out_shape=[jax.ShapeDtypeStruct(hidden.shape[2:],...  3.27 us
    pallas_call x2, Pallas kernels, output_parts(): pl.pallas_call(functools.partial(output_kernel, len(pieces)), out_shape=[...  2.82 us
    ppermute x1, starting transfers between devices, passed_along(): lax.ppermute(value, axis, [(source, source + steps) for source in range(l...  2.39 us
  transfers between devices with their start and end apart: 20, of which 10 were waited for; matrix products, arithmetic and copies ran while one was open for 0% of the time, Pallas kernels for 36%

profile of v4, /device:TPU:0, one launch (start us, length us, event | category | flops | bytes accessed | tf_op | source)
XLA Modules:
  0.0 105.8 jit_solution(18308667289995965093)
XLA Ops:
  0.0 2.4 %collective-permute-start.1 = (bf16[2,160,1024]{2,1,0:T(8,128)(2,1)}, bf16[2,160,1024]{2,1,0:T(8,128)(2,1)S(1)}, u32[]{:S(2)}, u32[]{:S(2)}) collective-permute-start(bf16[2,160,1024]{2,1,0:T(8,128)(2,1)} %bitcast.23), channel_id=1, source_target_pairs={{0,16},{1,17},{2,18},{3,19},{4,20},{5,21},{6,22},{7,23},{8,24},{9,... | collective-permute-start | bytes 1966088 | tf_op jit(solution)/shard_map/ppermute | solution.py:21
  2.4 0.1 stack.55.table
  2.5 1.6 %shard_map.91 = (bf16[160,1024]{1,0:T(8,128)(2,1)S(1)}, bf16[160,1024]{1,0:T(8,128)(2,1)S(1)}) custom-call(s32[12]{0:T(128)S(1)} %stack.55.table, bf16[1,2,160,1024]{3,2,1,0:T(8,128)(2,1)} %hidden.5), custom_call_target="tpu_custom_call" | custom-call | flops 1 | bytes 1 | tf_op jit(solution)/shard_map/pallas_call | solution.py:126
  4.2 2.5 %collective-permute-start = (bf16[160,1024]{1,0:T(8,128)(2,1)S(1)}, bf16[160,1024]{1,0:T(8,128)(2,1)S(1)}, u32[]{:S(2)}, u32[]{:S(2)}) collective-permute-start(bf16[160,1024]{1,0:T(8,128)(2,1)S(1)} %get-tuple-element.43), channel_id=1, source_target_pairs={{0,4},{1,5},{2,6},{3,7},{4,0},{5,1},{6,2},{7,3},{8,12},{9,13},{10,... | collective-permute-start | bytes 983048 | tf_op jit(solution)/shard_map/ppermute | solution.py:409
  6.6 0.0 collective-permute-done.1
  6.6 0.0 copy-start.2
  6.7 0.8 copy-done.2
  7.5 1.6 %shard_map.92 = (bf16[160,1024]{1,0:T(8,128)(2,1)S(1)}, bf16[160,1024]{1,0:T(8,128)(2,1)S(1)}) custom-call(s32[12]{0:T(128)S(1)} %stack.55.table, bf16[1,2,160,1024]{3,2,1,0:T(8,128)(2,1)} %hidden.5, bf16[1,2,160,1024]{3,2,1,0:T(8,128)(2,1)} %bitcast.18), custom_call_target="tpu_custom_call" | custom-call | flops 1 | bytes 1 | tf_op jit(solution)/shard_map/pallas_call | solution.py:126
  9.1 0.7 collective-permute-start.2
  9.8 1.6 %collective-permute-start.3 = (bf16[160,1024]{1,0:T(8,128)(2,1)S(1)}, bf16[160,1024]{1,0:T(8,128)(2,1)S(1)}, u32[]{:S(2)}, u32[]{:S(2)}) collective-permute-start(bf16[160,1024]{1,0:T(8,128)(2,1)S(1)} %get-tuple-element.46.refs_0_), channel_id=1, source_target_pairs={{0,1},{1,0},{2,3},{3,2},{4,5},{5,4},{6,7},{7,6},{8,9},{9,8},{10,11... | collective-permute-start | bytes 983048 | tf_op jit(solution)/shard_map/ppermute | solution.py:409
  11.4 0.7 collective-permute-start.4
  12.1 2.7 %collective-permute-start.6 = (bf16[160,1024]{1,0:T(8,128)(2,1)S(1)}, bf16[160,1024]{1,0:T(8,128)(2,1)S(1)}, u32[]{:S(2)}, u32[]{:S(2)}) collective-permute-start(bf16[160,1024]{1,0:T(8,128)(2,1)S(1)} %get-tuple-element.47.refs_2_), channel_id=1, source_target_pairs={{0,8},{1,9},{2,10},{3,11},{4,12},{5,13},{6,14},{7,15},{8,0},{9,1},... | collective-permute-start | bytes 983048 | tf_op jit(solution)/shard_map/ppermute | solution.py:409
  14.7 0.2 collective-permute-done.refs_0_
  15.0 1.8 %collective-permute-start.7 = (bf16[160,1024]{1,0:T(8,128)(2,1)S(1)}, bf16[160,1024]{1,0:T(8,128)(2,1)S(1)}, u32[]{:S(2)}, u32[]{:S(2)}) collective-permute-start(bf16[160,1024]{1,0:T(8,128)(2,1)S(1)} %collective-permute-done.refs_0_), channel_id=1, source_target_pairs={{0,1},{1,0},{2,3},{3,2},{4,5},{5,4},{6,7},{7,6},{8,9},{9,8},{10,11... | collective-permute-start | bytes 983048 | tf_op jit(solution)/shard_map/ppermute | solution.py:409
  16.8 0.0 collective-permute-done.2.refs_2_
  16.8 0.7 collective-permute-start.8
  17.5 2.7 %collective-permute-done.3.refs_1_ = bf16[160,1024]{1,0:T(8,128)(2,1)S(1)} collective-permute-done((bf16[160,1024]{1,0:T(8,128)(2,1)S(1)}, bf16[160,1024]{1,0:T(8,128)(2,1)S(1)}, u32[]{:S(2)}, u32[]{:S(2)}) %collective-permute-start.3) | collective-permute-done | bytes 327712 | tf_op jit(solution)/shard_map/ppermute | solution.py:409
  20.2 0.0 collective-permute-done.4.refs_3_
  20.2 7.0 %shard_map.93 = (bf16[160,1536]{1,0:T(8,128)(2,1)S(1)}, bf16[160,1536]{1,0:T(8,128)(2,1)S(1)}) custom-call(s32[12]{0:T(128)S(1)} %stack.55.table, bf16[160,1024]{1,0:T(8,128)(2,1)S(1)} %get-tuple-element.46.refs_0_, bf16[160,1024]{1,0:T(8,128)(2,1)S(1)} %collective-permute-done.3.refs_1_, bf16[160,1024]{1,0:T(8,128)(2,1)S(1)} %get-tuple-element.47.refs_2_, ...), custom_call_target="tpu_custom_call" | custom-call | flops 1 | bytes 1 | tf_op jit(solution)/shard_map/pallas_call | solution.py:227
  27.2 2.3 %collective-permute-done.6.refs_0_ = bf16[160,1024]{1,0:T(8,128)(2,1)S(1)} collective-permute-done((bf16[160,1024]{1,0:T(8,128)(2,1)S(1)}, bf16[160,1024]{1,0:T(8,128)(2,1)S(1)}, u32[]{:S(2)}, u32[]{:S(2)}) %collective-permute-start.6) | collective-permute-done | bytes 327712 | tf_op jit(solution)/shard_map/ppermute | solution.py:409
  29.4 2.3 %collective-permute-start.12 = (bf16[160,1024]{1,0:T(8,128)(2,1)S(1)}, bf16[160,1024]{1,0:T(8,128)(2,1)S(1)}, u32[]{:S(2)}, u32[]{:S(2)}) collective-permute-start(bf16[160,1024]{1,0:T(8,128)(2,1)S(1)} %get-tuple-element.57), channel_id=1, source_target_pairs={{0,12},{1,13},{2,14},{3,15},{4,8},{5,9},{6,10},{7,11},{8,4},{9,5},... | collective-permute-start | bytes 983048 | tf_op jit(solution)/shard_map/ppermute | solution.py:409
  31.7 1.5 %collective-permute-start.5 = (bf16[160,1536]{1,0:T(8,128)(2,1)S(1)}, bf16[160,1536]{1,0:T(8,128)(2,1)S(1)}, u32[]{:S(2)}, u32[]{:S(2)}) collective-permute-start(bf16[160,1536]{1,0:T(8,128)(2,1)S(1)} %get-tuple-element.49), channel_id=1, source_target_pairs={{0,2},{1,3},{2,0},{3,1},{4,6},{5,7},{6,4},{7,5},{8,10},{9,11},{10,... | collective-permute-start | bytes 1474568 | tf_op jit(solution)/shard_map/ppermute | solution.py:409
  33.2 0.0 collective-permute-done.7.refs_1_
  33.2 0.0 collective-permute-done.8.refs_3_
  33.2 7.0 %shard_map.94 = (bf16[160,1536]{1,0:T(8,128)(2,1)S(1)}, bf16[160,1536]{1,0:T(8,128)(2,1)S(1)}) custom-call(s32[12]{0:T(128)S(1)} %stack.55.table, bf16[160,1024]{1,0:T(8,128)(2,1)S(1)} %collective-permute-done.refs_0_, bf16[160,1024]{1,0:T(8,128)(2,1)S(1)} %collective-permute-done.7.refs_1_, bf16[160,1024]{1,0:T(8,128)(2,1)S(1)} %collective-permute-done.2.refs_2_, ...), custom_call_target="tpu_custom_call" | custom-call | flops 1 | bytes 1 | tf_op jit(solution)/shard_map/pallas_call | solution.py:227
  40.2 0.6 collective-permute-start.9
  40.8 0.0 collective-permute-start.10
  40.8 0.0 collective-permute-done.12.refs_0_
  40.8 2.0 %collective-permute-start.13 = (bf16[160,1024]{1,0:T(8,128)(2,1)S(1)}, bf16[160,1024]{1,0:T(8,128)(2,1)S(1)}, u32[]{:S(2)}, u32[]{:S(2)}) collective-permute-start(bf16[160,1024]{1,0:T(8,128)(2,1)S(1)} %collective-permute-done.12.refs_0_), channel_id=1, source_target_pairs={{0,1},{1,0},{2,3},{3,2},{4,5},{5,4},{6,7},{7,6},{8,9},{9,8},{10,11... | collective-permute-start | bytes 983048 | tf_op jit(solution)/shard_map/ppermute | solution.py:409
  42.8 0.1 collective-permute-done.5.refs_1_
  43.0 6.1 %collective-permute-done.10.refs_1_ = bf16[160,1024]{1,0:T(8,128)(2,1)S(1)} collective-permute-done((bf16[160,1024]{1,0:T(8,128)(2,1)S(1)}, bf16[160,1024]{1,0:T(8,128)(2,1)S(1)}, u32[]{:S(2)}, u32[]{:S(2)}) %collective-permute-start.10) | collective-permute-done | bytes 327712 | tf_op jit(solution)/shard_map/ppermute | solution.py:409
  49.1 6.0 %shard_map.95 = (bf16[160,1024]{1,0:T(8,128)(2,1)S(1)}, bf16[160,1024]{1,0:T(8,128)(2,1)}) custom-call(s32[12]{0:T(128)S(1)} %stack.55.table, bf16[160,1024]{1,0:T(8,128)(2,1)S(1)} %collective-permute-done.6.refs_0_, bf16[160,1024]{1,0:T(8,128)(2,1)S(1)} %collective-permute-done.10.refs_1_, f32[1,2048]{1,0:T(1,128)} %refs_2_.3, f32[1,2048]{1,0:T(1,128)} %bitcast.21, ...), custom_call_target="tpu_custom_call" | custom-call | flops 1 | bytes 1 | tf_op jit(solution)/shard_map/pallas_call | solution.py:227
  55.1 1.5 %collective-permute-start.11 = (bf16[160,1024]{1,0:T(8,128)(2,1)}, bf16[160,1024]{1,0:T(8,128)(2,1)S(1)}, u32[]{:S(2)}, u32[]{:S(2)}) collective-permute-start(bf16[160,1024]{1,0:T(8,128)(2,1)} %get-tuple-element.56), channel_id=1, source_target_pairs={{0,2},{1,3},{2,0},{3,1},{4,6},{5,7},{6,4},{7,5},{8,10},{9,11},{10,... | collective-permute-start | bytes 983048 | tf_op jit(solution)/shard_map/ppermute | solution.py:409
  56.6 0.0 collective-permute-done.9.refs_3_
  56.7 0.0 copy-start.3
  56.7 0.0 collective-permute-done.13.refs_1_
  56.7 6.0 %shard_map.96 = (bf16[160,1024]{1,0:T(8,128)(2,1)S(1)}, bf16[160,1024]{1,0:T(8,128)(2,1)}) custom-call(s32[12]{0:T(128)S(1)} %stack.55.table, bf16[160,1024]{1,0:T(8,128)(2,1)S(1)} %collective-permute-done.12.refs_0_, bf16[160,1024]{1,0:T(8,128)(2,1)S(1)} %collective-permute-done.13.refs_1_, f32[1,2048]{1,0:T(1,128)} %refs_2_.3, f32[1,2048]{1,0:T(1,128)} %bitcast.22, ...), custom_call_target="tpu_custom_call" | custom-call | flops 1 | bytes 1 | tf_op jit(solution)/shard_map/pallas_call | solution.py:227
  62.7 1.0 collective-permute-start.14
  63.7 0.0 copy-done.3
  63.7 0.1 reshape.6.lengths
  63.8 0.0 copy-start
  63.8 0.0 collective-permute-done.11.refs_5_
  63.8 6.3 %collective-permute-done.14.refs_7_ = bf16[160,1024]{1,0:T(8,128)(2,1)S(1)} collective-permute-done((bf16[160,1024]{1,0:T(8,128)(2,1)}, bf16[160,1024]{1,0:T(8,128)(2,1)S(1)}, u32[]{:S(2)}, u32[]{:S(2)}) %collective-permute-start.14) | collective-permute-done | bytes 327712 | tf_op jit(solution)/shard_map/ppermute | solution.py:409
  70.0 5.5 %shard_map.97 = (bf16[160,512]{1,0:T(8,128)(2,1)S(1)}, bf16[160,512]{1,0:T(8,128)(2,1)S(1)}) custom-call(s32[12]{0:T(128)S(1)} %stack.55.table, s32[4]{0:T(128)S(1)} %reshape.6.lengths, bf16[160,1536]{1,0:T(8,128)(2,1)S(1)} %get-tuple-element.64.refs_0_, bf16[160,1536]{1,0:T(8,128)(2,1)S(1)} %collective-permute-done.5.refs_1_, ...), custom_call_target="tpu_custom_call" | custom-call | flops 1 | bytes 1 | tf_op jit(solution)/shard_map/pallas_call | solution.py:309
  75.5 0.1 collective-permute-start.15
  75.6 3.2 %collective-permute-start.16 = (bf16[160,512]{1,0:T(8,128)(2,1)S(1)}, bf16[160,512]{1,0:T(8,128)(2,1)S(1)}, u32[]{:S(2)}, u32[]{:S(2)}) collective-permute-start(bf16[160,512]{1,0:T(8,128)(2,1)S(1)} %get-tuple-element.63), channel_id=1, source_target_pairs={{0,6},{1,7},{2,4},{3,5},{4,2},{5,3},{6,0},{7,1},{8,14},{9,15},{10,... | collective-permute-start | bytes 491528 | tf_op jit(solution)/shard_map/ppermute | solution.py:409
  78.8 5.5 %shard_map.98 = (bf16[160,512]{1,0:T(8,128)(2,1)S(1)}, bf16[160,512]{1,0:T(8,128)(2,1)S(1)}) custom-call(s32[12]{0:T(128)S(1)} %stack.55.table, s32[4]{0:T(128)S(1)} %reshape.6.lengths, bf16[160,1536]{1,0:T(8,128)(2,1)S(1)} %get-tuple-element.64.refs_0_, bf16[160,1536]{1,0:T(8,128)(2,1)S(1)} %collective-permute-done.5.refs_1_, ...), custom_call_target="tpu_custom_call" | custom-call | flops 1 | bytes 1 | tf_op jit(solution)/shard_map/pallas_call | solution.py:309
  84.4 0.0 collective-permute-done.15.refs_0_
  84.4 1.2 %collective-permute-done.16.refs_1_ = bf16[160,512]{1,0:T(8,128)(2,1)S(1)} collective-permute-done((bf16[160,512]{1,0:T(8,128)(2,1)S(1)}, bf16[160,512]{1,0:T(8,128)(2,1)S(1)}, u32[]{:S(2)}, u32[]{:S(2)}) %collective-permute-start.16) | collective-permute-done | bytes 163872 | tf_op jit(solution)/shard_map/ppermute | solution.py:409
  85.6 0.0 collective-permute-start.17
  85.6 0.0 copy-done
  85.6 0.0 copy-start.1
  85.6 1.4 %shard_map.100 = (bf16[160,1024]{1,0:T(8,128)(2,1)S(1)}, bf16[160,1024]{1,0:T(8,128)(2,1)S(1)}) custom-call(s32[12]{0:T(128)S(1)} %stack.55.table, bf16[1024,2048]{1,0:T(8,128)(2,1)S(1)} %bitcast.16, bf16[160,512]{1,0:T(8,128)(2,1)S(1)} %collective-permute-done.15.refs_0_, bf16[160,512]{1,0:T(8,128)(2,1)S(1)} %collective-permute-done.16.refs_1_), custom_call_target="tpu_custom_call" | custom-call | flops 1 | bytes 1 | tf_op jit(solution)/shard_map/pallas_call | solution.py:344
  87.0 1.1 %collective-permute-start.19 = (bf16[160,1024]{1,0:T(8,128)(2,1)S(1)}, bf16[160,1024]{1,0:T(8,128)(2,1)S(1)}, u32[]{:S(2)}, u32[]{:S(2)}) collective-permute-start(bf16[160,1024]{1,0:T(8,128)(2,1)S(1)} %get-tuple-element.78), channel_id=1, source_target_pairs={{0,1},{1,0},{2,3},{3,2},{4,5},{5,4},{6,7},{7,6},{8,9},{9,8},{10,11... | collective-permute-start | bytes 983048 | tf_op jit(solution)/shard_map/ppermute | solution.py:409
  88.1 4.0 %collective-permute-done.17.refs_1_ = bf16[160,512]{1,0:T(8,128)(2,1)S(1)} collective-permute-done((bf16[160,512]{1,0:T(8,128)(2,1)S(1)}, bf16[160,512]{1,0:T(8,128)(2,1)S(1)}, u32[]{:S(2)}, u32[]{:S(2)}) %collective-permute-start.17) | collective-permute-done | bytes 163872 | tf_op jit(solution)/shard_map/ppermute | solution.py:409
  92.1 1.4 %shard_map.99 = (bf16[160,1024]{1,0:T(8,128)(2,1)S(1)}, bf16[160,1024]{1,0:T(8,128)(2,1)S(1)}) custom-call(s32[12]{0:T(128)S(1)} %stack.55.table, bf16[1024,2048]{1,0:T(8,128)(2,1)S(1)} %bitcast.17, bf16[160,512]{1,0:T(8,128)(2,1)S(1)} %get-tuple-element.72.refs_0_, bf16[160,512]{1,0:T(8,128)(2,1)S(1)} %collective-permute-done.17.refs_1_), custom_call_target="tpu_custom_call" | custom-call | flops 1 | bytes 1 | tf_op jit(solution)/shard_map/pallas_call | solution.py:344
  93.5 1.1 %collective-permute-start.18 = (bf16[160,1024]{1,0:T(8,128)(2,1)S(1)}, bf16[160,1024]{1,0:T(8,128)(2,1)S(1)}, u32[]{:S(2)}, u32[]{:S(2)}) collective-permute-start(bf16[160,1024]{1,0:T(8,128)(2,1)S(1)} %get-tuple-element.76), channel_id=1, source_target_pairs={{0,1},{1,0},{2,3},{3,2},{4,5},{5,4},{6,7},{7,6},{8,9},{9,8},{10,11... | collective-permute-start | bytes 983048 | tf_op jit(solution)/shard_map/ppermute | solution.py:409
  94.5 2.5 %collective-permute-done.19.corner = bf16[160,1024]{1,0:T(8,128)(2,1)S(1)} collective-permute-done((bf16[160,1024]{1,0:T(8,128)(2,1)S(1)}, bf16[160,1024]{1,0:T(8,128)(2,1)S(1)}, u32[]{:S(2)}, u32[]{:S(2)}) %collective-permute-start.19) | collective-permute-done | bytes 327712 | tf_op jit(solution)/shard_map/ppermute | solution.py:409
  97.1 7.1 %collective-permute-done.18.beside = bf16[160,1024]{1,0:T(8,128)(2,1)S(1)} collective-permute-done((bf16[160,1024]{1,0:T(8,128)(2,1)S(1)}, bf16[160,1024]{1,0:T(8,128)(2,1)S(1)}, u32[]{:S(2)}, u32[]{:S(2)}) %collective-permute-start.18) | collective-permute-done | bytes 327712 | tf_op jit(solution)/shard_map/ppermute | solution.py:409
  104.2 0.0 copy-done.1
  104.2 1.6 %shard_map.101 = bf16[1,2,160,1024]{3,2,1,0:T(8,128)(2,1)} custom-call(s32[12]{0:T(128)S(1)} %stack.55.table, bf16[1,2,160,1024]{3,2,1,0:T(8,128)(2,1)S(1)} %copy-done.1, bf16[160,1024]{1,0:T(8,128)(2,1)S(1)} %get-tuple-element.75.own, bf16[160,1024]{1,0:T(8,128)(2,1)S(1)} %collective-permute-done.18.beside, bf16[160,1024]{1,0:T(8,128)(2,1)S(1)} %get-tuple-element.77.across, ...), custom_call_target="tpu_custom_call" | custom-call | tf_op jit(solution)/shard_map/pallas_call | solution.py:378
Async XLA Ops:
  0.0 6.6 %collective-permute-start.1 = (bf16[2,160,1024]{2,1,0:T(8,128)(2,1)}, bf16[2,160,1024]{2,1,0:T(8,128)(2,1)S(1)}, u32[]{:S(2)}, u32[]{:S(2)}) collective-permute-start(bf16[2,160,1024]{2,1,0:T(8,128)(2,1)} %bitcast.23), channel_id=1, source_target_pairs={{0,16},{1,17},{2,18},{3,19},{4,20},{5,21},{6,22},{7,23},{8,24},{9,... | collective-permute-start | bytes 1966088 | tf_op jit(solution)/shard_map/ppermute | solution.py:21
  4.2 10.8 %collective-permute-start = (bf16[160,1024]{1,0:T(8,128)(2,1)S(1)}, bf16[160,1024]{1,0:T(8,128)(2,1)S(1)}, u32[]{:S(2)}, u32[]{:S(2)}) collective-permute-start(bf16[160,1024]{1,0:T(8,128)(2,1)S(1)} %get-tuple-element.43), channel_id=1, source_target_pairs={{0,4},{1,5},{2,6},{3,7},{4,0},{5,1},{6,2},{7,3},{8,12},{9,13},{10,... | collective-permute-start | bytes 983048 | tf_op jit(solution)/shard_map/ppermute | solution.py:409
  6.6 0.8 copy-start.2
  9.1 7.7 %collective-permute-start.2 = (bf16[160,1024]{1,0:T(8,128)(2,1)S(1)}, bf16[160,1024]{1,0:T(8,128)(2,1)S(1)}, u32[]{:S(2)}, u32[]{:S(2)}) collective-permute-start(bf16[160,1024]{1,0:T(8,128)(2,1)S(1)} %get-tuple-element.57), channel_id=1, source_target_pairs={{16,20},{17,21},{18,22},{19,23},{20,16},{21,17},{22,18},{23,19},{2... | collective-permute-start | bytes 983048 | tf_op jit(solution)/shard_map/ppermute | solution.py:409
  9.8 10.3 %collective-permute-start.3 = (bf16[160,1024]{1,0:T(8,128)(2,1)S(1)}, bf16[160,1024]{1,0:T(8,128)(2,1)S(1)}, u32[]{:S(2)}, u32[]{:S(2)}) collective-permute-start(bf16[160,1024]{1,0:T(8,128)(2,1)S(1)} %get-tuple-element.46.refs_0_), channel_id=1, source_target_pairs={{0,1},{1,0},{2,3},{3,2},{4,5},{5,4},{6,7},{7,6},{8,9},{9,8},{10,11... | collective-permute-start | bytes 983048 | tf_op jit(solution)/shard_map/ppermute | solution.py:409
  11.4 8.8 %collective-permute-start.4 = (bf16[160,1024]{1,0:T(8,128)(2,1)S(1)}, bf16[160,1024]{1,0:T(8,128)(2,1)S(1)}, u32[]{:S(2)}, u32[]{:S(2)}) collective-permute-start(bf16[160,1024]{1,0:T(8,128)(2,1)S(1)} %get-tuple-element.47.refs_2_), channel_id=1, source_target_pairs={{16,17},{17,16},{18,19},{19,18},{20,21},{21,20},{22,23},{23,22},{2... | collective-permute-start | bytes 983048 | tf_op jit(solution)/shard_map/ppermute | solution.py:409
  12.1 17.4 %collective-permute-start.6 = (bf16[160,1024]{1,0:T(8,128)(2,1)S(1)}, bf16[160,1024]{1,0:T(8,128)(2,1)S(1)}, u32[]{:S(2)}, u32[]{:S(2)}) collective-permute-start(bf16[160,1024]{1,0:T(8,128)(2,1)S(1)} %get-tuple-element.47.refs_2_), channel_id=1, source_target_pairs={{0,8},{1,9},{2,10},{3,11},{4,12},{5,13},{6,14},{7,15},{8,0},{9,1},... | collective-permute-start | bytes 983048 | tf_op jit(solution)/shard_map/ppermute | solution.py:409
  15.0 18.2 %collective-permute-start.7 = (bf16[160,1024]{1,0:T(8,128)(2,1)S(1)}, bf16[160,1024]{1,0:T(8,128)(2,1)S(1)}, u32[]{:S(2)}, u32[]{:S(2)}) collective-permute-start(bf16[160,1024]{1,0:T(8,128)(2,1)S(1)} %collective-permute-done.refs_0_), channel_id=1, source_target_pairs={{0,1},{1,0},{2,3},{3,2},{4,5},{5,4},{6,7},{7,6},{8,9},{9,8},{10,11... | collective-permute-start | bytes 983048 | tf_op jit(solution)/shard_map/ppermute | solution.py:409
  16.8 16.4 %collective-permute-start.8 = (bf16[160,1024]{1,0:T(8,128)(2,1)S(1)}, bf16[160,1024]{1,0:T(8,128)(2,1)S(1)}, u32[]{:S(2)}, u32[]{:S(2)}) collective-permute-start(bf16[160,1024]{1,0:T(8,128)(2,1)S(1)} %collective-permute-done.2.refs_2_), channel_id=1, source_target_pairs={{16,17},{17,16},{18,19},{19,18},{20,21},{21,20},{22,23},{23,22},{2... | collective-permute-start | bytes 983048 | tf_op jit(solution)/shard_map/ppermute | solution.py:409
  29.4 11.4 %collective-permute-start.12 = (bf16[160,1024]{1,0:T(8,128)(2,1)S(1)}, bf16[160,1024]{1,0:T(8,128)(2,1)S(1)}, u32[]{:S(2)}, u32[]{:S(2)}) collective-permute-start(bf16[160,1024]{1,0:T(8,128)(2,1)S(1)} %get-tuple-element.57), channel_id=1, source_target_pairs={{0,12},{1,13},{2,14},{3,15},{4,8},{5,9},{6,10},{7,11},{8,4},{9,5},... | collective-permute-start | bytes 983048 | tf_op jit(solution)/shard_map/ppermute | solution.py:409
  31.7 11.2 %collective-permute-start.5 = (bf16[160,1536]{1,0:T(8,128)(2,1)S(1)}, bf16[160,1536]{1,0:T(8,128)(2,1)S(1)}, u32[]{:S(2)}, u32[]{:S(2)}) collective-permute-start(bf16[160,1536]{1,0:T(8,128)(2,1)S(1)} %get-tuple-element.49), channel_id=1, source_target_pairs={{0,2},{1,3},{2,0},{3,1},{4,6},{5,7},{6,4},{7,5},{8,10},{9,11},{10,... | collective-permute-start | bytes 1474568 | tf_op jit(solution)/shard_map/ppermute | solution.py:409
  40.2 16.5 %collective-permute-start.9 = (bf16[160,1536]{1,0:T(8,128)(2,1)S(1)}, bf16[160,1536]{1,0:T(8,128)(2,1)S(1)}, u32[]{:S(2)}, u32[]{:S(2)}) collective-permute-start(bf16[160,1536]{1,0:T(8,128)(2,1)S(1)} %get-tuple-element.53), channel_id=1, source_target_pairs={{0,2},{1,3},{2,0},{3,1},{4,6},{5,7},{6,4},{7,5},{8,10},{9,11},{10,... | collective-permute-start | bytes 1474568 | tf_op jit(solution)/shard_map/ppermute | solution.py:409
  40.8 8.3 %collective-permute-start.10 = (bf16[160,1024]{1,0:T(8,128)(2,1)S(1)}, bf16[160,1024]{1,0:T(8,128)(2,1)S(1)}, u32[]{:S(2)}, u32[]{:S(2)}) collective-permute-start(bf16[160,1024]{1,0:T(8,128)(2,1)S(1)} %collective-permute-done.6.refs_0_), channel_id=1, source_target_pairs={{0,1},{1,0},{2,3},{3,2},{4,5},{5,4},{6,7},{7,6},{8,9},{9,8},{10,11... | collective-permute-start | bytes 983048 | tf_op jit(solution)/shard_map/ppermute | solution.py:409
  40.8 15.8 %collective-permute-start.13 = (bf16[160,1024]{1,0:T(8,128)(2,1)S(1)}, bf16[160,1024]{1,0:T(8,128)(2,1)S(1)}, u32[]{:S(2)}, u32[]{:S(2)}) collective-permute-start(bf16[160,1024]{1,0:T(8,128)(2,1)S(1)} %collective-permute-done.12.refs_0_), channel_id=1, source_target_pairs={{0,1},{1,0},{2,3},{3,2},{4,5},{5,4},{6,7},{7,6},{8,9},{9,8},{10,11... | collective-permute-start | bytes 983048 | tf_op jit(solution)/shard_map/ppermute | solution.py:409
  55.1 8.7 %collective-permute-start.11 = (bf16[160,1024]{1,0:T(8,128)(2,1)}, bf16[160,1024]{1,0:T(8,128)(2,1)S(1)}, u32[]{:S(2)}, u32[]{:S(2)}) collective-permute-start(bf16[160,1024]{1,0:T(8,128)(2,1)} %get-tuple-element.56), channel_id=1, source_target_pairs={{0,2},{1,3},{2,0},{3,1},{4,6},{5,7},{6,4},{7,5},{8,10},{9,11},{10,... | collective-permute-start | bytes 983048 | tf_op jit(solution)/shard_map/ppermute | solution.py:409
  56.7 7.0 %copy-start.3 = (s32[1,2,2]{2,1,0:T(2,128)S(1)}, s32[1,2,2]{2,1,0:T(2,128)}, u32[]{:S(2)}) copy-start(s32[1,2,2]{2,1,0:T(2,128)} %param.17) | copy-start | bytes 52
  62.7 7.4 %collective-permute-start.14 = (bf16[160,1024]{1,0:T(8,128)(2,1)}, bf16[160,1024]{1,0:T(8,128)(2,1)S(1)}, u32[]{:S(2)}, u32[]{:S(2)}) collective-permute-start(bf16[160,1024]{1,0:T(8,128)(2,1)} %get-tuple-element.61), channel_id=1, source_target_pairs={{0,2},{1,3},{2,0},{3,1},{4,6},{5,7},{6,4},{7,5},{8,10},{9,11},{10,... | collective-permute-start | bytes 983048 | tf_op jit(solution)/shard_map/ppermute | solution.py:409
  63.8 21.8 %copy-start = (bf16[1,1024,2048]{2,1,0:T(8,128)(2,1)S(1)}, bf16[1,1024,2048]{2,1,0:T(8,128)(2,1)}, u32[]{:S(2)}) copy-start(bf16[1,1024,2048]{2,1,0:T(8,128)(2,1)} %param.14) | copy-start | bytes 12582916
  75.5 8.8 %collective-permute-start.15 = (bf16[160,512]{1,0:T(8,128)(2,1)S(1)}, bf16[160,512]{1,0:T(8,128)(2,1)S(1)}, u32[]{:S(2)}, u32[]{:S(2)}) collective-permute-start(bf16[160,512]{1,0:T(8,128)(2,1)S(1)} %get-tuple-element.62), channel_id=1, source_target_pairs={{0,4},{1,5},{2,6},{3,7},{4,0},{5,1},{6,2},{7,3},{8,12},{9,13},{10,... | collective-permute-start | bytes 491528 | tf_op jit(solution)/shard_map/ppermute | solution.py:409
  75.6 10.0 %collective-permute-start.16 = (bf16[160,512]{1,0:T(8,128)(2,1)S(1)}, bf16[160,512]{1,0:T(8,128)(2,1)S(1)}, u32[]{:S(2)}, u32[]{:S(2)}) collective-permute-start(bf16[160,512]{1,0:T(8,128)(2,1)S(1)} %get-tuple-element.63), channel_id=1, source_target_pairs={{0,6},{1,7},{2,4},{3,5},{4,2},{5,3},{6,0},{7,1},{8,14},{9,15},{10,... | collective-permute-start | bytes 491528 | tf_op jit(solution)/shard_map/ppermute | solution.py:409
  85.6 6.5 %collective-permute-start.17 = (bf16[160,512]{1,0:T(8,128)(2,1)S(1)}, bf16[160,512]{1,0:T(8,128)(2,1)S(1)}, u32[]{:S(2)}, u32[]{:S(2)}) collective-permute-start(bf16[160,512]{1,0:T(8,128)(2,1)S(1)} %get-tuple-element.74), channel_id=1, source_target_pairs={{0,2},{1,3},{2,0},{3,1},{4,6},{5,7},{6,4},{7,5},{8,10},{9,11},{10,... | collective-permute-start | bytes 491528 | tf_op jit(solution)/shard_map/ppermute | solution.py:409
  85.6 18.6 %copy-start.1 = (bf16[1,2,160,1024]{3,2,1,0:T(8,128)(2,1)S(1)}, bf16[1,2,160,1024]{3,2,1,0:T(8,128)(2,1)}, u32[]{:S(2)}) copy-start(bf16[1,2,160,1024]{3,2,1,0:T(8,128)(2,1)} %hidden.5) | copy-start | bytes 1966084
  87.0 10.0 %collective-permute-start.19 = (bf16[160,1024]{1,0:T(8,128)(2,1)S(1)}, bf16[160,1024]{1,0:T(8,128)(2,1)S(1)}, u32[]{:S(2)}, u32[]{:S(2)}) collective-permute-start(bf16[160,1024]{1,0:T(8,128)(2,1)S(1)} %get-tuple-element.78), channel_id=1, source_target_pairs={{0,1},{1,0},{2,3},{3,2},{4,5},{5,4},{6,7},{7,6},{8,9},{9,8},{10,11... | collective-permute-start | bytes 983048 | tf_op jit(solution)/shard_map/ppermute | solution.py:409
  93.5 10.7 %collective-permute-start.18 = (bf16[160,1024]{1,0:T(8,128)(2,1)S(1)}, bf16[160,1024]{1,0:T(8,128)(2,1)S(1)}, u32[]{:S(2)}, u32[]{:S(2)}) collective-permute-start(bf16[160,1024]{1,0:T(8,128)(2,1)S(1)} %get-tuple-element.76), channel_id=1, source_target_pairs={{0,1},{1,0},{2,3},{3,2},{4,5},{5,4},{6,7},{7,6},{8,9},{9,8},{10,11... | collective-permute-start | bytes 983048 | tf_op jit(solution)/shard_map/ppermute | solution.py:409

commit v5 on v4

--- a/solution.py
+++ b/solution.py
@@ -93,6 +93,10 @@
 BLOCK = 4
 
 
+def in_vmem(array):
+    return pltpu.with_memory_space_constraint(array, pltpu.VMEM)
+
+
 def in_hbm(array):
     return pltpu.with_memory_space_constraint(array, pltpu.HBM)
 
@@ -126,12 +130,13 @@
     return pl.pallas_call(
         kernel,
         out_shape=[jax.ShapeDtypeStruct(hidden.shape[2:], jnp.bfloat16)] * 2,
-        in_specs=[pl.BlockSpec(memory_space=pltpu.SMEM)] + [pl.BlockSpec(memory_space=pltpu.HBM)] * len(arrays),
+        in_specs=[pl.BlockSpec(memory_space=pltpu.SMEM), pl.BlockSpec(memory_space=pltpu.HBM)]
+        + [pl.BlockSpec(memory_space=pl.ANY)] * (len(arrays) - 1),
         out_specs=[IN_VMEM] * 2,
         scratch_shapes=[pltpu.SemaphoreType.DMA((2,))],
         compiler_params=pltpu.CompilerParams(vmem_limit_bytes=4 * MIB),
         cost_estimate=SMALL,
-    )(table, *[in_hbm(array) for array in arrays])
+    )(table, in_hbm(hidden), *arrays[1:])
 
 
 def mark(array):
@@ -159,23 +164,37 @@
     return lax.rsqrt(total / features + 1e-06)
 
 
-def project_kernel(parts, count, queried, table, *refs):
+def fetch_kernel(count, *refs):
+    sources, targets, sems = refs[:count], refs[count:-1], refs[-1]
+    copies = [
+        pltpu.make_async_copy(source.at[0], target, sems.at[n])
+        for n, (source, target) in enumerate(zip(sources, targets))
+    ]
+    for copy in copies:
+        copy.start()
+    for copy in copies:
+        copy.wait()
+
+
+def fetch(weights):
+    return pl.pallas_call(
+        functools.partial(fetch_kernel, len(weights)),
+        out_shape=[pltpu.VMEM(weight.shape[1:], jnp.bfloat16) for weight in weights],
+        in_specs=[pl.BlockSpec(memory_space=pltpu.HBM)] * len(weights),
+        out_specs=[IN_VMEM] * len(weights),
+        scratch_shapes=[pltpu.SemaphoreType.DMA((len(weights),))],
+        compiler_params=pltpu.CompilerParams(vmem_limit_bytes=2 * MIB),
+        cost_estimate=SMALL,
+    )(*[in_hbm(weight) for weight in weights])
+
+
+def project_kernel(count, queried, table, *refs):
     size = 4 if queried else 2
-    rest = refs[size:]
-    (gain, last_gain), weights, rest = rest[:2], rest[2 : 2 + size // 2 + 1], rest[2 + size // 2 + 1 :]
-    outs, (xk, xq, fk, fq, held, sems) = rest[:count], rest[count:]
+    (gain, last_gain), weights, rest = refs[size : size + 2], refs[size + 2 : size + 5], refs[size + 5 :]
+    outs, (xk, xq, fk, fq) = rest[:count], rest[-4:]
     side = table[SIDE]
     rows, half = refs[0].shape
-    width = held.shape[2] // count
-    copies = []
-    piece = 2 * half // parts
-    for n, weight in enumerate(weights):
-        for m in range(parts):
-            here = pl.ds(m * piece, piece)
-            copies.append(pltpu.make_async_copy(weight.at[0, here], held.at[n, here], sems.at[n, m]))
-    ahead = len(copies)
-    for copy in copies[:ahead]:
-        copy.start()
+    width = weights[0].shape[1] // count
 
     def fill(own, other, gains, x, f):
         total = times_gain(own, gains, side, x.at[0]) + times_gain(other, gains, 1 - side, x.at[1])
@@ -204,44 +223,39 @@
     def part(s):
         return pl.ds(pl.multiple_of(s * half, half), half)
 
-    for n in range(len(weights)):
-        for m in range(n * parts, (n + 1) * parts):
-            copies[m].wait()
-            if m + ahead < len(copies):
-                copies[m + ahead].start()
+    for n in range(3 if queried else 2):
         x, f = (xq, fq) if n == 2 else (xk, fk)
         scale = f[:, :1] * SCALE if n == 2 else f[:, :1]
         for turn in range(count - 1, -1, -1):
             columns = pl.ds(pl.multiple_of((table[HEAD] ^ turn) * width, width), width)
-            total = jnp.dot(x[0], held[n, part(side), columns], preferred_element_type=jnp.float32)
-            total += jnp.dot(x[1], held[n, part(1 - side), columns], preferred_element_type=jnp.float32)
+            total = jnp.dot(x[0], weights[n][part(side), columns], preferred_element_type=jnp.float32)
+            total += jnp.dot(x[1], weights[n][part(1 - side), columns], preferred_element_type=jnp.float32)
             outs[turn][:, n * width : (n + 1) * width] = (total * scale).astype(jnp.bfloat16)
 
 
-def project(table, arrays, gains, weights, count, parts=1):
+def project(table, arrays, gains, weights, count):
     rows, half = arrays[0].shape
-    columns = weights[0].shape[2]
+    columns = weights[0].shape[1]
     queried = len(arrays) == 4
-    weights = weights[: 3 if queried else 2]
-    width = len(weights) * columns // count
-    return pl.pallas_call(
-        functools.partial(project_kernel, parts, count, queried),
-        out_shape=[jax.ShapeDtypeStruct((rows, width), jnp.bfloat16)] * count,
+    width = (3 if queried else 2) * columns // count
+    first = 1 + len(arrays) + 2
+    products = pl.pallas_call(
+        functools.partial(project_kernel, count, queried),
+        out_shape=[jax.ShapeDtypeStruct((rows, width), jnp.bfloat16)] * count
+        + [pltpu.VMEM(weight.shape, jnp.bfloat16) for weight in weights],
         grid_spec=pltpu.PrefetchScalarGridSpec(
             num_scalar_prefetch=1,
             grid=(1,),
-            in_specs=[IN_VMEM] * (len(arrays) + 2) + [pl.BlockSpec(memory_space=pltpu.HBM)] * len(weights),
-            out_specs=[IN_VMEM] * count,
+            in_specs=[IN_VMEM] * (len(arrays) + 2 + len(weights)),
+            out_specs=[IN_VMEM] * (count + len(weights)),
             scratch_shapes=[pltpu.VMEM((2, rows, half), jnp.bfloat16)] * 2
-            + [pltpu.VMEM((rows, LANES), jnp.float32)] * 2
-            + [
-                pltpu.VMEM((len(weights), 2 * half, columns), jnp.bfloat16),
-                pltpu.SemaphoreType.DMA((len(weights), parts)),
-            ],
+            + [pltpu.VMEM((rows, LANES), jnp.float32)] * 2,
         ),
-        compiler_params=pltpu.CompilerParams(vmem_limit_bytes=24 * MIB),
+        input_output_aliases={first + n: count + n for n in range(len(weights))},
+        compiler_params=pltpu.CompilerParams(vmem_limit_bytes=8 * MIB),
         cost_estimate=SMALL,
-    )(table, *arrays, *gains, *[in_hbm(w) for w in weights])
+    )(table, *arrays, *gains, *[in_vmem(weight) for weight in weights])
+    return products[:count], products[count:]
 
 
 def attend_kernel(chosen, tile, blocks, table, lengths, *refs):
@@ -425,15 +439,16 @@
     source[2] = moved(source_away, 2, 0, (1,))
     if seq > 4:
         source[4] = moved(source_own, 4, 0)
-    query_other[2] = moved(query[2], 0, 1)
-    source_other[2] = moved(source[2], 0, 1, (1,))
+    held = [fetch([after(weight, query_other[0]) for weight in weights])]
+    query_other[2] = moved(after(query[2], held[0]), 0, 1)
+    source_other[2] = moved(after(source[2], held[0]), 0, 1, (1,))
 
     def projected(chunk, *others):
         parts = [source[chunk], source_other[chunk]]
         if chunk < 4:
             parts = [query[chunk], query_other[chunk]] + parts
         parts[0] = after(parts[0], *others)
-        kept, sent = project(table, parts, gains, weights, 2)
+        (kept, sent), held[0] = project(table, parts, gains, held[0], 2)
         return kept, moved(sent, 1, 0)
 
     done = {0: projected(0, query[2], source[2])}
@@ -456,14 +471,14 @@
     arrays = [array for chunk in chunks for array in done[chunk]]
 
     lengths = lengths.reshape(-1)
-    context = attend(table, lengths, arrays, (2, 3), width)
-    second_context = [moved(context[turn], 2 + turn, 0) for turn in range(2)]
-    context = attend(table, lengths, after(arrays, context), (0, 1), width)
-    first_context = [context[0], moved(after(context[1], second_context), 1, 0)]
+    context = attend(table, lengths, arrays, (0, 1), width)
+    first_context = [context[0], moved(context[1], 1, 0)]
+    context = attend(table, lengths, after(arrays, context), (2, 3), width)
+    second_context = [moved(after(context[turn], first_context[1]), 2 + turn, 0) for turn in range(2)]
+    away, own = output_parts(table, first_context, w_out[0])
+    first_beside = moved(away, 0, 1)
     away, second_own = output_parts(table, second_context, w_out[0])
     second_beside = moved(away, 0, 1)
-    away, own = output_parts(table, first_context, w_out[0])
-    first_beside = moved(away, 0, 1)
     return add_all(table, hidden, own, first_beside, second_own, second_beside)
 
 

time: 106 us -> 104 us (0.981)
  waiting for transfers between devices: 32.6 us -> 42.4 us
  Pallas kernels: 44.7 us -> 38.2 us
  starting transfers between devices: 27.3 us -> 22.4 us
    ppermute x19, waiting for transfers between devices: 32.6 us -> 42.4 us  [moved(): return lax.ppermute(value, ('segment', 'seq', 'mp'), pairs)]
    pallas_call x4 -> x5, Pallas kernels: 26 us -> 19.5 us  [the longest x4 14.8 us: project(): pl.pallas_call(functools.partial(project_kernel, count, queried), out_sha...]
    ppermute x19, starting transfers between devices: 24.9 us -> 20 us  [moved(): return lax.ppermute(value, ('segment', 'seq', 'mp'), pairs)]
  transfers between devices with their start and end apart: 20 -> 20, of which waited for: 10 -> 12; matrix products, arithmetic and copies ran while one was open for 0% -> 0% of each run, Pallas kernels for 36% -> 30%
where the time goes in v5:
time: 104 us; the launch traced here: 103 us
  waiting for transfers between devices  42.4 us (41%)
  Pallas kernels  38.2 us (37%)
  starting transfers between devices  22.4 us (22%)
    ppermute x19, waiting for transfers between devices, moved(): return lax.ppermute(value, ('segment', 'seq', 'mp'), pairs)  42.4 us
    ppermute x19, starting transfers between devices, moved(): return lax.ppermute(value, ('segment', 'seq', 'mp'), pairs)  20 us
    pallas_call x4, Pallas kernels, project(): pl.pallas_call(functools.partial(project_kernel, count, queried), out_sha...  14.8 us
    pallas_call x2, Pallas kernels, attend(): pl.pallas_call(functools.partial(attend_kernel, chosen, size, len(arrays)...  11 us
    pallas_call x1, Pallas kernels, fetch(): pl.pallas_call(functools.partial(fetch_kernel, len(weights)), out_shape=[...  4.69 us
    pallas_call x2, Pallas kernels, split(): pl.pallas_call(kernel, out_shape=[jax.ShapeDtypeStruct(hidden.shape[2:],...  3.27 us
    pallas_call x2, Pallas kernels, output_parts(): pl.pallas_call(functools.partial(output_kernel, len(pieces)), out_shape=[...  2.82 us
    ppermute x1, starting transfers between devices, passed_along(): lax.ppermute(value, axis, [(source, source + steps) for source in range(l...  2.39 us
  transfers between devices with their start and end apart: 20, of which 12 were waited for; matrix products, arithmetic and copies ran while one was open for 0% of the time, Pallas kernels for 30%

profile of v5, /device:TPU:0, one launch (start us, length us, event | category | flops | bytes accessed | tf_op | source)
XLA Modules:
  0.0 103.4 jit_solution(11846937527457578854)
XLA Ops:
  0.0 2.4 %collective-permute-start.1 = (bf16[2,160,1024]{2,1,0:T(8,128)(2,1)}, bf16[2,160,1024]{2,1,0:T(8,128)(2,1)S(1)}, u32[]{:S(2)}, u32[]{:S(2)}) collective-permute-start(bf16[2,160,1024]{2,1,0:T(8,128)(2,1)} %bitcast.23), channel_id=1, source_target_pairs={{0,16},{1,17},{2,18},{3,19},{4,20},{5,21},{6,22},{7,23},{8,24},{9,... | collective-permute-start | bytes 1966088 | tf_op jit(solution)/shard_map/ppermute | solution.py:21
  2.4 0.1 stack.55.table
  2.5 1.6 %shard_map.91 = (bf16[160,1024]{1,0:T(8,128)(2,1)S(1)}, bf16[160,1024]{1,0:T(8,128)(2,1)S(1)}) custom-call(s32[12]{0:T(128)S(1)} %stack.55.table, bf16[1,2,160,1024]{3,2,1,0:T(8,128)(2,1)} %hidden.5), custom_call_target="tpu_custom_call" | custom-call | flops 1 | bytes 1 | tf_op jit(solution)/shard_map/pallas_call | solution.py:130
  4.2 2.4 %collective-permute-start.3 = (bf16[160,1024]{1,0:T(8,128)(2,1)S(1)}, bf16[160,1024]{1,0:T(8,128)(2,1)S(1)}, u32[]{:S(2)}, u32[]{:S(2)}) collective-permute-start(bf16[160,1024]{1,0:T(8,128)(2,1)S(1)} %get-tuple-element.64.refs_0_), channel_id=1, source_target_pairs={{0,1},{1,0},{2,3},{3,2},{4,5},{5,4},{6,7},{7,6},{8,9},{9,8},{10,11... | collective-permute-start | bytes 983048 | tf_op jit(solution)/shard_map/ppermute | solution.py:423
  6.6 1.6 %collective-permute-start = (bf16[160,1024]{1,0:T(8,128)(2,1)S(1)}, bf16[160,1024]{1,0:T(8,128)(2,1)S(1)}, u32[]{:S(2)}, u32[]{:S(2)}) collective-permute-start(bf16[160,1024]{1,0:T(8,128)(2,1)S(1)} %get-tuple-element.61), channel_id=1, source_target_pairs={{0,4},{1,5},{2,6},{3,7},{4,0},{5,1},{6,2},{7,3},{8,12},{9,13},{10,... | collective-permute-start | bytes 983048 | tf_op jit(solution)/shard_map/ppermute | solution.py:423
  8.2 0.0 collective-permute-done.1
  8.2 1.6 %shard_map.92 = (bf16[160,1024]{1,0:T(8,128)(2,1)S(1)}, bf16[160,1024]{1,0:T(8,128)(2,1)S(1)}) custom-call(s32[12]{0:T(128)S(1)} %stack.55.table, bf16[1,2,160,1024]{3,2,1,0:T(8,128)(2,1)} %hidden.5, bf16[1,2,160,1024]{3,2,1,0:T(8,128)(2,1)S(1)} %bitcast.18), custom_call_target="tpu_custom_call" | custom-call | flops 1 | bytes 1 | tf_op jit(solution)/shard_map/pallas_call | solution.py:130
  9.8 0.7 collective-permute-start.2
  10.5 0.7 collective-permute-start.4
  11.2 2.7 %collective-permute-start.6 = (bf16[160,1024]{1,0:T(8,128)(2,1)S(1)}, bf16[160,1024]{1,0:T(8,128)(2,1)S(1)}, u32[]{:S(2)}, u32[]{:S(2)}) collective-permute-start(bf16[160,1024]{1,0:T(8,128)(2,1)S(1)} %get-tuple-element.65.refs_2_), channel_id=1, source_target_pairs={{0,8},{1,9},{2,10},{3,11},{4,12},{5,13},{6,14},{7,15},{8,0},{9,1},... | collective-permute-start | bytes 983048 | tf_op jit(solution)/shard_map/ppermute | solution.py:423
  13.8 0.0 collective-permute-done.3.refs_1_
  13.8 4.7 %shard_map.93 = (bf16[2048,1024]{1,0:T(8,128)(2,1)S(1)}, bf16[2048,1024]{1,0:T(8,128)(2,1)S(1)}, bf16[2048,1024]{1,0:T(8,128)(2,1)S(1)}) custom-call(bf16[1,2048,1024]{2,1,0:T(8,128)(2,1)} %refs_0_, bf16[1,2048,1024]{2,1,0:T(8,128)(2,1)} %refs_1_, bf16[1,2048,1024]{2,1,0:T(8,128)(2,1)} %refs_2_.2), custom_call_target="tpu_custom_call" | custom-call | flops 1 | bytes 1 | tf_op jit(solution)/shard_map/pallas_call | solution.py:180
  18.5 3.7 %collective-permute-done.refs_0_ = bf16[160,1024]{1,0:T(8,128)(2,1)S(1)} collective-permute-done((bf16[160,1024]{1,0:T(8,128)(2,1)S(1)}, bf16[160,1024]{1,0:T(8,128)(2,1)S(1)}, u32[]{:S(2)}, u32[]{:S(2)}) %collective-permute-start) | collective-permute-done | bytes 327712 | tf_op jit(solution)/shard_map/ppermute | solution.py:423
  22.2 0.0 collective-permute-start.7
  22.2 0.0 collective-permute-done.2.refs_2_
  22.2 0.7 collective-permute-start.8
  22.9 0.0 collective-permute-done.4.refs_3_
  22.9 3.8 %shard_map.94 = (bf16[160,1536]{1,0:T(8,128)(2,1)S(1)}, bf16[160,1536]{1,0:T(8,128)(2,1)S(1)}, bf16[2048,1024]{1,0:T(8,128)(2,1)S(1)}, bf16[2048,1024]{1,0:T(8,128)(2,1)S(1)}, bf16[2048,1024]{1,0:T(8,128)(2,1)S(1)}) custom-call(s32[12]{0:T(128)S(1)} %stack.55.table, ...), custom_call_target="tpu_custom_call", output_to_operand_aliasing={{2}: (7, {}), {3}: (8, {}), {4}: (9, {})} | custom-call | flops 1 | bytes 1 | tf_op jit(solution)/shard_map/pallas_call | solution.py:242
  26.8 2.7 %collective-permute-done.6.refs_0_ = bf16[160,1024]{1,0:T(8,128)(2,1)S(1)} collective-permute-done((bf16[160,1024]{1,0:T(8,128)(2,1)S(1)}, bf16[160,1024]{1,0:T(8,128)(2,1)S(1)}, u32[]{:S(2)}, u32[]{:S(2)}) %collective-permute-start.6) | collective-permute-done | bytes 327712 | tf_op jit(solution)/shard_map/ppermute | solution.py:423
  29.4 1.9 %collective-permute-start.12 = (bf16[160,1024]{1,0:T(8,128)(2,1)S(1)}, bf16[160,1024]{1,0:T(8,128)(2,1)S(1)}, u32[]{:S(2)}, u32[]{:S(2)}) collective-permute-start(bf16[160,1024]{1,0:T(8,128)(2,1)S(1)} %get-tuple-element.89), channel_id=1, source_target_pairs={{0,12},{1,13},{2,14},{3,15},{4,8},{5,9},{6,10},{7,11},{8,4},{9,5},... | collective-permute-start | bytes 983048 | tf_op jit(solution)/shard_map/ppermute | solution.py:423
  31.4 1.5 %collective-permute-start.5 = (bf16[160,1536]{1,0:T(8,128)(2,1)S(1)}, bf16[160,1536]{1,0:T(8,128)(2,1)S(1)}, u32[]{:S(2)}, u32[]{:S(2)}) collective-permute-start(bf16[160,1536]{1,0:T(8,128)(2,1)S(1)} %get-tuple-element.73), channel_id=1, source_target_pairs={{0,2},{1,3},{2,0},{3,1},{4,6},{5,7},{6,4},{7,5},{8,10},{9,11},{10,... | collective-permute-start | bytes 1474568 | tf_op jit(solution)/shard_map/ppermute | solution.py:423
  32.8 0.0 collective-permute-done.7.refs_1_
  32.8 0.0 collective-permute-done.8.refs_3_
  32.8 3.8 %shard_map.95 = (bf16[160,1536]{1,0:T(8,128)(2,1)S(1)}, bf16[160,1536]{1,0:T(8,128)(2,1)S(1)}, bf16[2048,1024]{1,0:T(8,128)(2,1)S(1)}, bf16[2048,1024]{1,0:T(8,128)(2,1)S(1)}, bf16[2048,1024]{1,0:T(8,128)(2,1)S(1)}) custom-call(s32[12]{0:T(128)S(1)} %stack.55.table, ...), custom_call_target="tpu_custom_call", output_to_operand_aliasing={{2}: (7, {}), {3}: (8, {}), {4}: (9, {})} | custom-call | flops 1 | bytes 1 | tf_op jit(solution)/shard_map/pallas_call | solution.py:242
  36.7 0.6 collective-permute-start.9
  37.3 0.1 collective-permute-start.10
  37.5 4.3 %collective-permute-done.12.refs_0_ = bf16[160,1024]{1,0:T(8,128)(2,1)S(1)} collective-permute-done((bf16[160,1024]{1,0:T(8,128)(2,1)S(1)}, bf16[160,1024]{1,0:T(8,128)(2,1)S(1)}, u32[]{:S(2)}, u32[]{:S(2)}) %collective-permute-start.12) | collective-permute-done | bytes 327712 | tf_op jit(solution)/shard_map/ppermute | solution.py:423
  41.8 0.0 collective-permute-start.13
  41.8 3.4 %collective-permute-done.5.refs_1_ = bf16[160,1536]{1,0:T(8,128)(2,1)S(1)} collective-permute-done((bf16[160,1536]{1,0:T(8,128)(2,1)S(1)}, bf16[160,1536]{1,0:T(8,128)(2,1)S(1)}, u32[]{:S(2)}, u32[]{:S(2)}) %collective-permute-start.5) | collective-permute-done | bytes 491552 | tf_op jit(solution)/shard_map/ppermute | solution.py:423
  45.2 2.7 %collective-permute-done.10.refs_1_ = bf16[160,1024]{1,0:T(8,128)(2,1)S(1)} collective-permute-done((bf16[160,1024]{1,0:T(8,128)(2,1)S(1)}, bf16[160,1024]{1,0:T(8,128)(2,1)S(1)}, u32[]{:S(2)}, u32[]{:S(2)}) %collective-permute-start.10) | collective-permute-done | bytes 327712 | tf_op jit(solution)/shard_map/ppermute | solution.py:423
  47.9 3.5 %shard_map.96 = (bf16[160,1024]{1,0:T(8,128)(2,1)S(1)}, bf16[160,1024]{1,0:T(8,128)(2,1)}, bf16[2048,1024]{1,0:T(8,128)(2,1)S(1)}, bf16[2048,1024]{1,0:T(8,128)(2,1)S(1)}, bf16[2048,1024]{1,0:T(8,128)(2,1)S(1)}) custom-call(s32[12]{0:T(128)S(1)} %stack.55.table, ...), custom_call_target="tpu_custom_call", output_to_operand_aliasing={{2}: (5, {}), {3}: (6, {}), {4}: (7, {})} | custom-call | flops 1 | bytes 1 | tf_op jit(solution)/shard_map/pallas_call | solution.py:242
  51.4 1.5 %collective-permute-start.11 = (bf16[160,1024]{1,0:T(8,128)(2,1)}, bf16[160,1024]{1,0:T(8,128)(2,1)S(1)}, u32[]{:S(2)}, u32[]{:S(2)}) collective-permute-start(bf16[160,1024]{1,0:T(8,128)(2,1)} %get-tuple-element.88), channel_id=1, source_target_pairs={{0,2},{1,3},{2,0},{3,1},{4,6},{5,7},{6,4},{7,5},{8,10},{9,11},{10,... | collective-permute-start | bytes 983048 | tf_op jit(solution)/shard_map/ppermute | solution.py:423
  52.9 2.9 %collective-permute-done.9.refs_3_ = bf16[160,1536]{1,0:T(8,128)(2,1)S(1)} collective-permute-done((bf16[160,1536]{1,0:T(8,128)(2,1)S(1)}, bf16[160,1536]{1,0:T(8,128)(2,1)S(1)}, u32[]{:S(2)}, u32[]{:S(2)}) %collective-permute-start.9) | collective-permute-done | bytes 491552 | tf_op jit(solution)/shard_map/ppermute | solution.py:423
  55.7 0.0 collective-permute-done.13.refs_1_
  55.7 0.0 copy-start.2
  55.7 3.7 %shard_map.97 = (bf16[160,1024]{1,0:T(8,128)(2,1)S(1)}, bf16[160,1024]{1,0:T(8,128)(2,1)}, bf16[2048,1024]{1,0:T(8,128)(2,1)S(1)}, bf16[2048,1024]{1,0:T(8,128)(2,1)S(1)}, bf16[2048,1024]{1,0:T(8,128)(2,1)S(1)}) custom-call(s32[12]{0:T(128)S(1)} %stack.55.table, ...), custom_call_target="tpu_custom_call", output_to_operand_aliasing={{2}: (5, {}), {3}: (6, {}), {4}: (7, {})} | custom-call | flops 1 | bytes 1 | tf_op jit(solution)/shard_map/pallas_call | solution.py:242
  59.4 1.5 %collective-permute-start.14 = (bf16[160,1024]{1,0:T(8,128)(2,1)}, bf16[160,1024]{1,0:T(8,128)(2,1)S(1)}, u32[]{:S(2)}, u32[]{:S(2)}) collective-permute-start(bf16[160,1024]{1,0:T(8,128)(2,1)} %get-tuple-element.96), channel_id=1, source_target_pairs={{0,2},{1,3},{2,0},{3,1},{4,6},{5,7},{6,4},{7,5},{8,10},{9,11},{10,... | collective-permute-start | bytes 983048 | tf_op jit(solution)/shard_map/ppermute | solution.py:423
  60.9 0.0 copy-done.2
  60.9 0.1 reshape.6.lengths
  61.0 0.0 copy-start
  61.0 1.7 %collective-permute-done.11.refs_5_ = bf16[160,1024]{1,0:T(8,128)(2,1)S(1)} collective-permute-done((bf16[160,1024]{1,0:T(8,128)(2,1)}, bf16[160,1024]{1,0:T(8,128)(2,1)S(1)}, u32[]{:S(2)}, u32[]{:S(2)}) %collective-permute-start.11) | collective-permute-done | bytes 327712 | tf_op jit(solution)/shard_map/ppermute | solution.py:423
  62.7 7.3 %collective-permute-done.14.refs_7_ = bf16[160,1024]{1,0:T(8,128)(2,1)S(1)} collective-permute-done((bf16[160,1024]{1,0:T(8,128)(2,1)}, bf16[160,1024]{1,0:T(8,128)(2,1)S(1)}, u32[]{:S(2)}, u32[]{:S(2)}) %collective-permute-start.14) | collective-permute-done | bytes 327712 | tf_op jit(solution)/shard_map/ppermute | solution.py:423
  70.0 5.5 %shard_map.98 = (bf16[160,512]{1,0:T(8,128)(2,1)S(1)}, bf16[160,512]{1,0:T(8,128)(2,1)S(1)}) custom-call(s32[12]{0:T(128)S(1)} %stack.55.table, s32[4]{0:T(128)S(1)} %reshape.6.lengths, bf16[160,1536]{1,0:T(8,128)(2,1)S(1)} %get-tuple-element.101.refs_0_, bf16[160,1536]{1,0:T(8,128)(2,1)S(1)} %collective-permute-done.5.refs_1_, ...), custom_call_target="tpu_custom_call" | custom-call | flops 1 | bytes 1 | tf_op jit(solution)/shard_map/pallas_call | solution.py:323
  75.6 1.6 %collective-permute-start.15 = (bf16[160,512]{1,0:T(8,128)(2,1)S(1)}, bf16[160,512]{1,0:T(8,128)(2,1)S(1)}, u32[]{:S(2)}, u32[]{:S(2)}) collective-permute-start(bf16[160,512]{1,0:T(8,128)(2,1)S(1)} %get-tuple-element.98), channel_id=1, source_target_pairs={{0,2},{1,3},{2,0},{3,1},{4,6},{5,7},{6,4},{7,5},{8,10},{9,11},{10,... | collective-permute-start | bytes 491528 | tf_op jit(solution)/shard_map/ppermute | solution.py:423
  77.1 5.5 %shard_map.100 = (bf16[160,512]{1,0:T(8,128)(2,1)S(1)}, bf16[160,512]{1,0:T(8,128)(2,1)S(1)}) custom-call(s32[12]{0:T(128)S(1)} %stack.55.table, s32[4]{0:T(128)S(1)} %reshape.6.lengths, bf16[160,1536]{1,0:T(8,128)(2,1)S(1)} %get-tuple-element.101.refs_0_, bf16[160,1536]{1,0:T(8,128)(2,1)S(1)} %collective-permute-done.5.refs_1_, ...), custom_call_target="tpu_custom_call" | custom-call | flops 1 | bytes 1 | tf_op jit(solution)/shard_map/pallas_call | solution.py:323
  82.6 0.0 collective-permute-done.15.refs_1_
  82.6 0.1 collective-permute-start.18
  82.7 2.0 %collective-permute-start.17 = (bf16[160,512]{1,0:T(8,128)(2,1)S(1)}, bf16[160,512]{1,0:T(8,128)(2,1)S(1)}, u32[]{:S(2)}, u32[]{:S(2)}) collective-permute-start(bf16[160,512]{1,0:T(8,128)(2,1)S(1)} %get-tuple-element.110), channel_id=1, source_target_pairs={{0,4},{1,5},{2,6},{3,7},{4,0},{5,1},{6,2},{7,3},{8,12},{9,13},{10,... | collective-permute-start | bytes 491528 | tf_op jit(solution)/shard_map/ppermute | solution.py:423
  84.7 0.0 copy-done
  84.7 0.0 copy-start.1
  84.7 1.4 %shard_map.99 = (bf16[160,1024]{1,0:T(8,128)(2,1)S(1)}, bf16[160,1024]{1,0:T(8,128)(2,1)S(1)}) custom-call(s32[12]{0:T(128)S(1)} %stack.55.table, bf16[1024,2048]{1,0:T(8,128)(2,1)S(1)} %bitcast.16, bf16[160,512]{1,0:T(8,128)(2,1)S(1)} %get-tuple-element.97.refs_0_, bf16[160,512]{1,0:T(8,128)(2,1)S(1)} %collective-permute-done.15.refs_1_), custom_call_target="tpu_custom_call" | custom-call | flops 1 | bytes 1 | tf_op jit(solution)/shard_map/pallas_call | solution.py:358
  86.1 0.1 collective-permute-start.16
  86.2 4.5 %collective-permute-done.18.refs_1_ = bf16[160,512]{1,0:T(8,128)(2,1)S(1)} collective-permute-done((bf16[160,512]{1,0:T(8,128)(2,1)S(1)}, bf16[160,512]{1,0:T(8,128)(2,1)S(1)}, u32[]{:S(2)}, u32[]{:S(2)}) %collective-permute-start.18) | collective-permute-done | bytes 163872 | tf_op jit(solution)/shard_map/ppermute | solution.py:423
  90.7 1.1 %collective-permute-done.17.refs_0_ = bf16[160,512]{1,0:T(8,128)(2,1)S(1)} collective-permute-done((bf16[160,512]{1,0:T(8,128)(2,1)S(1)}, bf16[160,512]{1,0:T(8,128)(2,1)S(1)}, u32[]{:S(2)}, u32[]{:S(2)}) %collective-permute-start.17) | collective-permute-done | bytes 163872 | tf_op jit(solution)/shard_map/ppermute | solution.py:423
  91.9 1.4 %shard_map.101 = (bf16[160,1024]{1,0:T(8,128)(2,1)S(1)}, bf16[160,1024]{1,0:T(8,128)(2,1)S(1)}) custom-call(s32[12]{0:T(128)S(1)} %stack.55.table, bf16[1024,2048]{1,0:T(8,128)(2,1)S(1)} %bitcast.17, bf16[160,512]{1,0:T(8,128)(2,1)S(1)} %collective-permute-done.17.refs_0_, bf16[160,512]{1,0:T(8,128)(2,1)S(1)} %collective-permute-done.18.refs_1_), custom_call_target="tpu_custom_call" | custom-call | flops 1 | bytes 1 | tf_op jit(solution)/shard_map/pallas_call | solution.py:358
  93.3 0.5 collective-permute-start.19
  93.8 1.2 %collective-permute-done.16.beside = bf16[160,1024]{1,0:T(8,128)(2,1)S(1)} collective-permute-done((bf16[160,1024]{1,0:T(8,128)(2,1)S(1)}, bf16[160,1024]{1,0:T(8,128)(2,1)S(1)}, u32[]{:S(2)}, u32[]{:S(2)}) %collective-permute-start.16) | collective-permute-done | bytes 327712 | tf_op jit(solution)/shard_map/ppermute | solution.py:423
  95.0 6.9 %collective-permute-done.19.corner = bf16[160,1024]{1,0:T(8,128)(2,1)S(1)} collective-permute-done((bf16[160,1024]{1,0:T(8,128)(2,1)S(1)}, bf16[160,1024]{1,0:T(8,128)(2,1)S(1)}, u32[]{:S(2)}, u32[]{:S(2)}) %collective-permute-start.19) | collective-permute-done | bytes 327712 | tf_op jit(solution)/shard_map/ppermute | solution.py:423
  101.8 0.0 copy-done.1
  101.8 1.6 %shard_map.102 = bf16[1,2,160,1024]{3,2,1,0:T(8,128)(2,1)} custom-call(s32[12]{0:T(128)S(1)} %stack.55.table, bf16[1,2,160,1024]{3,2,1,0:T(8,128)(2,1)S(1)} %copy-done.1, bf16[160,1024]{1,0:T(8,128)(2,1)S(1)} %get-tuple-element.99.own, bf16[160,1024]{1,0:T(8,128)(2,1)S(1)} %collective-permute-done.16.beside, ...), custom_call_target="tpu_custom_call" | custom-call | tf_op jit(solution)/shard_map/pallas_call | solution.py:392
Async XLA Ops:
  0.0 8.2 %collective-permute-start.1 = (bf16[2,160,1024]{2,1,0:T(8,128)(2,1)}, bf16[2,160,1024]{2,1,0:T(8,128)(2,1)S(1)}, u32[]{:S(2)}, u32[]{:S(2)}) collective-permute-start(bf16[2,160,1024]{2,1,0:T(8,128)(2,1)} %bitcast.23), channel_id=1, source_target_pairs={{0,16},{1,17},{2,18},{3,19},{4,20},{5,21},{6,22},{7,23},{8,24},{9,... | collective-permute-start | bytes 1966088 | tf_op jit(solution)/shard_map/ppermute | solution.py:21
  4.2 9.7 %collective-permute-start.3 = (bf16[160,1024]{1,0:T(8,128)(2,1)S(1)}, bf16[160,1024]{1,0:T(8,128)(2,1)S(1)}, u32[]{:S(2)}, u32[]{:S(2)}) collective-permute-start(bf16[160,1024]{1,0:T(8,128)(2,1)S(1)} %get-tuple-element.64.refs_0_), channel_id=1, source_target_pairs={{0,1},{1,0},{2,3},{3,2},{4,5},{5,4},{6,7},{7,6},{8,9},{9,8},{10,11... | collective-permute-start | bytes 983048 | tf_op jit(solution)/shard_map/ppermute | solution.py:423
  6.6 15.6 %collective-permute-start = (bf16[160,1024]{1,0:T(8,128)(2,1)S(1)}, bf16[160,1024]{1,0:T(8,128)(2,1)S(1)}, u32[]{:S(2)}, u32[]{:S(2)}) collective-permute-start(bf16[160,1024]{1,0:T(8,128)(2,1)S(1)} %get-tuple-element.61), channel_id=1, source_target_pairs={{0,4},{1,5},{2,6},{3,7},{4,0},{5,1},{6,2},{7,3},{8,12},{9,13},{10,... | collective-permute-start | bytes 983048 | tf_op jit(solution)/shard_map/ppermute | solution.py:423
  9.8 12.4 %collective-permute-start.2 = (bf16[160,1024]{1,0:T(8,128)(2,1)S(1)}, bf16[160,1024]{1,0:T(8,128)(2,1)S(1)}, u32[]{:S(2)}, u32[]{:S(2)}) collective-permute-start(bf16[160,1024]{1,0:T(8,128)(2,1)S(1)} %get-tuple-element.89), channel_id=1, source_target_pairs={{16,20},{17,21},{18,22},{19,23},{20,16},{21,17},{22,18},{23,19},{2... | collective-permute-start | bytes 983048 | tf_op jit(solution)/shard_map/ppermute | solution.py:423
  10.5 12.4 %collective-permute-start.4 = (bf16[160,1024]{1,0:T(8,128)(2,1)S(1)}, bf16[160,1024]{1,0:T(8,128)(2,1)S(1)}, u32[]{:S(2)}, u32[]{:S(2)}) collective-permute-start(bf16[160,1024]{1,0:T(8,128)(2,1)S(1)} %get-tuple-element.65.refs_2_), channel_id=1, source_target_pairs={{16,17},{17,16},{18,19},{19,18},{20,21},{21,20},{22,23},{23,22},{2... | collective-permute-start | bytes 983048 | tf_op jit(solution)/shard_map/ppermute | solution.py:423
  11.2 18.2 %collective-permute-start.6 = (bf16[160,1024]{1,0:T(8,128)(2,1)S(1)}, bf16[160,1024]{1,0:T(8,128)(2,1)S(1)}, u32[]{:S(2)}, u32[]{:S(2)}) collective-permute-start(bf16[160,1024]{1,0:T(8,128)(2,1)S(1)} %get-tuple-element.65.refs_2_), channel_id=1, source_target_pairs={{0,8},{1,9},{2,10},{3,11},{4,12},{5,13},{6,14},{7,15},{8,0},{9,1},... | collective-permute-start | bytes 983048 | tf_op jit(solution)/shard_map/ppermute | solution.py:423
  22.2 10.6 %collective-permute-start.7 = (bf16[160,1024]{1,0:T(8,128)(2,1)S(1)}, bf16[160,1024]{1,0:T(8,128)(2,1)S(1)}, u32[]{:S(2)}, u32[]{:S(2)}) collective-permute-start(bf16[160,1024]{1,0:T(8,128)(2,1)S(1)} %collective-permute-done.refs_0_), channel_id=1, source_target_pairs={{0,1},{1,0},{2,3},{3,2},{4,5},{5,4},{6,7},{7,6},{8,9},{9,8},{10,11... | collective-permute-start | bytes 983048 | tf_op jit(solution)/shard_map/ppermute | solution.py:423
  22.2 10.6 %collective-permute-start.8 = (bf16[160,1024]{1,0:T(8,128)(2,1)S(1)}, bf16[160,1024]{1,0:T(8,128)(2,1)S(1)}, u32[]{:S(2)}, u32[]{:S(2)}) collective-permute-start(bf16[160,1024]{1,0:T(8,128)(2,1)S(1)} %collective-permute-done.2.refs_2_), channel_id=1, source_target_pairs={{16,17},{17,16},{18,19},{19,18},{20,21},{21,20},{22,23},{23,22},{2... | collective-permute-start | bytes 983048 | tf_op jit(solution)/shard_map/ppermute | solution.py:423
  29.4 12.3 %collective-permute-start.12 = (bf16[160,1024]{1,0:T(8,128)(2,1)S(1)}, bf16[160,1024]{1,0:T(8,128)(2,1)S(1)}, u32[]{:S(2)}, u32[]{:S(2)}) collective-permute-start(bf16[160,1024]{1,0:T(8,128)(2,1)S(1)} %get-tuple-element.89), channel_id=1, source_target_pairs={{0,12},{1,13},{2,14},{3,15},{4,8},{5,9},{6,10},{7,11},{8,4},{9,5},... | collective-permute-start | bytes 983048 | tf_op jit(solution)/shard_map/ppermute | solution.py:423
  31.4 13.8 %collective-permute-start.5 = (bf16[160,1536]{1,0:T(8,128)(2,1)S(1)}, bf16[160,1536]{1,0:T(8,128)(2,1)S(1)}, u32[]{:S(2)}, u32[]{:S(2)}) collective-permute-start(bf16[160,1536]{1,0:T(8,128)(2,1)S(1)} %get-tuple-element.73), channel_id=1, source_target_pairs={{0,2},{1,3},{2,0},{3,1},{4,6},{5,7},{6,4},{7,5},{8,10},{9,11},{10,... | collective-permute-start | bytes 1474568 | tf_op jit(solution)/shard_map/ppermute | solution.py:423
  36.7 19.0 %collective-permute-start.9 = (bf16[160,1536]{1,0:T(8,128)(2,1)S(1)}, bf16[160,1536]{1,0:T(8,128)(2,1)S(1)}, u32[]{:S(2)}, u32[]{:S(2)}) collective-permute-start(bf16[160,1536]{1,0:T(8,128)(2,1)S(1)} %get-tuple-element.82), channel_id=1, source_target_pairs={{0,2},{1,3},{2,0},{3,1},{4,6},{5,7},{6,4},{7,5},{8,10},{9,11},{10,... | collective-permute-start | bytes 1474568 | tf_op jit(solution)/shard_map/ppermute | solution.py:423
  37.3 10.6 %collective-permute-start.10 = (bf16[160,1024]{1,0:T(8,128)(2,1)S(1)}, bf16[160,1024]{1,0:T(8,128)(2,1)S(1)}, u32[]{:S(2)}, u32[]{:S(2)}) collective-permute-start(bf16[160,1024]{1,0:T(8,128)(2,1)S(1)} %collective-permute-done.6.refs_0_), channel_id=1, source_target_pairs={{0,1},{1,0},{2,3},{3,2},{4,5},{5,4},{6,7},{7,6},{8,9},{9,8},{10,11... | collective-permute-start | bytes 983048 | tf_op jit(solution)/shard_map/ppermute | solution.py:423
  41.8 14.0 %collective-permute-start.13 = (bf16[160,1024]{1,0:T(8,128)(2,1)S(1)}, bf16[160,1024]{1,0:T(8,128)(2,1)S(1)}, u32[]{:S(2)}, u32[]{:S(2)}) collective-permute-start(bf16[160,1024]{1,0:T(8,128)(2,1)S(1)} %collective-permute-done.12.refs_0_), channel_id=1, source_target_pairs={{0,1},{1,0},{2,3},{3,2},{4,5},{5,4},{6,7},{7,6},{8,9},{9,8},{10,11... | collective-permute-start | bytes 983048 | tf_op jit(solution)/shard_map/ppermute | solution.py:423
  51.4 11.3 %collective-permute-start.11 = (bf16[160,1024]{1,0:T(8,128)(2,1)}, bf16[160,1024]{1,0:T(8,128)(2,1)S(1)}, u32[]{:S(2)}, u32[]{:S(2)}) collective-permute-start(bf16[160,1024]{1,0:T(8,128)(2,1)} %get-tuple-element.88), channel_id=1, source_target_pairs={{0,2},{1,3},{2,0},{3,1},{4,6},{5,7},{6,4},{7,5},{8,10},{9,11},{10,... | collective-permute-start | bytes 983048 | tf_op jit(solution)/shard_map/ppermute | solution.py:423
  55.7 5.2 %copy-start.2 = (s32[1,2,2]{2,1,0:T(2,128)S(1)}, s32[1,2,2]{2,1,0:T(2,128)}, u32[]{:S(2)}) copy-start(s32[1,2,2]{2,1,0:T(2,128)} %param.17) | copy-start | bytes 52
  59.4 10.6 %collective-permute-start.14 = (bf16[160,1024]{1,0:T(8,128)(2,1)}, bf16[160,1024]{1,0:T(8,128)(2,1)S(1)}, u32[]{:S(2)}, u32[]{:S(2)}) collective-permute-start(bf16[160,1024]{1,0:T(8,128)(2,1)} %get-tuple-element.96), channel_id=1, source_target_pairs={{0,2},{1,3},{2,0},{3,1},{4,6},{5,7},{6,4},{7,5},{8,10},{9,11},{10,... | collective-permute-start | bytes 983048 | tf_op jit(solution)/shard_map/ppermute | solution.py:423
  61.0 23.7 %copy-start = (bf16[1,1024,2048]{2,1,0:T(8,128)(2,1)S(1)}, bf16[1,1024,2048]{2,1,0:T(8,128)(2,1)}, u32[]{:S(2)}) copy-start(bf16[1,1024,2048]{2,1,0:T(8,128)(2,1)} %param.14) | copy-start | bytes 12582916
  75.6 7.1 %collective-permute-start.15 = (bf16[160,512]{1,0:T(8,128)(2,1)S(1)}, bf16[160,512]{1,0:T(8,128)(2,1)S(1)}, u32[]{:S(2)}, u32[]{:S(2)}) collective-permute-start(bf16[160,512]{1,0:T(8,128)(2,1)S(1)} %get-tuple-element.98), channel_id=1, source_target_pairs={{0,2},{1,3},{2,0},{3,1},{4,6},{5,7},{6,4},{7,5},{8,10},{9,11},{10,... | collective-permute-start | bytes 491528 | tf_op jit(solution)/shard_map/ppermute | solution.py:423
  82.6 8.1 %collective-permute-start.18 = (bf16[160,512]{1,0:T(8,128)(2,1)S(1)}, bf16[160,512]{1,0:T(8,128)(2,1)S(1)}, u32[]{:S(2)}, u32[]{:S(2)}) collective-permute-start(bf16[160,512]{1,0:T(8,128)(2,1)S(1)} %get-tuple-element.112), channel_id=1, source_target_pairs={{0,6},{1,7},{2,4},{3,5},{4,2},{5,3},{6,0},{7,1},{8,14},{9,15},{10,... | collective-permute-start | bytes 491528 | tf_op jit(solution)/shard_map/ppermute | solution.py:423
  82.7 9.2 %collective-permute-start.17 = (bf16[160,512]{1,0:T(8,128)(2,1)S(1)}, bf16[160,512]{1,0:T(8,128)(2,1)S(1)}, u32[]{:S(2)}, u32[]{:S(2)}) collective-permute-start(bf16[160,512]{1,0:T(8,128)(2,1)S(1)} %get-tuple-element.110), channel_id=1, source_target_pairs={{0,4},{1,5},{2,6},{3,7},{4,0},{5,1},{6,2},{7,3},{8,12},{9,13},{10,... | collective-permute-start | bytes 491528 | tf_op jit(solution)/shard_map/ppermute | solution.py:423
  84.7 17.1 %copy-start.1 = (bf16[1,2,160,1024]{3,2,1,0:T(8,128)(2,1)S(1)}, bf16[1,2,160,1024]{3,2,1,0:T(8,128)(2,1)}, u32[]{:S(2)}) copy-start(bf16[1,2,160,1024]{3,2,1,0:T(8,128)(2,1)} %hidden.5) | copy-start | bytes 1966084
  86.1 8.8 %collective-permute-start.16 = (bf16[160,1024]{1,0:T(8,128)(2,1)S(1)}, bf16[160,1024]{1,0:T(8,128)(2,1)S(1)}, u32[]{:S(2)}, u32[]{:S(2)}) collective-permute-start(bf16[160,1024]{1,0:T(8,128)(2,1)S(1)} %get-tuple-element.100), channel_id=1, source_target_pairs={{0,1},{1,0},{2,3},{3,2},{4,5},{5,4},{6,7},{7,6},{8,9},{9,8},{10,11... | collective-permute-start | bytes 983048 | tf_op jit(solution)/shard_map/ppermute | solution.py:423
  93.3 8.6 %collective-permute-start.19 = (bf16[160,1024]{1,0:T(8,128)(2,1)S(1)}, bf16[160,1024]{1,0:T(8,128)(2,1)S(1)}, u32[]{:S(2)}, u32[]{:S(2)}) collective-permute-start(bf16[160,1024]{1,0:T(8,128)(2,1)S(1)} %get-tuple-element.114), channel_id=1, source_target_pairs={{0,1},{1,0},{2,3},{3,2},{4,5},{5,4},{6,7},{7,6},{8,9},{9,8},{10,11... | collective-permute-start | bytes 983048 | tf_op jit(solution)/shard_map/ppermute | solution.py:423

commit v6 on v5

--- a/solution.py
+++ b/solution.py
@@ -139,20 +139,6 @@
     )(table, in_hbm(hidden), *arrays[1:])
 
 
-def mark(array):
-    def kernel(array, out):
-        out[...] = jnp.zeros(out.shape, out.dtype)
-
-    return pl.pallas_call(
-        kernel,
-        out_shape=jax.ShapeDtypeStruct((8, LANES), jnp.float32),
-        in_specs=[pl.BlockSpec(memory_space=pl.ANY)],
-        out_specs=IN_VMEM,
-        compiler_params=pltpu.CompilerParams(vmem_limit_bytes=MIB),
-        cost_estimate=pl.CostEstimate(flops=0, bytes_accessed=8 * MIB, transcendentals=0),
-    )(array)
-
-
 def times_gain(values, gains, side, into):
     half = values.shape[1]
     wide = values.astype(jnp.float32)
@@ -438,7 +424,7 @@
     source_other = {0: moved(source_own, 0, 1, (1,))}
     source[2] = moved(source_away, 2, 0, (1,))
     if seq > 4:
-        source[4] = moved(source_own, 4, 0)
+        source[4] = moved(after(source_own, query_other[0]), 4, 0)
     held = [fetch([after(weight, query_other[0]) for weight in weights])]
     query_other[2] = moved(after(query[2], held[0]), 0, 1)
     source_other[2] = moved(after(source[2], held[0]), 0, 1, (1,))
@@ -456,8 +442,7 @@
     if seq > 4:
         source[4] = after(source[4], before)
         source_other[4] = moved(source[4], 0, 1)
-        before = [before, mark(source[4])]
-    last = before
+    last = [before, source.get(4, before)]
     for chunk in chunks[3:]:
         source[chunk] = moved(after(source_away if chunk & 2 else source_own, last), chunk, 0)
         last = source[chunk]

time: 104 us -> 101 us (0.971)
  waiting for transfers between devices: 42.4 us -> 31.7 us
  starting transfers between devices: 22.4 us -> 30.5 us
    ppermute x19, waiting for transfers between devices: 42.4 us -> 31.7 us  [moved(): return lax.ppermute(value, ('segment', 'seq', 'mp'), pairs)]
    ppermute x19, starting transfers between devices: 20 us -> 28.1 us  [moved(): return lax.ppermute(value, ('segment', 'seq', 'mp'), pairs)]
  transfers between devices with their start and end apart: 20 -> 20, of which waited for: 12 -> 12; matrix products, arithmetic and copies ran while one was open for 0% -> 0% of each run, Pallas kernels for 30% -> 31%
where the time goes in v6:
time: 101 us
  Pallas kernels  38.2 us (38%)
  waiting for transfers between devices  31.7 us (31%)
  starting transfers between devices  30.5 us (30%)
    ppermute x19, waiting for transfers between devices, moved(): return lax.ppermute(value, ('segment', 'seq', 'mp'), pairs)  31.7 us
    ppermute x19, starting transfers between devices, moved(): return lax.ppermute(value, ('segment', 'seq', 'mp'), pairs)  28.1 us
    pallas_call x4, Pallas kernels, project(): pl.pallas_call(functools.partial(project_kernel, count, queried), out_sha...  14.8 us
    pallas_call x2, Pallas kernels, attend(): pl.pallas_call(functools.partial(attend_kernel, chosen, size, len(arrays)...  11 us
    pallas_call x1, Pallas kernels, fetch(): pl.pallas_call(functools.partial(fetch_kernel, len(weights)), out_shape=[...  4.68 us
    pallas_call x2, Pallas kernels, split(): pl.pallas_call(kernel, out_shape=[jax.ShapeDtypeStruct(hidden.shape[2:],...  3.27 us
    pallas_call x2, Pallas kernels, output_parts(): pl.pallas_call(functools.partial(output_kernel, len(pieces)), out_shape=[...  2.82 us
    ppermute x1, starting transfers between devices, passed_along(): lax.ppermute(value, axis, [(source, source + steps) for source in range(l...  2.39 us
  transfers between devices with their start and end apart: 20, of which 12 were waited for; matrix products, arithmetic and copies ran while one was open for 0% of the time, Pallas kernels for 31%

profile of v6, /device:TPU:0, one launch (start us, length us, event | category | flops | bytes accessed | tf_op | source)
XLA Modules:
  0.0 100.8 jit_solution(16566678381635349008)
XLA Ops:
  0.0 2.4 %collective-permute-start.1 = (bf16[2,160,1024]{2,1,0:T(8,128)(2,1)}, bf16[2,160,1024]{2,1,0:T(8,128)(2,1)S(1)}, u32[]{:S(2)}, u32[]{:S(2)}) collective-permute-start(bf16[2,160,1024]{2,1,0:T(8,128)(2,1)} %bitcast.23), channel_id=1, source_target_pairs={{0,16},{1,17},{2,18},{3,19},{4,20},{5,21},{6,22},{7,23},{8,24},{9,... | collective-permute-start | bytes 1966088 | tf_op jit(solution)/shard_map/ppermute | solution.py:21
  2.4 0.1 stack.55.table
  2.5 1.6 %shard_map.91 = (bf16[160,1024]{1,0:T(8,128)(2,1)S(1)}, bf16[160,1024]{1,0:T(8,128)(2,1)S(1)}) custom-call(s32[12]{0:T(128)S(1)} %stack.55.table, bf16[1,2,160,1024]{3,2,1,0:T(8,128)(2,1)} %hidden.5), custom_call_target="tpu_custom_call" | custom-call | flops 1 | bytes 1 | tf_op jit(solution)/shard_map/pallas_call | solution.py:130
  4.2 2.4 %collective-permute-start.3 = (bf16[160,1024]{1,0:T(8,128)(2,1)S(1)}, bf16[160,1024]{1,0:T(8,128)(2,1)S(1)}, u32[]{:S(2)}, u32[]{:S(2)}) collective-permute-start(bf16[160,1024]{1,0:T(8,128)(2,1)S(1)} %get-tuple-element.65.refs_0_), channel_id=1, source_target_pairs={{0,1},{1,0},{2,3},{3,2},{4,5},{5,4},{6,7},{7,6},{8,9},{9,8},{10,11... | collective-permute-start | bytes 983048 | tf_op jit(solution)/shard_map/ppermute | solution.py:409
  6.6 1.6 %collective-permute-start = (bf16[160,1024]{1,0:T(8,128)(2,1)S(1)}, bf16[160,1024]{1,0:T(8,128)(2,1)S(1)}, u32[]{:S(2)}, u32[]{:S(2)}) collective-permute-start(bf16[160,1024]{1,0:T(8,128)(2,1)S(1)} %get-tuple-element.62), channel_id=1, source_target_pairs={{0,4},{1,5},{2,6},{3,7},{4,0},{5,1},{6,2},{7,3},{8,12},{9,13},{10,... | collective-permute-start | bytes 983048 | tf_op jit(solution)/shard_map/ppermute | solution.py:409
  8.2 0.0 collective-permute-done.1
  8.2 1.6 %shard_map.92 = (bf16[160,1024]{1,0:T(8,128)(2,1)S(1)}, bf16[160,1024]{1,0:T(8,128)(2,1)S(1)}) custom-call(s32[12]{0:T(128)S(1)} %stack.55.table, bf16[1,2,160,1024]{3,2,1,0:T(8,128)(2,1)} %hidden.5, bf16[1,2,160,1024]{3,2,1,0:T(8,128)(2,1)S(1)} %bitcast.18), custom_call_target="tpu_custom_call" | custom-call | flops 1 | bytes 1 | tf_op jit(solution)/shard_map/pallas_call | solution.py:130
  9.8 0.7 collective-permute-start.2
  10.5 0.7 collective-permute-start.4
  11.2 2.6 %collective-permute-done.3.refs_1_ = bf16[160,1024]{1,0:T(8,128)(2,1)S(1)} collective-permute-done((bf16[160,1024]{1,0:T(8,128)(2,1)S(1)}, bf16[160,1024]{1,0:T(8,128)(2,1)S(1)}, u32[]{:S(2)}, u32[]{:S(2)}) %collective-permute-start.3) | collective-permute-done | bytes 327712 | tf_op jit(solution)/shard_map/ppermute | solution.py:409
  13.8 2.8 %collective-permute-start.9 = (bf16[160,1024]{1,0:T(8,128)(2,1)S(1)}, bf16[160,1024]{1,0:T(8,128)(2,1)S(1)}, u32[]{:S(2)}, u32[]{:S(2)}) collective-permute-start(bf16[160,1024]{1,0:T(8,128)(2,1)S(1)} %get-tuple-element.83.refs_2_), channel_id=1, source_target_pairs={{0,8},{1,9},{2,10},{3,11},{4,12},{5,13},{6,14},{7,15},{8,0},{9,1},... | collective-permute-start | bytes 983048 | tf_op jit(solution)/shard_map/ppermute | solution.py:409
  16.6 4.7 %shard_map.93 = (bf16[2048,1024]{1,0:T(8,128)(2,1)S(1)}, bf16[2048,1024]{1,0:T(8,128)(2,1)S(1)}, bf16[2048,1024]{1,0:T(8,128)(2,1)S(1)}) custom-call(bf16[1,2048,1024]{2,1,0:T(8,128)(2,1)} %refs_0_, bf16[1,2048,1024]{2,1,0:T(8,128)(2,1)} %refs_1_, bf16[1,2048,1024]{2,1,0:T(8,128)(2,1)} %refs_2_.2), custom_call_target="tpu_custom_call" | custom-call | flops 1 | bytes 1 | tf_op jit(solution)/shard_map/pallas_call | solution.py:166
  21.3 0.2 collective-permute-done.refs_0_
  21.6 1.4 %collective-permute-start.6 = (bf16[160,1024]{1,0:T(8,128)(2,1)S(1)}, bf16[160,1024]{1,0:T(8,128)(2,1)S(1)}, u32[]{:S(2)}, u32[]{:S(2)}) collective-permute-start(bf16[160,1024]{1,0:T(8,128)(2,1)S(1)} %collective-permute-done.refs_0_), channel_id=1, source_target_pairs={{0,1},{1,0},{2,3},{3,2},{4,5},{5,4},{6,7},{7,6},{8,9},{9,8},{10,11... | collective-permute-start | bytes 983048 | tf_op jit(solution)/shard_map/ppermute | solution.py:409
  22.9 0.0 collective-permute-done.2.refs_2_
  22.9 0.7 collective-permute-start.7
  23.6 0.0 collective-permute-done.4.refs_3_
  23.6 3.8 %shard_map.94 = (bf16[160,1536]{1,0:T(8,128)(2,1)S(1)}, bf16[160,1536]{1,0:T(8,128)(2,1)S(1)}, bf16[2048,1024]{1,0:T(8,128)(2,1)S(1)}, bf16[2048,1024]{1,0:T(8,128)(2,1)S(1)}, bf16[2048,1024]{1,0:T(8,128)(2,1)S(1)}) custom-call(s32[12]{0:T(128)S(1)} %stack.55.table, ...), custom_call_target="tpu_custom_call", output_to_operand_aliasing={{2}: (7, {}), {3}: (8, {}), {4}: (9, {})} | custom-call | flops 1 | bytes 1 | tf_op jit(solution)/shard_map/pallas_call | solution.py:228
  27.4 2.8 %collective-permute-done.9.refs_0_ = bf16[160,1024]{1,0:T(8,128)(2,1)S(1)} collective-permute-done((bf16[160,1024]{1,0:T(8,128)(2,1)S(1)}, bf16[160,1024]{1,0:T(8,128)(2,1)S(1)}, u32[]{:S(2)}, u32[]{:S(2)}) %collective-permute-start.9) | collective-permute-done | bytes 327712 | tf_op jit(solution)/shard_map/ppermute | solution.py:409
  30.3 4.1 %collective-permute-start.12 = (bf16[160,1024]{1,0:T(8,128)(2,1)S(1)}, bf16[160,1024]{1,0:T(8,128)(2,1)S(1)}, u32[]{:S(2)}, u32[]{:S(2)}) collective-permute-start(bf16[160,1024]{1,0:T(8,128)(2,1)S(1)} %get-tuple-element.91), channel_id=1, source_target_pairs={{0,12},{1,13},{2,14},{3,15},{4,8},{5,9},{6,10},{7,11},{8,4},{9,5},... | collective-permute-start | bytes 983048 | tf_op jit(solution)/shard_map/ppermute | solution.py:409
  34.4 1.5 %collective-permute-start.5 = (bf16[160,1536]{1,0:T(8,128)(2,1)S(1)}, bf16[160,1536]{1,0:T(8,128)(2,1)S(1)}, u32[]{:S(2)}, u32[]{:S(2)}) collective-permute-start(bf16[160,1536]{1,0:T(8,128)(2,1)S(1)} %get-tuple-element.74), channel_id=1, source_target_pairs={{0,2},{1,3},{2,0},{3,1},{4,6},{5,7},{6,4},{7,5},{8,10},{9,11},{10,... | collective-permute-start | bytes 1474568 | tf_op jit(solution)/shard_map/ppermute | solution.py:409
  35.9 0.0 collective-permute-done.6.refs_1_
  35.9 0.0 collective-permute-done.7.refs_3_
  35.9 3.8 %shard_map.95 = (bf16[160,1536]{1,0:T(8,128)(2,1)S(1)}, bf16[160,1536]{1,0:T(8,128)(2,1)S(1)}, bf16[2048,1024]{1,0:T(8,128)(2,1)S(1)}, bf16[2048,1024]{1,0:T(8,128)(2,1)S(1)}, bf16[2048,1024]{1,0:T(8,128)(2,1)S(1)}) custom-call(s32[12]{0:T(128)S(1)} %stack.55.table, ...), custom_call_target="tpu_custom_call", output_to_operand_aliasing={{2}: (7, {}), {3}: (8, {}), {4}: (9, {})} | custom-call | flops 1 | bytes 1 | tf_op jit(solution)/shard_map/pallas_call | solution.py:228
  39.7 0.6 collective-permute-start.8
  40.3 1.3 %collective-permute-start.10 = (bf16[160,1024]{1,0:T(8,128)(2,1)S(1)}, bf16[160,1024]{1,0:T(8,128)(2,1)S(1)}, u32[]{:S(2)}, u32[]{:S(2)}) collective-permute-start(bf16[160,1024]{1,0:T(8,128)(2,1)S(1)} %collective-permute-done.9.refs_0_), channel_id=1, source_target_pairs={{0,1},{1,0},{2,3},{3,2},{4,5},{5,4},{6,7},{7,6},{8,9},{9,8},{10,11... | collective-permute-start | bytes 983048 | tf_op jit(solution)/shard_map/ppermute | solution.py:409
  41.6 0.0 collective-permute-done.12.refs_0_
  41.6 1.3 %collective-permute-start.13 = (bf16[160,1024]{1,0:T(8,128)(2,1)S(1)}, bf16[160,1024]{1,0:T(8,128)(2,1)S(1)}, u32[]{:S(2)}, u32[]{:S(2)}) collective-permute-start(bf16[160,1024]{1,0:T(8,128)(2,1)S(1)} %collective-permute-done.12.refs_0_), channel_id=1, source_target_pairs={{0,1},{1,0},{2,3},{3,2},{4,5},{5,4},{6,7},{7,6},{8,9},{9,8},{10,11... | collective-permute-start | bytes 983048 | tf_op jit(solution)/shard_map/ppermute | solution.py:409
  42.9 5.6 %collective-permute-done.5.refs_1_ = bf16[160,1536]{1,0:T(8,128)(2,1)S(1)} collective-permute-done((bf16[160,1536]{1,0:T(8,128)(2,1)S(1)}, bf16[160,1536]{1,0:T(8,128)(2,1)S(1)}, u32[]{:S(2)}, u32[]{:S(2)}) %collective-permute-start.5) | collective-permute-done | bytes 491552 | tf_op jit(solution)/shard_map/ppermute | solution.py:409
  48.5 2.4 %collective-permute-done.10.refs_1_ = bf16[160,1024]{1,0:T(8,128)(2,1)S(1)} collective-permute-done((bf16[160,1024]{1,0:T(8,128)(2,1)S(1)}, bf16[160,1024]{1,0:T(8,128)(2,1)S(1)}, u32[]{:S(2)}, u32[]{:S(2)}) %collective-permute-start.10) | collective-permute-done | bytes 327712 | tf_op jit(solution)/shard_map/ppermute | solution.py:409
  50.9 3.5 %shard_map.96 = (bf16[160,1024]{1,0:T(8,128)(2,1)S(1)}, bf16[160,1024]{1,0:T(8,128)(2,1)}, bf16[2048,1024]{1,0:T(8,128)(2,1)S(1)}, bf16[2048,1024]{1,0:T(8,128)(2,1)S(1)}, bf16[2048,1024]{1,0:T(8,128)(2,1)S(1)}) custom-call(s32[12]{0:T(128)S(1)} %stack.55.table, ...), custom_call_target="tpu_custom_call", output_to_operand_aliasing={{2}: (5, {}), {3}: (6, {}), {4}: (7, {})} | custom-call | flops 1 | bytes 1 | tf_op jit(solution)/shard_map/pallas_call | solution.py:228
  54.4 0.9 collective-permute-start.11
  55.3 2.9 %collective-permute-done.8.refs_3_ = bf16[160,1536]{1,0:T(8,128)(2,1)S(1)} collective-permute-done((bf16[160,1536]{1,0:T(8,128)(2,1)S(1)}, bf16[160,1536]{1,0:T(8,128)(2,1)S(1)}, u32[]{:S(2)}, u32[]{:S(2)}) %collective-permute-start.8) | collective-permute-done | bytes 491552 | tf_op jit(solution)/shard_map/ppermute | solution.py:409
  58.2 0.0 collective-permute-done.13.refs_1_
  58.2 0.0 copy-start.2
  58.2 3.7 %shard_map.97 = (bf16[160,1024]{1,0:T(8,128)(2,1)S(1)}, bf16[160,1024]{1,0:T(8,128)(2,1)}, bf16[2048,1024]{1,0:T(8,128)(2,1)S(1)}, bf16[2048,1024]{1,0:T(8,128)(2,1)S(1)}, bf16[2048,1024]{1,0:T(8,128)(2,1)S(1)}) custom-call(s32[12]{0:T(128)S(1)} %stack.55.table, ...), custom_call_target="tpu_custom_call", output_to_operand_aliasing={{2}: (5, {}), {3}: (6, {}), {4}: (7, {})} | custom-call | flops 1 | bytes 1 | tf_op jit(solution)/shard_map/pallas_call | solution.py:228
  61.9 2.4 %collective-permute-start.14 = (bf16[160,1024]{1,0:T(8,128)(2,1)}, bf16[160,1024]{1,0:T(8,128)(2,1)S(1)}, u32[]{:S(2)}, u32[]{:S(2)}) collective-permute-start(bf16[160,1024]{1,0:T(8,128)(2,1)} %get-tuple-element.98), channel_id=1, source_target_pairs={{0,2},{1,3},{2,0},{3,1},{4,6},{5,7},{6,4},{7,5},{8,10},{9,11},{10,... | collective-permute-start | bytes 983048 | tf_op jit(solution)/shard_map/ppermute | solution.py:409
  64.2 0.0 copy-done.2
  64.2 0.1 reshape.6.lengths
  64.3 0.0 copy-start
  64.3 0.9 collective-permute-done.11.refs_5_
  65.2 4.3 %collective-permute-done.14.refs_7_ = bf16[160,1024]{1,0:T(8,128)(2,1)S(1)} collective-permute-done((bf16[160,1024]{1,0:T(8,128)(2,1)}, bf16[160,1024]{1,0:T(8,128)(2,1)S(1)}, u32[]{:S(2)}, u32[]{:S(2)}) %collective-permute-start.14) | collective-permute-done | bytes 327712 | tf_op jit(solution)/shard_map/ppermute | solution.py:409
  69.5 5.5 %shard_map.98 = (bf16[160,512]{1,0:T(8,128)(2,1)S(1)}, bf16[160,512]{1,0:T(8,128)(2,1)S(1)}) custom-call(s32[12]{0:T(128)S(1)} %stack.55.table, s32[4]{0:T(128)S(1)} %reshape.6.lengths, bf16[160,1536]{1,0:T(8,128)(2,1)S(1)} %get-tuple-element.103.refs_0_, bf16[160,1536]{1,0:T(8,128)(2,1)S(1)} %collective-permute-done.5.refs_1_, ...), custom_call_target="tpu_custom_call" | custom-call | flops 1 | bytes 1 | tf_op jit(solution)/shard_map/pallas_call | solution.py:309
  75.0 2.1 %collective-permute-start.15 = (bf16[160,512]{1,0:T(8,128)(2,1)S(1)}, bf16[160,512]{1,0:T(8,128)(2,1)S(1)}, u32[]{:S(2)}, u32[]{:S(2)}) collective-permute-start(bf16[160,512]{1,0:T(8,128)(2,1)S(1)} %get-tuple-element.100), channel_id=1, source_target_pairs={{0,2},{1,3},{2,0},{3,1},{4,6},{5,7},{6,4},{7,5},{8,10},{9,11},{10,... | collective-permute-start | bytes 491528 | tf_op jit(solution)/shard_map/ppermute | solution.py:409
  77.1 5.5 %shard_map.100 = (bf16[160,512]{1,0:T(8,128)(2,1)S(1)}, bf16[160,512]{1,0:T(8,128)(2,1)S(1)}) custom-call(s32[12]{0:T(128)S(1)} %stack.55.table, s32[4]{0:T(128)S(1)} %reshape.6.lengths, bf16[160,1536]{1,0:T(8,128)(2,1)S(1)} %get-tuple-element.103.refs_0_, bf16[160,1536]{1,0:T(8,128)(2,1)S(1)} %collective-permute-done.5.refs_1_, ...), custom_call_target="tpu_custom_call" | custom-call | flops 1 | bytes 1 | tf_op jit(solution)/shard_map/pallas_call | solution.py:309
  82.6 0.0 collective-permute-done.15.refs_1_
  82.7 0.1 collective-permute-start.18
  82.7 2.9 %collective-permute-start.17 = (bf16[160,512]{1,0:T(8,128)(2,1)S(1)}, bf16[160,512]{1,0:T(8,128)(2,1)S(1)}, u32[]{:S(2)}, u32[]{:S(2)}) collective-permute-start(bf16[160,512]{1,0:T(8,128)(2,1)S(1)} %get-tuple-element.112), channel_id=1, source_target_pairs={{0,4},{1,5},{2,6},{3,7},{4,0},{5,1},{6,2},{7,3},{8,12},{9,13},{10,... | collective-permute-start | bytes 491528 | tf_op jit(solution)/shard_map/ppermute | solution.py:409
  85.7 0.0 copy-done
  85.7 0.0 copy-start.1
  85.7 1.4 %shard_map.99 = (bf16[160,1024]{1,0:T(8,128)(2,1)S(1)}, bf16[160,1024]{1,0:T(8,128)(2,1)S(1)}) custom-call(s32[12]{0:T(128)S(1)} %stack.55.table, bf16[1024,2048]{1,0:T(8,128)(2,1)S(1)} %bitcast.16, bf16[160,512]{1,0:T(8,128)(2,1)S(1)} %get-tuple-element.99.refs_0_, bf16[160,512]{1,0:T(8,128)(2,1)S(1)} %collective-permute-done.15.refs_1_), custom_call_target="tpu_custom_call" | custom-call | flops 1 | bytes 1 | tf_op jit(solution)/shard_map/pallas_call | solution.py:344
  87.1 0.4 collective-permute-start.16
  87.5 1.4 %collective-permute-done.18.refs_1_ = bf16[160,512]{1,0:T(8,128)(2,1)S(1)} collective-permute-done((bf16[160,512]{1,0:T(8,128)(2,1)S(1)}, bf16[160,512]{1,0:T(8,128)(2,1)S(1)}, u32[]{:S(2)}, u32[]{:S(2)}) %collective-permute-start.18) | collective-permute-done | bytes 163872 | tf_op jit(solution)/shard_map/ppermute | solution.py:409
  88.9 1.8 %collective-permute-done.17.refs_0_ = bf16[160,512]{1,0:T(8,128)(2,1)S(1)} collective-permute-done((bf16[160,512]{1,0:T(8,128)(2,1)S(1)}, bf16[160,512]{1,0:T(8,128)(2,1)S(1)}, u32[]{:S(2)}, u32[]{:S(2)}) %collective-permute-start.17) | collective-permute-done | bytes 163872 | tf_op jit(solution)/shard_map/ppermute | solution.py:409
  90.7 1.4 %shard_map.101 = (bf16[160,1024]{1,0:T(8,128)(2,1)S(1)}, bf16[160,1024]{1,0:T(8,128)(2,1)S(1)}) custom-call(s32[12]{0:T(128)S(1)} %stack.55.table, bf16[1024,2048]{1,0:T(8,128)(2,1)S(1)} %bitcast.17, bf16[160,512]{1,0:T(8,128)(2,1)S(1)} %collective-permute-done.17.refs_0_, bf16[160,512]{1,0:T(8,128)(2,1)S(1)} %collective-permute-done.18.refs_1_), custom_call_target="tpu_custom_call" | custom-call | flops 1 | bytes 1 | tf_op jit(solution)/shard_map/pallas_call | solution.py:344
  92.1 0.4 collective-permute-start.19
  92.5 2.6 %collective-permute-done.16.beside = bf16[160,1024]{1,0:T(8,128)(2,1)S(1)} collective-permute-done((bf16[160,1024]{1,0:T(8,128)(2,1)S(1)}, bf16[160,1024]{1,0:T(8,128)(2,1)S(1)}, u32[]{:S(2)}, u32[]{:S(2)}) %collective-permute-start.16) | collective-permute-done | bytes 327712 | tf_op jit(solution)/shard_map/ppermute | solution.py:409
  95.2 4.1 %collective-permute-done.19.corner = bf16[160,1024]{1,0:T(8,128)(2,1)S(1)} collective-permute-done((bf16[160,1024]{1,0:T(8,128)(2,1)S(1)}, bf16[160,1024]{1,0:T(8,128)(2,1)S(1)}, u32[]{:S(2)}, u32[]{:S(2)}) %collective-permute-start.19) | collective-permute-done | bytes 327712 | tf_op jit(solution)/shard_map/ppermute | solution.py:409
  99.3 0.0 copy-done.1
  99.3 1.6 %shard_map.102 = bf16[1,2,160,1024]{3,2,1,0:T(8,128)(2,1)} custom-call(s32[12]{0:T(128)S(1)} %stack.55.table, bf16[1,2,160,1024]{3,2,1,0:T(8,128)(2,1)S(1)} %copy-done.1, bf16[160,1024]{1,0:T(8,128)(2,1)S(1)} %get-tuple-element.101.own, bf16[160,1024]{1,0:T(8,128)(2,1)S(1)} %collective-permute-done.16.beside, ...), custom_call_target="tpu_custom_call" | custom-call | tf_op jit(solution)/shard_map/pallas_call | solution.py:378
Async XLA Ops:
  0.0 8.2 %collective-permute-start.1 = (bf16[2,160,1024]{2,1,0:T(8,128)(2,1)}, bf16[2,160,1024]{2,1,0:T(8,128)(2,1)S(1)}, u32[]{:S(2)}, u32[]{:S(2)}) collective-permute-start(bf16[2,160,1024]{2,1,0:T(8,128)(2,1)} %bitcast.23), channel_id=1, source_target_pairs={{0,16},{1,17},{2,18},{3,19},{4,20},{5,21},{6,22},{7,23},{8,24},{9,... | collective-permute-start | bytes 1966088 | tf_op jit(solution)/shard_map/ppermute | solution.py:21
  4.2 9.6 %collective-permute-start.3 = (bf16[160,1024]{1,0:T(8,128)(2,1)S(1)}, bf16[160,1024]{1,0:T(8,128)(2,1)S(1)}, u32[]{:S(2)}, u32[]{:S(2)}) collective-permute-start(bf16[160,1024]{1,0:T(8,128)(2,1)S(1)} %get-tuple-element.65.refs_0_), channel_id=1, source_target_pairs={{0,1},{1,0},{2,3},{3,2},{4,5},{5,4},{6,7},{7,6},{8,9},{9,8},{10,11... | collective-permute-start | bytes 983048 | tf_op jit(solution)/shard_map/ppermute | solution.py:409
  6.6 15.0 %collective-permute-start = (bf16[160,1024]{1,0:T(8,128)(2,1)S(1)}, bf16[160,1024]{1,0:T(8,128)(2,1)S(1)}, u32[]{:S(2)}, u32[]{:S(2)}) collective-permute-start(bf16[160,1024]{1,0:T(8,128)(2,1)S(1)} %get-tuple-element.62), channel_id=1, source_target_pairs={{0,4},{1,5},{2,6},{3,7},{4,0},{5,1},{6,2},{7,3},{8,12},{9,13},{10,... | collective-permute-start | bytes 983048 | tf_op jit(solution)/shard_map/ppermute | solution.py:409
  9.8 13.1 %collective-permute-start.2 = (bf16[160,1024]{1,0:T(8,128)(2,1)S(1)}, bf16[160,1024]{1,0:T(8,128)(2,1)S(1)}, u32[]{:S(2)}, u32[]{:S(2)}) collective-permute-start(bf16[160,1024]{1,0:T(8,128)(2,1)S(1)} %get-tuple-element.91), channel_id=1, source_target_pairs={{16,20},{17,21},{18,22},{19,23},{20,16},{21,17},{22,18},{23,19},{2... | collective-permute-start | bytes 983048 | tf_op jit(solution)/shard_map/ppermute | solution.py:409
  10.5 13.1 %collective-permute-start.4 = (bf16[160,1024]{1,0:T(8,128)(2,1)S(1)}, bf16[160,1024]{1,0:T(8,128)(2,1)S(1)}, u32[]{:S(2)}, u32[]{:S(2)}) collective-permute-start(bf16[160,1024]{1,0:T(8,128)(2,1)S(1)} %get-tuple-element.83.refs_2_), channel_id=1, source_target_pairs={{16,17},{17,16},{18,19},{19,18},{20,21},{21,20},{22,23},{23,22},{2... | collective-permute-start | bytes 983048 | tf_op jit(solution)/shard_map/ppermute | solution.py:409
  13.8 16.5 %collective-permute-start.9 = (bf16[160,1024]{1,0:T(8,128)(2,1)S(1)}, bf16[160,1024]{1,0:T(8,128)(2,1)S(1)}, u32[]{:S(2)}, u32[]{:S(2)}) collective-permute-start(bf16[160,1024]{1,0:T(8,128)(2,1)S(1)} %get-tuple-element.83.refs_2_), channel_id=1, source_target_pairs={{0,8},{1,9},{2,10},{3,11},{4,12},{5,13},{6,14},{7,15},{8,0},{9,1},... | collective-permute-start | bytes 983048 | tf_op jit(solution)/shard_map/ppermute | solution.py:409
  21.6 14.3 %collective-permute-start.6 = (bf16[160,1024]{1,0:T(8,128)(2,1)S(1)}, bf16[160,1024]{1,0:T(8,128)(2,1)S(1)}, u32[]{:S(2)}, u32[]{:S(2)}) collective-permute-start(bf16[160,1024]{1,0:T(8,128)(2,1)S(1)} %collective-permute-done.refs_0_), channel_id=1, source_target_pairs={{0,1},{1,0},{2,3},{3,2},{4,5},{5,4},{6,7},{7,6},{8,9},{9,8},{10,11... | collective-permute-start | bytes 983048 | tf_op jit(solution)/shard_map/ppermute | solution.py:409
  22.9 13.0 %collective-permute-start.7 = (bf16[160,1024]{1,0:T(8,128)(2,1)S(1)}, bf16[160,1024]{1,0:T(8,128)(2,1)S(1)}, u32[]{:S(2)}, u32[]{:S(2)}) collective-permute-start(bf16[160,1024]{1,0:T(8,128)(2,1)S(1)} %collective-permute-done.2.refs_2_), channel_id=1, source_target_pairs={{16,17},{17,16},{18,19},{19,18},{20,21},{21,20},{22,23},{23,22},{2... | collective-permute-start | bytes 983048 | tf_op jit(solution)/shard_map/ppermute | solution.py:409
  30.3 11.3 %collective-permute-start.12 = (bf16[160,1024]{1,0:T(8,128)(2,1)S(1)}, bf16[160,1024]{1,0:T(8,128)(2,1)S(1)}, u32[]{:S(2)}, u32[]{:S(2)}) collective-permute-start(bf16[160,1024]{1,0:T(8,128)(2,1)S(1)} %get-tuple-element.91), channel_id=1, source_target_pairs={{0,12},{1,13},{2,14},{3,15},{4,8},{5,9},{6,10},{7,11},{8,4},{9,5},... | collective-permute-start | bytes 983048 | tf_op jit(solution)/shard_map/ppermute | solution.py:409
  34.4 14.2 %collective-permute-start.5 = (bf16[160,1536]{1,0:T(8,128)(2,1)S(1)}, bf16[160,1536]{1,0:T(8,128)(2,1)S(1)}, u32[]{:S(2)}, u32[]{:S(2)}) collective-permute-start(bf16[160,1536]{1,0:T(8,128)(2,1)S(1)} %get-tuple-element.74), channel_id=1, source_target_pairs={{0,2},{1,3},{2,0},{3,1},{4,6},{5,7},{6,4},{7,5},{8,10},{9,11},{10,... | collective-permute-start | bytes 1474568 | tf_op jit(solution)/shard_map/ppermute | solution.py:409
  39.7 18.5 %collective-permute-start.8 = (bf16[160,1536]{1,0:T(8,128)(2,1)S(1)}, bf16[160,1536]{1,0:T(8,128)(2,1)S(1)}, u32[]{:S(2)}, u32[]{:S(2)}) collective-permute-start(bf16[160,1536]{1,0:T(8,128)(2,1)S(1)} %get-tuple-element.82), channel_id=1, source_target_pairs={{0,2},{1,3},{2,0},{3,1},{4,6},{5,7},{6,4},{7,5},{8,10},{9,11},{10,... | collective-permute-start | bytes 1474568 | tf_op jit(solution)/shard_map/ppermute | solution.py:409
  40.3 10.7 %collective-permute-start.10 = (bf16[160,1024]{1,0:T(8,128)(2,1)S(1)}, bf16[160,1024]{1,0:T(8,128)(2,1)S(1)}, u32[]{:S(2)}, u32[]{:S(2)}) collective-permute-start(bf16[160,1024]{1,0:T(8,128)(2,1)S(1)} %collective-permute-done.9.refs_0_), channel_id=1, source_target_pairs={{0,1},{1,0},{2,3},{3,2},{4,5},{5,4},{6,7},{7,6},{8,9},{9,8},{10,11... | collective-permute-start | bytes 983048 | tf_op jit(solution)/shard_map/ppermute | solution.py:409
  41.6 16.6 %collective-permute-start.13 = (bf16[160,1024]{1,0:T(8,128)(2,1)S(1)}, bf16[160,1024]{1,0:T(8,128)(2,1)S(1)}, u32[]{:S(2)}, u32[]{:S(2)}) collective-permute-start(bf16[160,1024]{1,0:T(8,128)(2,1)S(1)} %collective-permute-done.12.refs_0_), channel_id=1, source_target_pairs={{0,1},{1,0},{2,3},{3,2},{4,5},{5,4},{6,7},{7,6},{8,9},{9,8},{10,11... | collective-permute-start | bytes 983048 | tf_op jit(solution)/shard_map/ppermute | solution.py:409
  54.4 10.8 %collective-permute-start.11 = (bf16[160,1024]{1,0:T(8,128)(2,1)}, bf16[160,1024]{1,0:T(8,128)(2,1)S(1)}, u32[]{:S(2)}, u32[]{:S(2)}) collective-permute-start(bf16[160,1024]{1,0:T(8,128)(2,1)} %get-tuple-element.90), channel_id=1, source_target_pairs={{0,2},{1,3},{2,0},{3,1},{4,6},{5,7},{6,4},{7,5},{8,10},{9,11},{10,... | collective-permute-start | bytes 983048 | tf_op jit(solution)/shard_map/ppermute | solution.py:409
  58.2 6.1 %copy-start.2 = (s32[1,2,2]{2,1,0:T(2,128)S(1)}, s32[1,2,2]{2,1,0:T(2,128)}, u32[]{:S(2)}) copy-start(s32[1,2,2]{2,1,0:T(2,128)} %param.17) | copy-start | bytes 52
  61.9 7.6 %collective-permute-start.14 = (bf16[160,1024]{1,0:T(8,128)(2,1)}, bf16[160,1024]{1,0:T(8,128)(2,1)S(1)}, u32[]{:S(2)}, u32[]{:S(2)}) collective-permute-start(bf16[160,1024]{1,0:T(8,128)(2,1)} %get-tuple-element.98), channel_id=1, source_target_pairs={{0,2},{1,3},{2,0},{3,1},{4,6},{5,7},{6,4},{7,5},{8,10},{9,11},{10,... | collective-permute-start | bytes 983048 | tf_op jit(solution)/shard_map/ppermute | solution.py:409
  64.3 21.3 %copy-start = (bf16[1,1024,2048]{2,1,0:T(8,128)(2,1)S(1)}, bf16[1,1024,2048]{2,1,0:T(8,128)(2,1)}, u32[]{:S(2)}) copy-start(bf16[1,1024,2048]{2,1,0:T(8,128)(2,1)} %param.14) | copy-start | bytes 12582916
  75.0 7.6 %collective-permute-start.15 = (bf16[160,512]{1,0:T(8,128)(2,1)S(1)}, bf16[160,512]{1,0:T(8,128)(2,1)S(1)}, u32[]{:S(2)}, u32[]{:S(2)}) collective-permute-start(bf16[160,512]{1,0:T(8,128)(2,1)S(1)} %get-tuple-element.100), channel_id=1, source_target_pairs={{0,2},{1,3},{2,0},{3,1},{4,6},{5,7},{6,4},{7,5},{8,10},{9,11},{10,... | collective-permute-start | bytes 491528 | tf_op jit(solution)/shard_map/ppermute | solution.py:409
  82.7 6.3 %collective-permute-start.18 = (bf16[160,512]{1,0:T(8,128)(2,1)S(1)}, bf16[160,512]{1,0:T(8,128)(2,1)S(1)}, u32[]{:S(2)}, u32[]{:S(2)}) collective-permute-start(bf16[160,512]{1,0:T(8,128)(2,1)S(1)} %get-tuple-element.114), channel_id=1, source_target_pairs={{0,6},{1,7},{2,4},{3,5},{4,2},{5,3},{6,0},{7,1},{8,14},{9,15},{10,... | collective-permute-start | bytes 491528 | tf_op jit(solution)/shard_map/ppermute | solution.py:409
  82.7 8.0 %collective-permute-start.17 = (bf16[160,512]{1,0:T(8,128)(2,1)S(1)}, bf16[160,512]{1,0:T(8,128)(2,1)S(1)}, u32[]{:S(2)}, u32[]{:S(2)}) collective-permute-start(bf16[160,512]{1,0:T(8,128)(2,1)S(1)} %get-tuple-element.112), channel_id=1, source_target_pairs={{0,4},{1,5},{2,6},{3,7},{4,0},{5,1},{6,2},{7,3},{8,12},{9,13},{10,... | collective-permute-start | bytes 491528 | tf_op jit(solution)/shard_map/ppermute | solution.py:409
  85.7 13.6 %copy-start.1 = (bf16[1,2,160,1024]{3,2,1,0:T(8,128)(2,1)S(1)}, bf16[1,2,160,1024]{3,2,1,0:T(8,128)(2,1)}, u32[]{:S(2)}) copy-start(bf16[1,2,160,1024]{3,2,1,0:T(8,128)(2,1)} %hidden.5) | copy-start | bytes 1966084
  87.1 8.1 %collective-permute-start.16 = (bf16[160,1024]{1,0:T(8,128)(2,1)S(1)}, bf16[160,1024]{1,0:T(8,128)(2,1)S(1)}, u32[]{:S(2)}, u32[]{:S(2)}) collective-permute-start(bf16[160,1024]{1,0:T(8,128)(2,1)S(1)} %get-tuple-element.102), channel_id=1, source_target_pairs={{0,1},{1,0},{2,3},{3,2},{4,5},{5,4},{6,7},{7,6},{8,9},{9,8},{10,11... | collective-permute-start | bytes 983048 | tf_op jit(solution)/shard_map/ppermute | solution.py:409
  92.1 7.1 %collective-permute-start.19 = (bf16[160,1024]{1,0:T(8,128)(2,1)S(1)}, bf16[160,1024]{1,0:T(8,128)(2,1)S(1)}, u32[]{:S(2)}, u32[]{:S(2)}) collective-permute-start(bf16[160,1024]{1,0:T(8,128)(2,1)S(1)} %get-tuple-element.116), channel_id=1, source_target_pairs={{0,1},{1,0},{2,3},{3,2},{4,5},{5,4},{6,7},{7,6},{8,9},{9,8},{10,11... | collective-permute-start | bytes 983048 | tf_op jit(solution)/shard_map/ppermute | solution.py:409

commit v7 on v6

--- a/solution.py
+++ b/solution.py
@@ -437,7 +437,7 @@
         (kept, sent), held[0] = project(table, parts, gains, held[0], 2)
         return kept, moved(sent, 1, 0)
 
-    done = {0: projected(0, query[2], source[2])}
+    done = {0: projected(0)}
     before = done[0][0]
     if seq > 4:
         source[4] = after(source[4], before)

time: 101 us -> 101 us (level)
  no operation moved by 1% of the time
where the time goes in v7:
time: 101 us
  Pallas kernels  38.2 us (38%)
  waiting for transfers between devices  31.7 us (31%)
  starting transfers between devices  30.5 us (30%)
    ppermute x19, waiting for transfers between devices, moved(): return lax.ppermute(value, ('segment', 'seq', 'mp'), pairs)  31.7 us
    ppermute x19, starting transfers between devices, moved(): return lax.ppermute(value, ('segment', 'seq', 'mp'), pairs)  28.1 us
    pallas_call x4, Pallas kernels, project(): pl.pallas_call(functools.partial(project_kernel, count, queried), out_sha...  14.8 us
    pallas_call x2, Pallas kernels, attend(): pl.pallas_call(functools.partial(attend_kernel, chosen, size, len(arrays)...  11 us
    pallas_call x1, Pallas kernels, fetch(): pl.pallas_call(functools.partial(fetch_kernel, len(weights)), out_shape=[...  4.68 us
    pallas_call x2, Pallas kernels, split(): pl.pallas_call(kernel, out_shape=[jax.ShapeDtypeStruct(hidden.shape[2:],...  3.27 us
    pallas_call x2, Pallas kernels, output_parts(): pl.pallas_call(functools.partial(output_kernel, len(pieces)), out_shape=[...  2.82 us
    ppermute x1, starting transfers between devices, passed_along(): lax.ppermute(value, axis, [(source, source + steps) for source in range(l...  2.39 us
  transfers between devices with their start and end apart: 20, of which 12 were waited for; matrix products, arithmetic and copies ran while one was open for 0% of the time, Pallas kernels for 31%

profile of v7, /device:TPU:0, one launch (start us, length us, event | category | flops | bytes accessed | tf_op | source)
XLA Modules:
  0.0 100.8 jit_solution(16566678381635349008)
XLA Ops:
  0.0 2.4 %collective-permute-start.1 = (bf16[2,160,1024]{2,1,0:T(8,128)(2,1)}, bf16[2,160,1024]{2,1,0:T(8,128)(2,1)S(1)}, u32[]{:S(2)}, u32[]{:S(2)}) collective-permute-start(bf16[2,160,1024]{2,1,0:T(8,128)(2,1)} %bitcast.23), channel_id=1, source_target_pairs={{0,16},{1,17},{2,18},{3,19},{4,20},{5,21},{6,22},{7,23},{8,24},{9,... | collective-permute-start | bytes 1966088 | tf_op jit(solution)/shard_map/ppermute | solution.py:21
  2.4 0.1 stack.55.table
  2.5 1.6 %shard_map.91 = (bf16[160,1024]{1,0:T(8,128)(2,1)S(1)}, bf16[160,1024]{1,0:T(8,128)(2,1)S(1)}) custom-call(s32[12]{0:T(128)S(1)} %stack.55.table, bf16[1,2,160,1024]{3,2,1,0:T(8,128)(2,1)} %hidden.5), custom_call_target="tpu_custom_call" | custom-call | flops 1 | bytes 1 | tf_op jit(solution)/shard_map/pallas_call | solution.py:130
  4.2 2.4 %collective-permute-start = (bf16[160,1024]{1,0:T(8,128)(2,1)S(1)}, bf16[160,1024]{1,0:T(8,128)(2,1)S(1)}, u32[]{:S(2)}, u32[]{:S(2)}) collective-permute-start(bf16[160,1024]{1,0:T(8,128)(2,1)S(1)} %get-tuple-element.60.refs_0_), channel_id=1, source_target_pairs={{0,1},{1,0},{2,3},{3,2},{4,5},{5,4},{6,7},{7,6},{8,9},{9,8},{10,11... | collective-permute-start | bytes 983048 | tf_op jit(solution)/shard_map/ppermute | solution.py:409
  6.6 1.6 %collective-permute-start.4 = (bf16[160,1024]{1,0:T(8,128)(2,1)S(1)}, bf16[160,1024]{1,0:T(8,128)(2,1)S(1)}, u32[]{:S(2)}, u32[]{:S(2)}) collective-permute-start(bf16[160,1024]{1,0:T(8,128)(2,1)S(1)} %get-tuple-element.71), channel_id=1, source_target_pairs={{0,4},{1,5},{2,6},{3,7},{4,0},{5,1},{6,2},{7,3},{8,12},{9,13},{10,... | collective-permute-start | bytes 983048 | tf_op jit(solution)/shard_map/ppermute | solution.py:409
  8.2 0.0 collective-permute-done.1
  8.2 1.6 %shard_map.92 = (bf16[160,1024]{1,0:T(8,128)(2,1)S(1)}, bf16[160,1024]{1,0:T(8,128)(2,1)S(1)}) custom-call(s32[12]{0:T(128)S(1)} %stack.55.table, bf16[1,2,160,1024]{3,2,1,0:T(8,128)(2,1)} %hidden.5, bf16[1,2,160,1024]{3,2,1,0:T(8,128)(2,1)S(1)} %bitcast.18), custom_call_target="tpu_custom_call" | custom-call | flops 1 | bytes 1 | tf_op jit(solution)/shard_map/pallas_call | solution.py:130
  9.8 0.7 collective-permute-start.6
  10.5 0.7 collective-permute-start.2
  11.2 2.6 %collective-permute-done.refs_1_ = bf16[160,1024]{1,0:T(8,128)(2,1)S(1)} collective-permute-done((bf16[160,1024]{1,0:T(8,128)(2,1)S(1)}, bf16[160,1024]{1,0:T(8,128)(2,1)S(1)}, u32[]{:S(2)}, u32[]{:S(2)}) %collective-permute-start) | collective-permute-done | bytes 327712 | tf_op jit(solution)/shard_map/ppermute | solution.py:409
  13.8 2.8 %collective-permute-start.9 = (bf16[160,1024]{1,0:T(8,128)(2,1)S(1)}, bf16[160,1024]{1,0:T(8,128)(2,1)S(1)}, u32[]{:S(2)}, u32[]{:S(2)}) collective-permute-start(bf16[160,1024]{1,0:T(8,128)(2,1)S(1)} %get-tuple-element.81.refs_2_), channel_id=1, source_target_pairs={{0,8},{1,9},{2,10},{3,11},{4,12},{5,13},{6,14},{7,15},{8,0},{9,1},... | collective-permute-start | bytes 983048 | tf_op jit(solution)/shard_map/ppermute | solution.py:409
  16.6 4.7 %shard_map.93 = (bf16[2048,1024]{1,0:T(8,128)(2,1)S(1)}, bf16[2048,1024]{1,0:T(8,128)(2,1)S(1)}, bf16[2048,1024]{1,0:T(8,128)(2,1)S(1)}) custom-call(bf16[1,2048,1024]{2,1,0:T(8,128)(2,1)} %refs_0_, bf16[1,2048,1024]{2,1,0:T(8,128)(2,1)} %refs_1_, bf16[1,2048,1024]{2,1,0:T(8,128)(2,1)} %refs_2_.2), custom_call_target="tpu_custom_call" | custom-call | flops 1 | bytes 1 | tf_op jit(solution)/shard_map/pallas_call | solution.py:166
  21.3 0.2 collective-permute-done.4.refs_0_
  21.6 1.4 %collective-permute-start.5 = (bf16[160,1024]{1,0:T(8,128)(2,1)S(1)}, bf16[160,1024]{1,0:T(8,128)(2,1)S(1)}, u32[]{:S(2)}, u32[]{:S(2)}) collective-permute-start(bf16[160,1024]{1,0:T(8,128)(2,1)S(1)} %collective-permute-done.4.refs_0_), channel_id=1, source_target_pairs={{0,1},{1,0},{2,3},{3,2},{4,5},{5,4},{6,7},{7,6},{8,9},{9,8},{10,11... | collective-permute-start | bytes 983048 | tf_op jit(solution)/shard_map/ppermute | solution.py:409
  22.9 0.0 collective-permute-done.6.refs_2_
  22.9 0.7 collective-permute-start.7
  23.6 0.0 collective-permute-done.2.refs_3_
  23.6 3.8 %shard_map.94 = (bf16[160,1536]{1,0:T(8,128)(2,1)S(1)}, bf16[160,1536]{1,0:T(8,128)(2,1)S(1)}, bf16[2048,1024]{1,0:T(8,128)(2,1)S(1)}, bf16[2048,1024]{1,0:T(8,128)(2,1)S(1)}, bf16[2048,1024]{1,0:T(8,128)(2,1)S(1)}) custom-call(s32[12]{0:T(128)S(1)} %stack.55.table, ...), custom_call_target="tpu_custom_call", output_to_operand_aliasing={{2}: (7, {}), {3}: (8, {}), {4}: (9, {})} | custom-call | flops 1 | bytes 1 | tf_op jit(solution)/shard_map/pallas_call | solution.py:228
  27.4 2.8 %collective-permute-done.9.refs_0_ = bf16[160,1024]{1,0:T(8,128)(2,1)S(1)} collective-permute-done((bf16[160,1024]{1,0:T(8,128)(2,1)S(1)}, bf16[160,1024]{1,0:T(8,128)(2,1)S(1)}, u32[]{:S(2)}, u32[]{:S(2)}) %collective-permute-start.9) | collective-permute-done | bytes 327712 | tf_op jit(solution)/shard_map/ppermute | solution.py:409
  30.3 4.1 %collective-permute-start.12 = (bf16[160,1024]{1,0:T(8,128)(2,1)S(1)}, bf16[160,1024]{1,0:T(8,128)(2,1)S(1)}, u32[]{:S(2)}, u32[]{:S(2)}) collective-permute-start(bf16[160,1024]{1,0:T(8,128)(2,1)S(1)} %get-tuple-element.89), channel_id=1, source_target_pairs={{0,12},{1,13},{2,14},{3,15},{4,8},{5,9},{6,10},{7,11},{8,4},{9,5},... | collective-permute-start | bytes 983048 | tf_op jit(solution)/shard_map/ppermute | solution.py:409
  34.4 1.5 %collective-permute-start.3 = (bf16[160,1536]{1,0:T(8,128)(2,1)S(1)}, bf16[160,1536]{1,0:T(8,128)(2,1)S(1)}, u32[]{:S(2)}, u32[]{:S(2)}) collective-permute-start(bf16[160,1536]{1,0:T(8,128)(2,1)S(1)} %get-tuple-element.70), channel_id=1, source_target_pairs={{0,2},{1,3},{2,0},{3,1},{4,6},{5,7},{6,4},{7,5},{8,10},{9,11},{10,... | collective-permute-start | bytes 1474568 | tf_op jit(solution)/shard_map/ppermute | solution.py:409
  35.9 0.0 collective-permute-done.5.refs_1_
  35.9 0.0 collective-permute-done.7.refs_3_
  35.9 3.8 %shard_map.95 = (bf16[160,1536]{1,0:T(8,128)(2,1)S(1)}, bf16[160,1536]{1,0:T(8,128)(2,1)S(1)}, bf16[2048,1024]{1,0:T(8,128)(2,1)S(1)}, bf16[2048,1024]{1,0:T(8,128)(2,1)S(1)}, bf16[2048,1024]{1,0:T(8,128)(2,1)S(1)}) custom-call(s32[12]{0:T(128)S(1)} %stack.55.table, ...), custom_call_target="tpu_custom_call", output_to_operand_aliasing={{2}: (7, {}), {3}: (8, {}), {4}: (9, {})} | custom-call | flops 1 | bytes 1 | tf_op jit(solution)/shard_map/pallas_call | solution.py:228
  39.7 0.6 collective-permute-start.8
  40.3 1.3 %collective-permute-start.10 = (bf16[160,1024]{1,0:T(8,128)(2,1)S(1)}, bf16[160,1024]{1,0:T(8,128)(2,1)S(1)}, u32[]{:S(2)}, u32[]{:S(2)}) collective-permute-start(bf16[160,1024]{1,0:T(8,128)(2,1)S(1)} %collective-permute-done.9.refs_0_), channel_id=1, source_target_pairs={{0,1},{1,0},{2,3},{3,2},{4,5},{5,4},{6,7},{7,6},{8,9},{9,8},{10,11... | collective-permute-start | bytes 983048 | tf_op jit(solution)/shard_map/ppermute | solution.py:409
  41.6 0.0 collective-permute-done.12.refs_0_
  41.6 1.3 %collective-permute-start.13 = (bf16[160,1024]{1,0:T(8,128)(2,1)S(1)}, bf16[160,1024]{1,0:T(8,128)(2,1)S(1)}, u32[]{:S(2)}, u32[]{:S(2)}) collective-permute-start(bf16[160,1024]{1,0:T(8,128)(2,1)S(1)} %collective-permute-done.12.refs_0_), channel_id=1, source_target_pairs={{0,1},{1,0},{2,3},{3,2},{4,5},{5,4},{6,7},{7,6},{8,9},{9,8},{10,11... | collective-permute-start | bytes 983048 | tf_op jit(solution)/shard_map/ppermute | solution.py:409
  42.9 5.6 %collective-permute-done.3.refs_1_ = bf16[160,1536]{1,0:T(8,128)(2,1)S(1)} collective-permute-done((bf16[160,1536]{1,0:T(8,128)(2,1)S(1)}, bf16[160,1536]{1,0:T(8,128)(2,1)S(1)}, u32[]{:S(2)}, u32[]{:S(2)}) %collective-permute-start.3) | collective-permute-done | bytes 491552 | tf_op jit(solution)/shard_map/ppermute | solution.py:409
  48.5 2.4 %collective-permute-done.10.refs_1_ = bf16[160,1024]{1,0:T(8,128)(2,1)S(1)} collective-permute-done((bf16[160,1024]{1,0:T(8,128)(2,1)S(1)}, bf16[160,1024]{1,0:T(8,128)(2,1)S(1)}, u32[]{:S(2)}, u32[]{:S(2)}) %collective-permute-start.10) | collective-permute-done | bytes 327712 | tf_op jit(solution)/shard_map/ppermute | solution.py:409
  50.9 3.5 %shard_map.96 = (bf16[160,1024]{1,0:T(8,128)(2,1)S(1)}, bf16[160,1024]{1,0:T(8,128)(2,1)}, bf16[2048,1024]{1,0:T(8,128)(2,1)S(1)}, bf16[2048,1024]{1,0:T(8,128)(2,1)S(1)}, bf16[2048,1024]{1,0:T(8,128)(2,1)S(1)}) custom-call(s32[12]{0:T(128)S(1)} %stack.55.table, ...), custom_call_target="tpu_custom_call", output_to_operand_aliasing={{2}: (5, {}), {3}: (6, {}), {4}: (7, {})} | custom-call | flops 1 | bytes 1 | tf_op jit(solution)/shard_map/pallas_call | solution.py:228
  54.4 0.9 collective-permute-start.11
  55.3 2.9 %collective-permute-done.8.refs_3_ = bf16[160,1536]{1,0:T(8,128)(2,1)S(1)} collective-permute-done((bf16[160,1536]{1,0:T(8,128)(2,1)S(1)}, bf16[160,1536]{1,0:T(8,128)(2,1)S(1)}, u32[]{:S(2)}, u32[]{:S(2)}) %collective-permute-start.8) | collective-permute-done | bytes 491552 | tf_op jit(solution)/shard_map/ppermute | solution.py:409
  58.2 0.0 collective-permute-done.13.refs_1_
  58.2 0.0 copy-start.2
  58.2 3.7 %shard_map.97 = (bf16[160,1024]{1,0:T(8,128)(2,1)S(1)}, bf16[160,1024]{1,0:T(8,128)(2,1)}, bf16[2048,1024]{1,0:T(8,128)(2,1)S(1)}, bf16[2048,1024]{1,0:T(8,128)(2,1)S(1)}, bf16[2048,1024]{1,0:T(8,128)(2,1)S(1)}) custom-call(s32[12]{0:T(128)S(1)} %stack.55.table, ...), custom_call_target="tpu_custom_call", output_to_operand_aliasing={{2}: (5, {}), {3}: (6, {}), {4}: (7, {})} | custom-call | flops 1 | bytes 1 | tf_op jit(solution)/shard_map/pallas_call | solution.py:228
  61.9 2.4 %collective-permute-start.14 = (bf16[160,1024]{1,0:T(8,128)(2,1)}, bf16[160,1024]{1,0:T(8,128)(2,1)S(1)}, u32[]{:S(2)}, u32[]{:S(2)}) collective-permute-start(bf16[160,1024]{1,0:T(8,128)(2,1)} %get-tuple-element.96), channel_id=1, source_target_pairs={{0,2},{1,3},{2,0},{3,1},{4,6},{5,7},{6,4},{7,5},{8,10},{9,11},{10,... | collective-permute-start | bytes 983048 | tf_op jit(solution)/shard_map/ppermute | solution.py:409
  64.2 0.0 copy-done.2
  64.2 0.1 reshape.6.lengths
  64.3 0.0 copy-start
  64.3 0.9 collective-permute-done.11.refs_5_
  65.2 4.3 %collective-permute-done.14.refs_7_ = bf16[160,1024]{1,0:T(8,128)(2,1)S(1)} collective-permute-done((bf16[160,1024]{1,0:T(8,128)(2,1)}, bf16[160,1024]{1,0:T(8,128)(2,1)S(1)}, u32[]{:S(2)}, u32[]{:S(2)}) %collective-permute-start.14) | collective-permute-done | bytes 327712 | tf_op jit(solution)/shard_map/ppermute | solution.py:409
  69.5 5.5 %shard_map.98 = (bf16[160,512]{1,0:T(8,128)(2,1)S(1)}, bf16[160,512]{1,0:T(8,128)(2,1)S(1)}) custom-call(s32[12]{0:T(128)S(1)} %stack.55.table, s32[4]{0:T(128)S(1)} %reshape.6.lengths, bf16[160,1536]{1,0:T(8,128)(2,1)S(1)} %get-tuple-element.101.refs_0_, bf16[160,1536]{1,0:T(8,128)(2,1)S(1)} %collective-permute-done.3.refs_1_, ...), custom_call_target="tpu_custom_call" | custom-call | flops 1 | bytes 1 | tf_op jit(solution)/shard_map/pallas_call | solution.py:309
  75.0 2.1 %collective-permute-start.15 = (bf16[160,512]{1,0:T(8,128)(2,1)S(1)}, bf16[160,512]{1,0:T(8,128)(2,1)S(1)}, u32[]{:S(2)}, u32[]{:S(2)}) collective-permute-start(bf16[160,512]{1,0:T(8,128)(2,1)S(1)} %get-tuple-element.98), channel_id=1, source_target_pairs={{0,2},{1,3},{2,0},{3,1},{4,6},{5,7},{6,4},{7,5},{8,10},{9,11},{10,... | collective-permute-start | bytes 491528 | tf_op jit(solution)/shard_map/ppermute | solution.py:409
  77.1 5.5 %shard_map.100 = (bf16[160,512]{1,0:T(8,128)(2,1)S(1)}, bf16[160,512]{1,0:T(8,128)(2,1)S(1)}) custom-call(s32[12]{0:T(128)S(1)} %stack.55.table, s32[4]{0:T(128)S(1)} %reshape.6.lengths, bf16[160,1536]{1,0:T(8,128)(2,1)S(1)} %get-tuple-element.101.refs_0_, bf16[160,1536]{1,0:T(8,128)(2,1)S(1)} %collective-permute-done.3.refs_1_, ...), custom_call_target="tpu_custom_call" | custom-call | flops 1 | bytes 1 | tf_op jit(solution)/shard_map/pallas_call | solution.py:309
  82.6 0.0 collective-permute-done.15.refs_1_
  82.7 0.1 collective-permute-start.18
  82.7 2.9 %collective-permute-start.17 = (bf16[160,512]{1,0:T(8,128)(2,1)S(1)}, bf16[160,512]{1,0:T(8,128)(2,1)S(1)}, u32[]{:S(2)}, u32[]{:S(2)}) collective-permute-start(bf16[160,512]{1,0:T(8,128)(2,1)S(1)} %get-tuple-element.110), channel_id=1, source_target_pairs={{0,4},{1,5},{2,6},{3,7},{4,0},{5,1},{6,2},{7,3},{8,12},{9,13},{10,... | collective-permute-start | bytes 491528 | tf_op jit(solution)/shard_map/ppermute | solution.py:409
  85.7 0.0 copy-done
  85.7 0.0 copy-start.1
  85.7 1.4 %shard_map.99 = (bf16[160,1024]{1,0:T(8,128)(2,1)S(1)}, bf16[160,1024]{1,0:T(8,128)(2,1)S(1)}) custom-call(s32[12]{0:T(128)S(1)} %stack.55.table, bf16[1024,2048]{1,0:T(8,128)(2,1)S(1)} %bitcast.16, bf16[160,512]{1,0:T(8,128)(2,1)S(1)} %get-tuple-element.97.refs_0_, bf16[160,512]{1,0:T(8,128)(2,1)S(1)} %collective-permute-done.15.refs_1_), custom_call_target="tpu_custom_call" | custom-call | flops 1 | bytes 1 | tf_op jit(solution)/shard_map/pallas_call | solution.py:344
  87.1 0.4 collective-permute-start.16
  87.5 1.4 %collective-permute-done.18.refs_1_ = bf16[160,512]{1,0:T(8,128)(2,1)S(1)} collective-permute-done((bf16[160,512]{1,0:T(8,128)(2,1)S(1)}, bf16[160,512]{1,0:T(8,128)(2,1)S(1)}, u32[]{:S(2)}, u32[]{:S(2)}) %collective-permute-start.18) | collective-permute-done | bytes 163872 | tf_op jit(solution)/shard_map/ppermute | solution.py:409
  88.9 1.8 %collective-permute-done.17.refs_0_ = bf16[160,512]{1,0:T(8,128)(2,1)S(1)} collective-permute-done((bf16[160,512]{1,0:T(8,128)(2,1)S(1)}, bf16[160,512]{1,0:T(8,128)(2,1)S(1)}, u32[]{:S(2)}, u32[]{:S(2)}) %collective-permute-start.17) | collective-permute-done | bytes 163872 | tf_op jit(solution)/shard_map/ppermute | solution.py:409
  90.7 1.4 %shard_map.101 = (bf16[160,1024]{1,0:T(8,128)(2,1)S(1)}, bf16[160,1024]{1,0:T(8,128)(2,1)S(1)}) custom-call(s32[12]{0:T(128)S(1)} %stack.55.table, bf16[1024,2048]{1,0:T(8,128)(2,1)S(1)} %bitcast.17, bf16[160,512]{1,0:T(8,128)(2,1)S(1)} %collective-permute-done.17.refs_0_, bf16[160,512]{1,0:T(8,128)(2,1)S(1)} %collective-permute-done.18.refs_1_), custom_call_target="tpu_custom_call" | custom-call | flops 1 | bytes 1 | tf_op jit(solution)/shard_map/pallas_call | solution.py:344
  92.1 0.4 collective-permute-start.19
  92.5 2.6 %collective-permute-done.16.beside = bf16[160,1024]{1,0:T(8,128)(2,1)S(1)} collective-permute-done((bf16[160,1024]{1,0:T(8,128)(2,1)S(1)}, bf16[160,1024]{1,0:T(8,128)(2,1)S(1)}, u32[]{:S(2)}, u32[]{:S(2)}) %collective-permute-start.16) | collective-permute-done | bytes 327712 | tf_op jit(solution)/shard_map/ppermute | solution.py:409
  95.2 4.1 %collective-permute-done.19.corner = bf16[160,1024]{1,0:T(8,128)(2,1)S(1)} collective-permute-done((bf16[160,1024]{1,0:T(8,128)(2,1)S(1)}, bf16[160,1024]{1,0:T(8,128)(2,1)S(1)}, u32[]{:S(2)}, u32[]{:S(2)}) %collective-permute-start.19) | collective-permute-done | bytes 327712 | tf_op jit(solution)/shard_map/ppermute | solution.py:409
  99.3 0.0 copy-done.1
  99.3 1.6 %shard_map.102 = bf16[1,2,160,1024]{3,2,1,0:T(8,128)(2,1)} custom-call(s32[12]{0:T(128)S(1)} %stack.55.table, bf16[1,2,160,1024]{3,2,1,0:T(8,128)(2,1)S(1)} %copy-done.1, bf16[160,1024]{1,0:T(8,128)(2,1)S(1)} %get-tuple-element.99.own, bf16[160,1024]{1,0:T(8,128)(2,1)S(1)} %collective-permute-done.16.beside, ...), custom_call_target="tpu_custom_call" | custom-call | tf_op jit(solution)/shard_map/pallas_call | solution.py:378
Async XLA Ops:
  0.0 8.2 %collective-permute-start.1 = (bf16[2,160,1024]{2,1,0:T(8,128)(2,1)}, bf16[2,160,1024]{2,1,0:T(8,128)(2,1)S(1)}, u32[]{:S(2)}, u32[]{:S(2)}) collective-permute-start(bf16[2,160,1024]{2,1,0:T(8,128)(2,1)} %bitcast.23), channel_id=1, source_target_pairs={{0,16},{1,17},{2,18},{3,19},{4,20},{5,21},{6,22},{7,23},{8,24},{9,... | collective-permute-start | bytes 1966088 | tf_op jit(solution)/shard_map/ppermute | solution.py:21
  4.2 9.6 %collective-permute-start = (bf16[160,1024]{1,0:T(8,128)(2,1)S(1)}, bf16[160,1024]{1,0:T(8,128)(2,1)S(1)}, u32[]{:S(2)}, u32[]{:S(2)}) collective-permute-start(bf16[160,1024]{1,0:T(8,128)(2,1)S(1)} %get-tuple-element.60.refs_0_), channel_id=1, source_target_pairs={{0,1},{1,0},{2,3},{3,2},{4,5},{5,4},{6,7},{7,6},{8,9},{9,8},{10,11... | collective-permute-start | bytes 983048 | tf_op jit(solution)/shard_map/ppermute | solution.py:409
  6.6 15.0 %collective-permute-start.4 = (bf16[160,1024]{1,0:T(8,128)(2,1)S(1)}, bf16[160,1024]{1,0:T(8,128)(2,1)S(1)}, u32[]{:S(2)}, u32[]{:S(2)}) collective-permute-start(bf16[160,1024]{1,0:T(8,128)(2,1)S(1)} %get-tuple-element.71), channel_id=1, source_target_pairs={{0,4},{1,5},{2,6},{3,7},{4,0},{5,1},{6,2},{7,3},{8,12},{9,13},{10,... | collective-permute-start | bytes 983048 | tf_op jit(solution)/shard_map/ppermute | solution.py:409
  9.8 13.1 %collective-permute-start.6 = (bf16[160,1024]{1,0:T(8,128)(2,1)S(1)}, bf16[160,1024]{1,0:T(8,128)(2,1)S(1)}, u32[]{:S(2)}, u32[]{:S(2)}) collective-permute-start(bf16[160,1024]{1,0:T(8,128)(2,1)S(1)} %get-tuple-element.89), channel_id=1, source_target_pairs={{16,20},{17,21},{18,22},{19,23},{20,16},{21,17},{22,18},{23,19},{2... | collective-permute-start | bytes 983048 | tf_op jit(solution)/shard_map/ppermute | solution.py:409
  10.5 13.1 %collective-permute-start.2 = (bf16[160,1024]{1,0:T(8,128)(2,1)S(1)}, bf16[160,1024]{1,0:T(8,128)(2,1)S(1)}, u32[]{:S(2)}, u32[]{:S(2)}) collective-permute-start(bf16[160,1024]{1,0:T(8,128)(2,1)S(1)} %get-tuple-element.81.refs_2_), channel_id=1, source_target_pairs={{16,17},{17,16},{18,19},{19,18},{20,21},{21,20},{22,23},{23,22},{2... | collective-permute-start | bytes 983048 | tf_op jit(solution)/shard_map/ppermute | solution.py:409
  13.8 16.5 %collective-permute-start.9 = (bf16[160,1024]{1,0:T(8,128)(2,1)S(1)}, bf16[160,1024]{1,0:T(8,128)(2,1)S(1)}, u32[]{:S(2)}, u32[]{:S(2)}) collective-permute-start(bf16[160,1024]{1,0:T(8,128)(2,1)S(1)} %get-tuple-element.81.refs_2_), channel_id=1, source_target_pairs={{0,8},{1,9},{2,10},{3,11},{4,12},{5,13},{6,14},{7,15},{8,0},{9,1},... | collective-permute-start | bytes 983048 | tf_op jit(solution)/shard_map/ppermute | solution.py:409
  21.6 14.3 %collective-permute-start.5 = (bf16[160,1024]{1,0:T(8,128)(2,1)S(1)}, bf16[160,1024]{1,0:T(8,128)(2,1)S(1)}, u32[]{:S(2)}, u32[]{:S(2)}) collective-permute-start(bf16[160,1024]{1,0:T(8,128)(2,1)S(1)} %collective-permute-done.4.refs_0_), channel_id=1, source_target_pairs={{0,1},{1,0},{2,3},{3,2},{4,5},{5,4},{6,7},{7,6},{8,9},{9,8},{10,11... | collective-permute-start | bytes 983048 | tf_op jit(solution)/shard_map/ppermute | solution.py:409
  22.9 13.0 %collective-permute-start.7 = (bf16[160,1024]{1,0:T(8,128)(2,1)S(1)}, bf16[160,1024]{1,0:T(8,128)(2,1)S(1)}, u32[]{:S(2)}, u32[]{:S(2)}) collective-permute-start(bf16[160,1024]{1,0:T(8,128)(2,1)S(1)} %collective-permute-done.6.refs_2_), channel_id=1, source_target_pairs={{16,17},{17,16},{18,19},{19,18},{20,21},{21,20},{22,23},{23,22},{2... | collective-permute-start | bytes 983048 | tf_op jit(solution)/shard_map/ppermute | solution.py:409
  30.3 11.3 %collective-permute-start.12 = (bf16[160,1024]{1,0:T(8,128)(2,1)S(1)}, bf16[160,1024]{1,0:T(8,128)(2,1)S(1)}, u32[]{:S(2)}, u32[]{:S(2)}) collective-permute-start(bf16[160,1024]{1,0:T(8,128)(2,1)S(1)} %get-tuple-element.89), channel_id=1, source_target_pairs={{0,12},{1,13},{2,14},{3,15},{4,8},{5,9},{6,10},{7,11},{8,4},{9,5},... | collective-permute-start | bytes 983048 | tf_op jit(solution)/shard_map/ppermute | solution.py:409
  34.4 14.2 %collective-permute-start.3 = (bf16[160,1536]{1,0:T(8,128)(2,1)S(1)}, bf16[160,1536]{1,0:T(8,128)(2,1)S(1)}, u32[]{:S(2)}, u32[]{:S(2)}) collective-permute-start(bf16[160,1536]{1,0:T(8,128)(2,1)S(1)} %get-tuple-element.70), channel_id=1, source_target_pairs={{0,2},{1,3},{2,0},{3,1},{4,6},{5,7},{6,4},{7,5},{8,10},{9,11},{10,... | collective-permute-start | bytes 1474568 | tf_op jit(solution)/shard_map/ppermute | solution.py:409
  39.7 18.5 %collective-permute-start.8 = (bf16[160,1536]{1,0:T(8,128)(2,1)S(1)}, bf16[160,1536]{1,0:T(8,128)(2,1)S(1)}, u32[]{:S(2)}, u32[]{:S(2)}) collective-permute-start(bf16[160,1536]{1,0:T(8,128)(2,1)S(1)} %get-tuple-element.80), channel_id=1, source_target_pairs={{0,2},{1,3},{2,0},{3,1},{4,6},{5,7},{6,4},{7,5},{8,10},{9,11},{10,... | collective-permute-start | bytes 1474568 | tf_op jit(solution)/shard_map/ppermute | solution.py:409
  40.3 10.7 %collective-permute-start.10 = (bf16[160,1024]{1,0:T(8,128)(2,1)S(1)}, bf16[160,1024]{1,0:T(8,128)(2,1)S(1)}, u32[]{:S(2)}, u32[]{:S(2)}) collective-permute-start(bf16[160,1024]{1,0:T(8,128)(2,1)S(1)} %collective-permute-done.9.refs_0_), channel_id=1, source_target_pairs={{0,1},{1,0},{2,3},{3,2},{4,5},{5,4},{6,7},{7,6},{8,9},{9,8},{10,11... | collective-permute-start | bytes 983048 | tf_op jit(solution)/shard_map/ppermute | solution.py:409
  41.6 16.6 %collective-permute-start.13 = (bf16[160,1024]{1,0:T(8,128)(2,1)S(1)}, bf16[160,1024]{1,0:T(8,128)(2,1)S(1)}, u32[]{:S(2)}, u32[]{:S(2)}) collective-permute-start(bf16[160,1024]{1,0:T(8,128)(2,1)S(1)} %collective-permute-done.12.refs_0_), channel_id=1, source_target_pairs={{0,1},{1,0},{2,3},{3,2},{4,5},{5,4},{6,7},{7,6},{8,9},{9,8},{10,11... | collective-permute-start | bytes 983048 | tf_op jit(solution)/shard_map/ppermute | solution.py:409
  54.4 10.8 %collective-permute-start.11 = (bf16[160,1024]{1,0:T(8,128)(2,1)}, bf16[160,1024]{1,0:T(8,128)(2,1)S(1)}, u32[]{:S(2)}, u32[]{:S(2)}) collective-permute-start(bf16[160,1024]{1,0:T(8,128)(2,1)} %get-tuple-element.88), channel_id=1, source_target_pairs={{0,2},{1,3},{2,0},{3,1},{4,6},{5,7},{6,4},{7,5},{8,10},{9,11},{10,... | collective-permute-start | bytes 983048 | tf_op jit(solution)/shard_map/ppermute | solution.py:409
  58.2 6.1 %copy-start.2 = (s32[1,2,2]{2,1,0:T(2,128)S(1)}, s32[1,2,2]{2,1,0:T(2,128)}, u32[]{:S(2)}) copy-start(s32[1,2,2]{2,1,0:T(2,128)} %param.17) | copy-start | bytes 52
  61.9 7.6 %collective-permute-start.14 = (bf16[160,1024]{1,0:T(8,128)(2,1)}, bf16[160,1024]{1,0:T(8,128)(2,1)S(1)}, u32[]{:S(2)}, u32[]{:S(2)}) collective-permute-start(bf16[160,1024]{1,0:T(8,128)(2,1)} %get-tuple-element.96), channel_id=1, source_target_pairs={{0,2},{1,3},{2,0},{3,1},{4,6},{5,7},{6,4},{7,5},{8,10},{9,11},{10,... | collective-permute-start | bytes 983048 | tf_op jit(solution)/shard_map/ppermute | solution.py:409
  64.3 21.3 %copy-start = (bf16[1,1024,2048]{2,1,0:T(8,128)(2,1)S(1)}, bf16[1,1024,2048]{2,1,0:T(8,128)(2,1)}, u32[]{:S(2)}) copy-start(bf16[1,1024,2048]{2,1,0:T(8,128)(2,1)} %param.14) | copy-start | bytes 12582916
  75.0 7.6 %collective-permute-start.15 = (bf16[160,512]{1,0:T(8,128)(2,1)S(1)}, bf16[160,512]{1,0:T(8,128)(2,1)S(1)}, u32[]{:S(2)}, u32[]{:S(2)}) collective-permute-start(bf16[160,512]{1,0:T(8,128)(2,1)S(1)} %get-tuple-element.98), channel_id=1, source_target_pairs={{0,2},{1,3},{2,0},{3,1},{4,6},{5,7},{6,4},{7,5},{8,10},{9,11},{10,... | collective-permute-start | bytes 491528 | tf_op jit(solution)/shard_map/ppermute | solution.py:409
  82.7 6.3 %collective-permute-start.18 = (bf16[160,512]{1,0:T(8,128)(2,1)S(1)}, bf16[160,512]{1,0:T(8,128)(2,1)S(1)}, u32[]{:S(2)}, u32[]{:S(2)}) collective-permute-start(bf16[160,512]{1,0:T(8,128)(2,1)S(1)} %get-tuple-element.112), channel_id=1, source_target_pairs={{0,6},{1,7},{2,4},{3,5},{4,2},{5,3},{6,0},{7,1},{8,14},{9,15},{10,... | collective-permute-start | bytes 491528 | tf_op jit(solution)/shard_map/ppermute | solution.py:409
  82.7 8.0 %collective-permute-start.17 = (bf16[160,512]{1,0:T(8,128)(2,1)S(1)}, bf16[160,512]{1,0:T(8,128)(2,1)S(1)}, u32[]{:S(2)}, u32[]{:S(2)}) collective-permute-start(bf16[160,512]{1,0:T(8,128)(2,1)S(1)} %get-tuple-element.110), channel_id=1, source_target_pairs={{0,4},{1,5},{2,6},{3,7},{4,0},{5,1},{6,2},{7,3},{8,12},{9,13},{10,... | collective-permute-start | bytes 491528 | tf_op jit(solution)/shard_map/ppermute | solution.py:409
  85.7 13.6 %copy-start.1 = (bf16[1,2,160,1024]{3,2,1,0:T(8,128)(2,1)S(1)}, bf16[1,2,160,1024]{3,2,1,0:T(8,128)(2,1)}, u32[]{:S(2)}) copy-start(bf16[1,2,160,1024]{3,2,1,0:T(8,128)(2,1)} %hidden.5) | copy-start | bytes 1966084
  87.1 8.1 %collective-permute-start.16 = (bf16[160,1024]{1,0:T(8,128)(2,1)S(1)}, bf16[160,1024]{1,0:T(8,128)(2,1)S(1)}, u32[]{:S(2)}, u32[]{:S(2)}) collective-permute-start(bf16[160,1024]{1,0:T(8,128)(2,1)S(1)} %get-tuple-element.100), channel_id=1, source_target_pairs={{0,1},{1,0},{2,3},{3,2},{4,5},{5,4},{6,7},{7,6},{8,9},{9,8},{10,11... | collective-permute-start | bytes 983048 | tf_op jit(solution)/shard_map/ppermute | solution.py:409
  92.1 7.1 %collective-permute-start.19 = (bf16[160,1024]{1,0:T(8,128)(2,1)S(1)}, bf16[160,1024]{1,0:T(8,128)(2,1)S(1)}, u32[]{:S(2)}, u32[]{:S(2)}) collective-permute-start(bf16[160,1024]{1,0:T(8,128)(2,1)S(1)} %get-tuple-element.114), channel_id=1, source_target_pairs={{0,1},{1,0},{2,3},{3,2},{4,5},{5,4},{6,7},{7,6},{8,9},{9,8},{10,11... | collective-permute-start | bytes 983048 | tf_op jit(solution)/shard_map/ppermute | solution.py:409
